TPU v7x, 32 devices: a whole 2x2x4 slice. The times are simulated.
32 devices in a mesh: frame: 8 (over z, x), head: 4 (over y, core).
Axes of the slice: x: 2, y: 2, z: 4, core: 2. Of those that a mesh axis runs over, the one named last changes fastest.
Arguments:
- video_queries: bfloat16 [6144, 3072], P(('frame', 'head')), may hold values from -16 to 16
- video_keys: bfloat16 [6144, 3072], P(('frame', 'head')), may hold values from -16 to 16
- video_values: bfloat16 [6144, 3072], P(('frame', 'head')), may hold values from -6 to 6
- text_keys: bfloat16 [256, 3072], P('frame', 'head'), may hold values from -15 to 15
- text_values: bfloat16 [256, 3072], P('frame', 'head'), may hold values from -6 to 6
- kept_tiles: int32 [48, 12], P('frame'), may hold values from 0 to 47, as said below
- kept_count: int32 [48], P('frame'), may hold values from 1 to 12
- text_len: int32 [1], replicated, may hold values from 128 to 256
Outputs:
- attention_out: bfloat16 [6144, 3072], P(('frame', 'head'))
Inputs may be any that keep to these rules, and one draw needn't show every extreme that they name: `kept_tiles`: each row holds 12 distinct tiles; its first entry is the query tile itself, and every entry lies in the query tile's slab or in the slab just before or after it on the loop, where slab 8 - 1 is next to slab 0.
All inputs are finite; a program needn't handle non-finite values.
Results may differ from a plain program's by a relative error of at most 0.003.
Values may be sent and summed in bfloat16 or wider, within the bound.
No kernel may reach another device: no remote copies, remote signals or barrier semaphores. Data moves between devices by JAX's collectives and lax.ppermute only.
A program may use at most 128 MiB of HBM per device.

v0:
```python
import math

import jax
import jax.numpy as jnp
from jax import lax
from jax.sharding import PartitionSpec as P

HD = 128
TILE = 128


def shifted(value, axis, by):
    length = lax.axis_size(axis)
    return lax.ppermute(value, axis, [(i, (i + by) % length) for i in range(length)])


def tile_mask(tile_lists, live_counts, slab_index, slab_count, tile_count):
    key_ids = (slab_index + slab_count) % slab_count * tile_count + jnp.arange(
        tile_count, dtype=jnp.int32
    )
    slot_live = jnp.arange(tile_lists.shape[1], dtype=jnp.int32)[None, :] < live_counts[:, None]
    matches = (tile_lists[:, :, None] == key_ids[None, None, :]) & slot_live[:, :, None]
    return jnp.any(matches, axis=1)


def token_mask(tile_allow, tile_size):
    query_tiles, key_tiles = tile_allow.shape
    spread_out = jnp.broadcast_to(
        tile_allow[:, None, :, None], (query_tiles, tile_size, key_tiles, tile_size)
    )
    return spread_out.reshape(query_tiles * tile_size, key_tiles * tile_size)


def partial_attention(queries, keys_here, values, allowed, head_dim):
    row_count = queries.shape[0]
    feature_width = queries.shape[1]
    heads_here = feature_width // head_dim
    query_heads = jnp.transpose(queries.reshape(row_count, heads_here, head_dim), (1, 0, 2))
    key_heads = jnp.transpose(
        keys_here.reshape(keys_here.shape[0], heads_here, head_dim), (1, 0, 2)
    )
    value_heads = jnp.transpose(values.reshape(values.shape[0], heads_here, head_dim), (1, 0, 2))
    scale = 1.0 / math.sqrt(head_dim)

    def one_head(operands):
        query_one, key_one, value_one = operands
        scores = (
            jnp.einsum("qd,kd->qk", query_one, key_one, preferred_element_type=jnp.float32) * scale
        )
        masked = jnp.where(allowed, scores, -1e30)
        row_max = jnp.max(masked, axis=1)
        weights = jnp.where(allowed, jnp.exp(masked - row_max[:, None]), 0.0)
        row_sum = jnp.sum(weights, axis=1)
        weighted = jnp.dot(
            weights.astype(jnp.bfloat16), value_one, preferred_element_type=jnp.float32
        )
        return (weighted, row_max, row_sum)

    weighted, row_max, row_sum = lax.map(one_head, (query_heads, key_heads, value_heads))
    return (
        jnp.transpose(weighted, (1, 0, 2)).reshape(row_count, feature_width),
        row_max.T,
        row_sum.T,
    )


def combine(partials, head_dim):
    row_count, feature_width = partials[0][0].shape
    heads_here = feature_width // head_dim
    overall = partials[0][1]
    for member in partials[1:]:
        overall = jnp.maximum(overall, member[1])
    numerator = jnp.zeros((row_count, heads_here, head_dim), jnp.float32)
    denominator = jnp.zeros((row_count, heads_here), jnp.float32)
    for weighted, row_max, row_sum in partials:
        factor = jnp.exp(row_max - overall)
        numerator = (
            numerator + weighted.reshape(row_count, heads_here, head_dim) * factor[:, :, None]
        )
        denominator = denominator + row_sum * factor
    return (
        (numerator / denominator[:, :, None]).reshape(row_count, feature_width).astype(jnp.bfloat16)
    )


def body(
    video_queries,
    video_keys,
    video_values,
    text_keys,
    text_values,
    kept_tiles,
    kept_count,
    text_len,
):
    slab_count = lax.axis_size("frame")
    slab_index = lax.axis_index("frame")
    tile_count = kept_tiles.shape[0]
    text_block_keys, text_block_values = (
        lax.all_gather(text_keys, "frame", axis=0, tiled=True),
        lax.all_gather(text_values, "frame", axis=0, tiled=True),
    )
    text_live = jnp.arange(text_block_keys.shape[0], dtype=jnp.int32) < text_len[0]
    own_tiles = tile_mask(kept_tiles, kept_count, slab_index, slab_count, tile_count)
    before_tiles = tile_mask(kept_tiles, kept_count, slab_index - 1, slab_count, tile_count)
    after_tiles = tile_mask(kept_tiles, kept_count, slab_index + 1, slab_count, tile_count)
    queries, keys_here, values = (
        lax.all_to_all(video_queries, "head", split_axis=1, concat_axis=0, tiled=True),
        lax.all_to_all(video_keys, "head", split_axis=1, concat_axis=0, tiled=True),
        lax.all_to_all(video_values, "head", split_axis=1, concat_axis=0, tiled=True),
    )
    keys_before, values_before = shifted((keys_here, values), "frame", 1)
    keys_after, values_after = shifted((keys_here, values), "frame", -1)
    row_count = queries.shape[0]
    text_allow = jnp.broadcast_to(text_live[None, :], (row_count, text_live.shape[0]))
    own_allow = jnp.concatenate([token_mask(own_tiles, TILE), text_allow], axis=1)
    own_part = partial_attention(
        queries,
        jnp.concatenate([keys_here, text_block_keys], axis=0),
        jnp.concatenate([values, text_block_values], axis=0),
        own_allow,
        HD,
    )
    before_part = partial_attention(
        queries, keys_before, values_before, token_mask(before_tiles, TILE), HD
    )
    after_part = partial_attention(
        queries, keys_after, values_after, token_mask(after_tiles, TILE), HD
    )
    mixed = combine([tuple(own_part), tuple(before_part), tuple(after_part)], HD)
    return lax.all_to_all(mixed, "head", split_axis=0, concat_axis=1, tiled=True)


def solution(mesh):
    in_specs = (
        P(("frame", "head"), None),
        P(("frame", "head"), None),
        P(("frame", "head"), None),
        P("frame", "head"),
        P("frame", "head"),
        P("frame", None),
        P("frame"),
        P(),
    )
    out_specs = P(("frame", "head"), None)
    return jax.shard_map(body, mesh=mesh, in_specs=in_specs, out_specs=out_specs, check_vma=False)
```

profile of v0, /device:TPU:0, one launch (start us, length us, event | category | flops | bytes accessed | tf_op | source)
XLA Modules:
  0.0 343.9 jit_solution(10015793964592838226)
XLA Ops:
  0.0 2.5 copy.133
  2.5 4.3 %all-to-all-start.1 = ((bf16[192,4,768]{2,0,1:T(8,128)(2,1)}), bf16[192,4,768]{2,0,1:T(8,128)(2,1)}, u32[]{:S(2)}, u32[]{:S(2)}) async-start(bf16[192,4,768]{2,0,1:T(8,128)(2,1)} %bitcast.186), calls=%async_computation.1 | async-start | bytes 2359296 | tf_op jit(solution)/shard_map/all_to_all | solution.py:109
  7.9 15.4 %all-to-all-done.1 = bf16[192,4,768]{2,0,1:T(8,128)(2,1)} async-done(((bf16[192,4,768]{2,0,1:T(8,128)(2,1)}), bf16[192,4,768]{2,0,1:T(8,128)(2,1)}, u32[]{:S(2)}, u32[]{:S(2)}) %all-to-all-start.1) | async-done | bytes 1179680 | tf_op jit(solution)/shard_map/all_to_all | solution.py:109
  23.3 4.4 %all-to-all-start.2 = ((bf16[192,4,768]{2,0,1:T(8,128)(2,1)}), bf16[192,4,768]{2,0,1:T(8,128)(2,1)}, u32[]{:S(2)}, u32[]{:S(2)}) async-start(bf16[192,4,768]{2,0,1:T(8,128)(2,1)} %bitcast.185), calls=%async_computation.2 | async-start | bytes 2359296 | tf_op jit(solution)/shard_map/all_to_all | solution.py:110
  28.9 14.7 %all-to-all-done.2 = bf16[192,4,768]{2,0,1:T(8,128)(2,1)} async-done(((bf16[192,4,768]{2,0,1:T(8,128)(2,1)}), bf16[192,4,768]{2,0,1:T(8,128)(2,1)}, u32[]{:S(2)}, u32[]{:S(2)}) %all-to-all-start.2) | async-done | bytes 1179680 | tf_op jit(solution)/shard_map/all_to_all | solution.py:110
  43.6 3.5 %all-to-all-start = ((bf16[192,4,768]{2,0,1:T(8,128)(2,1)}), bf16[192,4,768]{2,0,1:T(8,128)(2,1)S(1)}, u32[]{:S(2)}, u32[]{:S(2)}) async-start(bf16[192,4,768]{2,0,1:T(8,128)(2,1)} %bitcast.187), calls=%async_computation | async-start | bytes 2359296 | tf_op jit(solution)/shard_map/all_to_all | solution.py:108
  48.9 32.3 %all_gather.6 = bf16[256,768]{1,0:T(8,128)(2,1)S(1)} all-gather(bf16[32,768]{1,0:T(8,128)(2,1)S(1)} %copy-done.7), channel_id=1, replica_groups=mesh['frame'=8,'head'=4] {'frame'}, dimensions={0}, use_global_device_ids=true | all-gather | bytes 442368 | tf_op jit(solution)/shard_map/all_gather | solution.py:100
  82.5 53.9 %all_gather.7 = bf16[256,768]{1,0:T(8,128)(2,1)S(1)} all-gather(bf16[32,768]{1,0:T(8,128)(2,1)S(1)} %copy-done.8), channel_id=1, replica_groups=mesh['frame'=8,'head'=4] {'frame'}, dimensions={0}, use_global_device_ids=true | all-gather | bytes 442368 | tf_op jit(solution)/shard_map/all_gather | solution.py:101
  138.2 4.7 %collective-permute-start.2 = (bf16[768,768]{1,0:T(8,128)(2,1)}, bf16[768,768]{1,0:T(8,128)(2,1)}, u32[]{:S(2)}, u32[]{:S(2)}) collective-permute-start(bf16[768,768]{1,0:T(8,128)(2,1)} %bitcast.15), channel_id=1, source_target_pairs={{0,28},{4,0},{8,4},{12,8},{16,12},{20,16},{24,20},{28,24},{1,29},{... | collective-permute-start | bytes 3538952 | tf_op jit(solution)/shard_map/ppermute | solution.py:14
  142.9 4.7 %collective-permute-start.3 = (bf16[768,768]{1,0:T(8,128)(2,1)}, bf16[768,768]{1,0:T(8,128)(2,1)}, u32[]{:S(2)}, u32[]{:S(2)}) collective-permute-start(bf16[768,768]{1,0:T(8,128)(2,1)} %bitcast.18), channel_id=1, source_target_pairs={{0,28},{4,0},{8,4},{12,8},{16,12},{20,16},{24,20},{28,24},{1,29},{... | collective-permute-start | bytes 3538952 | tf_op jit(solution)/shard_map/ppermute | solution.py:14
  150.2 2.8 concatenate.19
  153.5 1.4 copy.98
  154.8 2.8 concatenate.23
  159.4 1.6 broadcast.59.clone.2
  161.0 41.7 %while.44 = (s32[]{:T(128)}, f32[6,768,128]{2,1,0:T(8,128)}, f32[6,768]{1,0:T(8,128)S(1)}, f32[6,768]{1,0:T(8,128)S(1)}, bf16[6,768,128]{2,1,0:T(8,128)(2,1)}, /...) while((s32[]{:T(128)}, f32[6,768,128]{2,1,0:T(8,128)}, ...), condition=%wide.region_4.5_spmd, body=%wide.region_1.0_spmd.sunk | while | flops 412875264 | bytes 16095369 | solution.py:59
  161.0 2.2 fusion.96
  164.5 3.4 fusion.97
  168.0 2.2 fusion.96
  171.5 3.4 fusion.97
  175.0 2.2 fusion.96
  178.5 3.3 fusion.97
  181.9 2.2 fusion.96
  185.4 3.3 fusion.97
  188.8 2.2 fusion.96
  192.3 3.3 fusion.97
  195.8 2.2 fusion.96
  199.3 3.3 fusion.97
  203.9 1.6 copy.100
  205.5 1.7 collective-permute-done.1
  207.1 2.4 copy.101
  210.9 49.2 %while.45 = (s32[]{:T(128)}, f32[6,768,128]{2,1,0:T(8,128)S(1)}, f32[6,768]{1,0:T(8,128)}, f32[6,768]{1,0:T(8,128)}, bf16[6,768,128]{2,1,0:T(8,128)(2,1)}, /*ind...) while((s32[]{:T(128)}, f32[6,768,128]{2,1,0:T(8,128)S(1)}, ...), condition=%wide.region_9.10_spmd.clone, body=%wide.region_6.9_spmd.clone.sunk | while | flops 309656064 | bytes 12819601 | solution.py:59
  212.2 1.5 fusion.101
  213.7 1.9 fusion.102
  220.4 1.5 fusion.101
  221.9 1.9 fusion.102
  228.6 1.5 fusion.101
  230.1 1.9 fusion.102
  236.8 1.5 fusion.101
  238.3 1.9 fusion.102
  245.0 1.5 fusion.101
  246.5 1.9 fusion.102
  253.2 1.5 fusion.101
  254.7 1.9 fusion.102
  260.1 2.3 copy.105
  262.5 2.6 copy.106
  266.5 49.2 %while.46 = (s32[]{:T(128)}, f32[6,768,128]{2,1,0:T(8,128)S(1)}, f32[6,768]{1,0:T(8,128)}, f32[6,768]{1,0:T(8,128)}, bf16[6,768,128]{2,1,0:T(8,128)(2,1)}, /*ind...) while((s32[]{:T(128)}, f32[6,768,128]{2,1,0:T(8,128)S(1)}, ...), condition=%wide.region_14.15_spmd.clone, body=%wide.region_11.14_spmd.clone.sunk | while | flops 309656064 | bytes 12819601 | solution.py:59
  267.7 1.5 fusion.106
  269.3 1.9 fusion.107
  271.9 1.4 dynamic_update_slice.55
  275.9 1.5 fusion.106
  277.5 1.9 fusion.107
  284.1 1.5 fusion.106
  285.7 1.9 fusion.107
  288.3 1.4 dynamic_update_slice.55
  292.3 1.5 fusion.106
  293.9 1.9 fusion.107
  296.5 1.4 dynamic_update_slice.55
  300.5 1.5 fusion.106
  302.1 1.9 fusion.107
  308.7 1.5 fusion.106
  310.3 1.9 fusion.107
  316.5 5.5 %fusion.69 = bf16[768,6,128]{2,0,1:T(8,128)(2,1)S(1)} fusion(f32[6,768,128]{2,1,0:T(8,128)S(1)} %get-tuple-element.142, f32[6,768,128]{2,1,0:T(8,128)} %copy-done.1, f32[6,768,128]{2,1,0:T(8,128)} %get-tuple-element.137, f32[768,6]{0,1:T(8,128)S(1)} %get-tuple-element.331, f32[768,6]{0,1:T(8,128)S(1)} %get-tuple-element.334, ...), kind=kLoop, calls=%fused_computation.72 | loop fusion | flops 4128768 | bytes 8331264 | tf_op jit(solution)/shard_map/convert_element_type | solution.py:82
  322.8 1.4 convert_element_type.17
  324.2 18.6 %all_to_all.70 = bf16[4,192,768]{2,1,0:T(8,128)(2,1)S(1)} all-to-all(bf16[4,192,768]{2,1,0:T(8,128)(2,1)S(1)} %convert_element_type.17), channel_id=1, replica_groups=mesh['frame'=8,'head'=4] {'head'}, dimensions={0} | all-to-all | bytes 2359296 | tf_op jit(solution)/shard_map/all_to_all | solution.py:131
  (192 shorter events, 77.9 us)
Async XLA Ops:
  0.0 6.8 %copy-start.3 = (bf16[192,3072]{1,0:T(8,128)(2,1)S(1)}, bf16[192,3072]{1,0:T(8,128)(2,1)}, u32[]{:S(2)}) copy-start(bf16[192,3072]{1,0:T(8,128)(2,1)} %param.16) | copy-start | bytes 3538948
  2.5 20.9 %all-to-all-start.1 = ((bf16[192,4,768]{2,0,1:T(8,128)(2,1)}), bf16[192,4,768]{2,0,1:T(8,128)(2,1)}, u32[]{:S(2)}, u32[]{:S(2)}) async-start(bf16[192,4,768]{2,0,1:T(8,128)(2,1)} %bitcast.186), calls=%async_computation.1 | async-start | bytes 2359296 | tf_op jit(solution)/shard_map/all_to_all | solution.py:109
  6.8 21.0 %copy-start.4 = (bf16[192,3072]{1,0:T(8,128)(2,1)S(1)}, bf16[192,3072]{1,0:T(8,128)(2,1)}, u32[]{:S(2)}) copy-start(bf16[192,3072]{1,0:T(8,128)(2,1)} %param.14) | copy-start | bytes 3538948
  23.3 5.5 %copy-start.10 = (s32[6]{0:T(128)S(1)}, s32[6]{0:T(128)}, u32[]{:S(2)}) copy-start(s32[6]{0:T(128)} %param.20) | copy-start | bytes 76
  23.3 20.3 %all-to-all-start.2 = ((bf16[192,4,768]{2,0,1:T(8,128)(2,1)}), bf16[192,4,768]{2,0,1:T(8,128)(2,1)}, u32[]{:S(2)}, u32[]{:S(2)}) async-start(bf16[192,4,768]{2,0,1:T(8,128)(2,1)} %bitcast.185), calls=%async_computation.2 | async-start | bytes 2359296 | tf_op jit(solution)/shard_map/all_to_all | solution.py:110
  27.7 19.5 %copy-start.9 = (s32[6,12]{1,0:T(8,128)S(1)}, s32[6,12]{1,0:T(8,128)}, u32[]{:S(2)}) copy-start(s32[6,12]{1,0:T(8,128)} %param.19) | copy-start | bytes 868
  28.9 20.1 %copy-start.7 = (bf16[32,768]{1,0:T(8,128)(2,1)S(1)}, bf16[32,768]{1,0:T(8,128)(2,1)}, u32[]{:S(2)}) copy-start(bf16[32,768]{1,0:T(8,128)(2,1)} %param.17) | copy-start | bytes 147460
  43.6 104.0 %all-to-all-start = ((bf16[192,4,768]{2,0,1:T(8,128)(2,1)}), bf16[192,4,768]{2,0,1:T(8,128)(2,1)S(1)}, u32[]{:S(2)}, u32[]{:S(2)}) async-start(bf16[192,4,768]{2,0,1:T(8,128)(2,1)} %bitcast.187), calls=%async_computation | async-start | bytes 2359296 | tf_op jit(solution)/shard_map/all_to_all | solution.py:108
  47.2 35.3 %copy-start.8 = (bf16[32,768]{1,0:T(8,128)(2,1)S(1)}, bf16[32,768]{1,0:T(8,128)(2,1)}, u32[]{:S(2)}) copy-start(bf16[32,768]{1,0:T(8,128)(2,1)} %param.18) | copy-start | bytes 147460
  138.2 65.7 %collective-permute-start = (bf16[768,768]{1,0:T(8,128)(2,1)}, bf16[768,768]{1,0:T(8,128)(2,1)}, u32[]{:S(2)}, u32[]{:S(2)}) collective-permute-start(bf16[768,768]{1,0:T(8,128)(2,1)} %bitcast.15), channel_id=1, source_target_pairs={{0,4},{4,8},{8,12},{12,16},{16,20},{20,24},{24,28},{28,0},{1,5},{5... | collective-permute-start | bytes 3538952 | tf_op jit(solution)/shard_map/ppermute | solution.py:14
  138.2 121.9 %collective-permute-start.2 = (bf16[768,768]{1,0:T(8,128)(2,1)}, bf16[768,768]{1,0:T(8,128)(2,1)}, u32[]{:S(2)}, u32[]{:S(2)}) collective-permute-start(bf16[768,768]{1,0:T(8,128)(2,1)} %bitcast.15), channel_id=1, source_target_pairs={{0,28},{4,0},{8,4},{12,8},{16,12},{20,16},{24,20},{28,24},{1,29},{... | collective-permute-start | bytes 3538952 | tf_op jit(solution)/shard_map/ppermute | solution.py:14
  142.9 64.2 %collective-permute-start.1 = (bf16[768,768]{1,0:T(8,128)(2,1)}, bf16[768,768]{1,0:T(8,128)(2,1)}, u32[]{:S(2)}, u32[]{:S(2)}) collective-permute-start(bf16[768,768]{1,0:T(8,128)(2,1)} %bitcast.18), channel_id=1, source_target_pairs={{0,4},{4,8},{8,12},{12,16},{16,20},{20,24},{24,28},{28,0},{1,5},{5... | collective-permute-start | bytes 3538952 | tf_op jit(solution)/shard_map/ppermute | solution.py:14
  142.9 119.5 %collective-permute-start.3 = (bf16[768,768]{1,0:T(8,128)(2,1)}, bf16[768,768]{1,0:T(8,128)(2,1)}, u32[]{:S(2)}, u32[]{:S(2)}) collective-permute-start(bf16[768,768]{1,0:T(8,128)(2,1)} %bitcast.18), channel_id=1, source_target_pairs={{0,28},{4,0},{8,4},{12,8},{16,12},{20,16},{24,20},{28,24},{1,29},{... | collective-permute-start | bytes 3538952 | tf_op jit(solution)/shard_map/ppermute | solution.py:14
  149.0 4.0 %copy-start.2 = (bf16[256,6,128]{2,1,0:T(8,128)(2,1)S(1)}, bf16[256,6,128]{2,1,0:T(8,128)(2,1)}, u32[]{:S(2)}) copy-start(bf16[256,6,128]{2,1,0:T(8,128)(2,1)} %copy.93) | copy-start | bytes 1179652
  161.0 2.2 copy-start
  168.0 2.2 copy-start
  174.9 2.2 copy-start
  181.9 2.2 copy-start
  188.8 2.2 copy-start
  195.7 2.2 copy-start
  202.7 0.6 copy-start.5
  203.3 0.6 copy-start.6
  260.1 5.0 %copy-start.1 = (f32[6,768,128]{2,1,0:T(8,128)}, f32[6,768,128]{2,1,0:T(8,128)S(1)}, u32[]{:S(2)}) copy-start(f32[6,768,128]{2,1,0:T(8,128)S(1)} %get-tuple-element.141) | copy-start | bytes 7077892
where the time goes:
time: 347 us; the launch traced here: 344 us
  blocking collectives  105 us (30%)
  local copies, waits for them, and re-layouts  84.3 us (24%)
  matrix products  75 us (22%)
  waiting for transfers between devices  31.8 us (9%)
  other arithmetic  24.6 us (7%)
  starting transfers between devices  21.6 us (6%)
    all_gather x1, blocking collectives, body(): lax.all_gather(text_values, 'frame', axis=0, tiled=True)  53.9 us
    dot_general x18, matrix products, one_head(): jnp.dot(weights.astype(jnp.bfloat16), value_one, preferred_element_type=j...  43.3 us
    dynamic_update_slice x36, local copies, waits for them, and re-layouts, partial_attention(): lax.map(one_head, (query_heads, key_heads, value_heads))  33.5 us
    all_gather x1, blocking collectives, body(): lax.all_gather(text_keys, 'frame', axis=0, tiled=True)  32.3 us
    dot_general x18, matrix products, one_head(): jnp.einsum('qd,kd->qk', query_one, key_one, preferred_element_type=jnp.fl...  31.6 us
    all_to_all x1, blocking collectives, body(): lax.all_to_all(mixed, 'head', split_axis=0, concat_axis=1, tiled=True)  18.6 us
    reduce_sum x18, other arithmetic, one_head(): row_sum = jnp.sum(weights, axis=1)  15.6 us
    all_to_all x1, waiting for transfers between devices, body(): lax.all_to_all(video_keys, 'head', split_axis=1, concat_axis=0, tiled=True)  15.4 us
  transfers between devices with their start and end apart: 7, of which 3 were waited for; matrix products, arithmetic and copies ran while one was open for 34% of the time, Pallas kernels for 0%

commit v1 on v0

v1 whole, which is shorter than its diff:
```python
import functools
import math

import jax
import jax.numpy as jnp
from jax import lax
from jax.experimental import pallas as pl
from jax.experimental.pallas import tpu as pltpu
from jax.sharding import PartitionSpec as P

HD = 128
TILE = 128
AXES = ("frame", "head")
SCALE = math.log2(math.e) / math.sqrt(HD)
LOW = -1e30
NT = (((1,), (1,)), ((), ()))
SMEM = pl.BlockSpec(memory_space=pltpu.SMEM)
PARAMS = pltpu.CompilerParams(vmem_limit_bytes=48 << 20)


def group(queries, keys, values_t, biases):
    scores = lax.dot_general(keys, queries, NT, preferred_element_type=jnp.float32)
    key_tiles, query_tiles = keys.shape[0] // TILE, queries.shape[0] // TILE
    tops, totals, weights = [], [], []
    for t in range(query_tiles):
        blocks = [
            scores[u * TILE : (u + 1) * TILE, t * TILE : (t + 1) * TILE] + biases[u][t]
            for u in range(key_tiles)
        ]
        top = functools.reduce(jnp.maximum, blocks)
        top = jnp.max(top, axis=0, keepdims=True)
        parts = [jnp.exp2((block - top) * SCALE) for block in blocks]
        total = functools.reduce(jnp.add, parts)
        tops.append(top)
        totals.append(jnp.sum(total, axis=0, keepdims=True))
        weights.append(jnp.concatenate([p.astype(jnp.bfloat16) for p in parts], axis=0))
    weighted = jnp.dot(
        values_t, jnp.concatenate(weights, axis=1), preferred_element_type=jnp.float32
    )
    return weighted, jnp.concatenate(tops, axis=1), jnp.concatenate(totals, axis=1)


def merge(one, two):
    top = jnp.maximum(one[1], two[1])
    first, second = jnp.exp2((one[1] - top) * SCALE), jnp.exp2((two[1] - top) * SCALE)
    return one[0] * first + two[0] * second, top, one[2] * first + two[2] * second


def local_kernel(
    tiles, bias, q_ref, k_ref, v_ref, tk_ref, tv_ref, tb_ref, sum_ref, stat_ref
):
    side = pl.program_id(1)
    rows = tiles * TILE
    own = pl.ds(pl.multiple_of(side * rows, rows), rows)
    other = pl.ds(pl.multiple_of((1 - side) * rows, rows), rows)
    queries = q_ref[...]
    at = lambda t, u: bias[(side * tiles + t) * 3 * tiles + u]
    text_tiles = tk_ref.shape[0] // TILE
    own_bias = [[at(t, u) for t in range(tiles)] for u in range(tiles)]
    own_bias += [[tb_ref[j * TILE : (j + 1) * TILE, :]] * tiles for j in range(text_tiles)]
    mine = group(
        queries,
        jnp.concatenate([k_ref[own, :], tk_ref[...]], axis=0),
        jnp.concatenate([v_ref[own, :], tv_ref[...]], axis=0).T,
        own_bias,
    )
    theirs = group(
        queries,
        k_ref[other, :],
        v_ref[other, :].T,
        [[at(t, tiles + u) for t in range(tiles)] for u in range(tiles)],
    )
    weighted, top, total = merge(mine, theirs)
    sum_ref[0, 0] = weighted
    stat_ref[0, 0, 0:1, :] = top
    stat_ref[0, 0, 1:2, :] = total


def halo_kernel(tiles, bias, q_ref, k_ref, v_ref, sum_ref, stat_ref, out_ref):
    side = pl.program_id(1)
    at = lambda t, u: bias[(side * tiles + t) * 3 * tiles + u]

    def run(keys, values):
        far = group(
            q_ref[...],
            keys,
            values.T,
            [[at(t, 2 * tiles + u) for t in range(tiles)] for u in range(tiles)],
        )
        near = (sum_ref[0, 0], stat_ref[0, 0, 0:1, :], stat_ref[0, 0, 1:2, :])
        weighted, _, total = merge(near, far)
        out_ref[...] = (weighted / total).T.astype(out_ref.dtype)

    run(k_ref[0], v_ref[0])


def local_attention(tiles, bias, q, k, v, text_k, text_v, text_bias):
    heads, rows, text = q.shape[1] // HD, tiles * TILE, text_k.shape[0]
    whole = pl.BlockSpec((2 * rows, HD), lambda h, s: (0, h))
    text_block = pl.BlockSpec((text, HD), lambda h, s: (0, h))
    return pl.pallas_call(
        functools.partial(local_kernel, tiles),
        grid=(heads, 2),
        in_specs=[
            SMEM,
            pl.BlockSpec((rows, HD), lambda h, s: (s, h)),
            whole,
            whole,
            text_block,
            text_block,
            pl.BlockSpec((text, TILE), lambda h, s: (0, 0)),
        ],
        out_specs=[
            pl.BlockSpec((1, 1, HD, rows), lambda h, s: (h, s, 0, 0)),
            pl.BlockSpec((1, 1, 2, rows), lambda h, s: (h, s, 0, 0)),
        ],
        out_shape=[
            jax.ShapeDtypeStruct((heads, 2, HD, rows), jnp.float32),
            jax.ShapeDtypeStruct((heads, 2, 2, rows), jnp.float32),
        ],
        compiler_params=PARAMS,
    )(bias, q, k, v, text_k, text_v, text_bias)


def halo_attention(tiles, bias, q, k, v, sums, stats):
    heads, rows = q.shape[1] // HD, tiles * TILE
    block = pl.BlockSpec((rows, HD), lambda h, s: (s, h))
    far = pl.BlockSpec((1, rows, HD), lambda h, s: (s, 0, h))
    return pl.pallas_call(
        functools.partial(halo_kernel, tiles),
        grid=(heads, 2),
        in_specs=[
            SMEM,
            block,
            far,
            far,
            pl.BlockSpec((1, 1, HD, rows), lambda h, s: (h, s, 0, 0)),
            pl.BlockSpec((1, 1, 2, rows), lambda h, s: (h, s, 0, 0)),
        ],
        out_specs=block,
        out_shape=jax.ShapeDtypeStruct(q.shape, jnp.bfloat16),
        compiler_params=PARAMS,
    )(bias, q, k, v, sums, stats)


def kept_mask(lists, counts, slab, slabs, tiles):
    ids = (slab + slabs) % slabs * tiles + jnp.arange(tiles, dtype=jnp.int32)
    live = jnp.arange(lists.shape[1], dtype=jnp.int32)[None, :] < counts[:, None]
    return jnp.any((lists[:, :, None] == ids[None, None, :]) & live[:, :, None], axis=1)


def body(queries, keys, values, text_keys, text_values, lists, counts, text_len):
    slabs, heads = lax.axis_size("frame"), lax.axis_size("head")
    slab, pair, side = lax.axis_index("frame"), lax.axis_index("frame") // 2, lax.axis_index("frame") % 2
    ways, pairs = 2 * heads, slabs // 2
    tiles = lists.shape[0]
    rows, width = queries.shape
    part = width // ways
    count = slabs * heads
    groups = [list(range(ways * i, ways * (i + 1))) for i in range(pairs)]

    def shifted(x, by):
        return lax.ppermute(x, AXES, [(i, (i + by * ways) % count) for i in range(count)])

    def swapped(x):
        flip = lambda i: i // ways * ways + (i + heads) % ways
        return lax.ppermute(x, AXES, [(i, flip(i)) for i in range(count)])

    def exchange(x):
        return lax.all_to_all(
            x, AXES, split_axis=0, concat_axis=0, tiled=True, axis_index_groups=groups
        )

    def spread(x):
        x = x.reshape(rows, heads, 2, part).transpose(2, 1, 0, 3)
        return exchange(x.reshape(ways, rows, part))

    toward, away = jnp.where(side == 0, 1, -1), jnp.where(side == 0, -1, 1)
    mask = jnp.concatenate(
        [kept_mask(lists, counts, slab + by, slabs, tiles) for by in (0, toward, away)], axis=1
    ).astype(jnp.bfloat16)

    text_rows = text_keys.shape[0]
    text = jnp.stack([text_keys, text_values]).reshape(2, text_rows, 2, part)
    send = lax.dynamic_index_in_dim(text, 1 - side, 2, keepdims=False)
    keep = lax.dynamic_index_in_dim(text, side, 2, keepdims=False)
    flat = mask.reshape(1, 1, -1)
    row = jnp.pad(flat, ((0, 0), (0, text_rows - 1), (0, part - flat.shape[2])))
    got = swapped(jnp.concatenate([send, row], axis=0))
    got_mask = got[2, 0, : flat.shape[2]].reshape(mask.shape)
    first = lambda a, b: jnp.where(side == 0, a, b)
    text = jnp.concatenate([first(keep, got[:2]), first(got[:2], keep)], axis=1)
    masks = jnp.stack([first(mask, got_mask), first(got_mask, mask)])
    bias = jnp.where(masks.astype(jnp.float32) > 0.5, 0.0, LOW).astype(jnp.float32).reshape(-1)
    pieces, have = text, 1
    while have < pairs:
        take = min(have, pairs - have)
        more = shifted(pieces[:, : take * 2 * text_rows], have)
        pieces, have = jnp.concatenate([pieces, more], axis=1), have + take
    place = jnp.arange(pairs * 2 * text_rows, dtype=jnp.int32)
    token = (pair - place // (2 * text_rows)) % pairs * (2 * text_rows) + place % (2 * text_rows)
    text_bias = jnp.where(token < text_len[0], 0.0, LOW).astype(jnp.float32)
    text_bias = jnp.broadcast_to(text_bias[:, None], (token.shape[0], TILE))

    def both_ways(x):
        half = x.shape[0] // 2
        before, after = shifted(x[half:], 1), shifted(x[:half], -1)
        return before, after

    k = spread(keys)
    k_before, k_after = both_ways(k)
    v = spread(values)
    v_before, v_after = both_ways(v)
    q = spread(queries)
    q, k, v = (x.reshape(ways * rows, part) for x in (q, k, v))
    sums, stats = local_attention(tiles, bias, q, k, v, pieces[0], pieces[1], text_bias)
    k_far = jnp.stack([x.reshape(-1, part) for x in (k_before, k_after)])
    v_far = jnp.stack([x.reshape(-1, part) for x in (v_before, v_after)])
    out = halo_attention(tiles, bias, q, k_far, v_far, sums, stats)
    out = exchange(out.reshape(ways, rows, part))
    return out.reshape(2, heads, rows, part).transpose(2, 1, 0, 3).reshape(rows, width)


def solution(mesh):
    in_specs = (
        P(AXES, None),
        P(AXES, None),
        P(AXES, None),
        P("frame", "head"),
        P("frame", "head"),
        P("frame", None),
        P("frame"),
        P(),
    )
    return jax.shard_map(
        body, mesh=mesh, in_specs=in_specs, out_specs=P(AXES, None), check_vma=False
    )
```

time: 347 us -> 152 us (0.44)
  blocking collectives: 105 us -> 20.3 us
  matrix products: 75 us -> 0 us
  local copies, waits for them, and re-layouts: 84.3 us -> 22.6 us
  Pallas kernels: 0 us -> 25 us
  waiting for transfers between devices: 31.8 us -> 48.9 us
  other arithmetic: 24.6 us -> 9.38 us
    all_gather x2 -> x0, blocking collectives: 86.2 us -> none  [the longest x1 53.9 us: body(): lax.all_gather(text_values, 'frame', axis=0, tiled=True)]
    dot_general x36 -> x0, matrix products: 75 us -> none  [the longest x18 43.3 us: one_head(): jnp.dot(weights.astype(jnp.bfloat16), value_one, preferred_element_type=j...]
    ppermute x4 -> x7, waiting for transfers between devices: 1.7 us -> 37.2 us  [the longest x6 28.1 us: shifted(): lax.ppermute(x, AXES, [(i, (i + by * ways) % count) for i in range(count)])]
    dynamic_update_slice x36 -> x0, local copies, waits for them, and re-layouts: 33.5 us -> none  [partial_attention(): lax.map(one_head, (query_heads, key_heads, value_heads))]
    pallas_call x0 -> x2, Pallas kernels: none -> 25 us  [the longest x1 15.7 us: local_attention(): pl.pallas_call(functools.partial(local_kernel, tiles), grid=(heads, 2), i...]
    all_to_all x3, waiting for transfers between devices: 30.1 us -> 11.7 us  [exchange(): lax.all_to_all(x, AXES, split_axis=0, concat_axis=0, tiled=True, axis_ind...]
    reduce_sum x18 -> x0, other arithmetic: 15.6 us -> none  [one_head(): row_sum = jnp.sum(weights, axis=1)]
    ppermute x4 -> x0, local copies, waits for them, and re-layouts: 8.92 us -> none  [shifted(): lax.ppermute(value, axis, [(i, (i + by) % length) for i in range(length)])]
  transfers between devices with their start and end apart: 7 -> 10, of which waited for: 3 -> 5; matrix products, arithmetic and copies ran while one was open for 34% -> 14% of each run, Pallas kernels for 0% -> 10%
where the time goes in v1:
time: 152 us; the launch traced here: 151 us
  waiting for transfers between devices  48.9 us (32%)
  Pallas kernels  25 us (16%)
  starting transfers between devices  24.3 us (16%)
  local copies, waits for them, and re-layouts  22.6 us (15%)
  blocking collectives  20.3 us (13%)
  other arithmetic  9.38 us (6%)
    ppermute x6, waiting for transfers between devices, shifted(): lax.ppermute(x, AXES, [(i, (i + by * ways) % count) for i in range(count)])  28.1 us
    all_to_all x1, blocking collectives, exchange(): lax.all_to_all(x, AXES, split_axis=0, concat_axis=0, tiled=True, axis_ind...  20.3 us
    pallas_call x1, Pallas kernels, local_attention(): pl.pallas_call(functools.partial(local_kernel, tiles), grid=(heads, 2), i...  15.7 us
    all_to_all x3, starting transfers between devices, exchange(): lax.all_to_all(x, AXES, split_axis=0, concat_axis=0, tiled=True, axis_ind...  12.4 us
    all_to_all x3, waiting for transfers between devices, exchange(): lax.all_to_all(x, AXES, split_axis=0, concat_axis=0, tiled=True, axis_ind...  11.7 us
    ppermute x6, starting transfers between devices, shifted(): lax.ppermute(x, AXES, [(i, (i + by * ways) % count) for i in range(count)])  9.94 us
    pallas_call x1, Pallas kernels, halo_attention(): pl.pallas_call(functools.partial(halo_kernel, tiles), grid=(heads, 2), in...  9.23 us
    ppermute x1, waiting for transfers between devices, swapped(): return lax.ppermute(x, AXES, [(i, flip(i)) for i in range(count)])  9.1 us
  transfers between devices with their start and end apart: 10, of which 5 were waited for; matrix products, arithmetic and copies ran while one was open for 14% of the time, Pallas kernels for 10%

profile of v1, /device:TPU:0, one launch (start us, length us, event | category | flops | bytes accessed | tf_op | source)
XLA Modules:
  0.0 151.3 jit_solution(973140826779275997)
XLA Ops:
  0.0 3.3 %reshape.209 = bf16[192,4,2,384]{3,2,1,0:T(2,128)(2,1)S(1)} reshape(bf16[192,3072]{1,0:T(8,128)(2,1)} %param.9) | data formatting | bytes 2359296 | tf_op jit(solution)/shard_map/reshape | solution.py:175
  3.3 1.2 copy.24
  4.5 0.0 copy-start.2
  4.5 5.3 %all-to-all-start.1 = ((bf16[8,192,384]{2,1,0:T(8,128)(2,1)}), bf16[8,192,384]{2,1,0:T(8,128)(2,1)S(1)}, u32[]{:S(2)}, u32[]{:S(2)}) async-start(bf16[8,192,384]{2,1,0:T(8,128)(2,1)} %bitcast.8), calls=%async_computation.1 | async-start | bytes 2359296 | tf_op jit(solution)/shard_map/all_to_all | solution.py:170
  9.9 0.0 copy-done.8
  9.9 0.6 stack.20
  10.5 0.0 copy-done.9
  10.5 0.6 stack.21
  11.1 0.0 copy-done.12
  11.1 0.1 iota_compare_fusion
  11.2 0.0 copy-done.11
  11.2 0.5 and_reduce_fusion.2
  11.7 0.1 pad_add_fusion
  11.8 0.1 convert_element_type.32
  11.8 0.0 copy-done.2
  11.9 0.9 reshape.211
  12.8 1.2 copy.25
  14.0 11.7 %all-to-all-done.1 = bf16[8,192,384]{2,1,0:T(8,128)(2,1)S(1)} async-done(((bf16[8,192,384]{2,1,0:T(8,128)(2,1)}), bf16[8,192,384]{2,1,0:T(8,128)(2,1)S(1)}, u32[]{:S(2)}, u32[]{:S(2)}) %all-to-all-start.1) | async-done | bytes 1179680 | tf_op jit(solution)/shard_map/all_to_all | solution.py:170
  25.7 3.6 %all-to-all-start.2 = ((bf16[8,192,384]{2,1,0:T(8,128)(2,1)}), bf16[8,192,384]{2,1,0:T(8,128)(2,1)S(1)}, u32[]{:S(2)}, u32[]{:S(2)}) async-start(bf16[8,192,384]{2,1,0:T(8,128)(2,1)} %bitcast.12), calls=%async_computation.2 | async-start | bytes 2359296 | tf_op jit(solution)/shard_map/all_to_all | solution.py:170
  29.3 0.6 pad_maximum_fusion.5
  30.0 1.9 %collective-permute-start = (bf16[3,32,384]{2,1,0:T(8,128)(2,1)}, bf16[3,32,384]{2,1,0:T(8,128)(2,1)}, u32[]{:S(2)}, u32[]{:S(2)}) collective-permute-start(bf16[3,32,384]{2,1,0:T(8,128)(2,1)} %pad_maximum_fusion.5), channel_id=1, source_target_pairs={{0,4},{1,5},{2,6},{3,7},{4,0},{5,1},{6,2},{7,3},{8,12},{9,13},{10,... | collective-permute-start | bytes 221192 | tf_op jit(solution)/shard_map/ppermute | solution.py:167
  32.6 3.3 %reshape.206 = bf16[192,4,2,384]{3,2,1,0:T(2,128)(2,1)S(1)} reshape(bf16[192,3072]{1,0:T(8,128)(2,1)} %param.8) | data formatting | bytes 2359296 | tf_op jit(solution)/shard_map/reshape | solution.py:175
  35.9 1.2 copy.23
  37.1 0.6 compare_select_fusion.2
  37.6 9.1 %collective-permute-done = bf16[3,32,384]{2,1,0:T(8,128)(2,1)} collective-permute-done((bf16[3,32,384]{2,1,0:T(8,128)(2,1)}, bf16[3,32,384]{2,1,0:T(8,128)(2,1)}, u32[]{:S(2)}, u32[]{:S(2)}) %collective-permute-start) | collective-permute-done | bytes 73760 | tf_op jit(solution)/shard_map/ppermute | solution.py:167
  46.7 0.8 bitcast_select_fusion.1
  47.6 0.0 copy-start.3
  47.6 0.0 copy-start.4
  47.6 0.6 copy-done.3
  48.2 0.6 pad_maximum_fusion.4
  48.8 1.6 %collective-permute-start.5 = (bf16[2,64,384]{2,1,0:T(8,128)(2,1)}, bf16[2,64,384]{2,1,0:T(8,128)(2,1)}, u32[]{:S(2)}, u32[]{:S(2)}) collective-permute-start(bf16[2,64,384]{2,1,0:T(8,128)(2,1)} %pad_maximum_fusion.4), channel_id=1, source_target_pairs={{0,8},{1,9},{2,10},{3,11},{4,12},{5,13},{6,14},{7,15},{8,16},{9,17... | collective-permute-start | bytes 294920 | tf_op jit(solution)/shard_map/ppermute | solution.py:163
  50.4 0.7 slice_reduce_fusion
  51.1 0.1 reshape_squeeze.3
  51.2 0.7 broadcast_select_fusion.1
  51.9 0.0 all-to-all-done.2
  51.9 3.6 %all-to-all-start = ((bf16[8,192,384]{2,1,0:T(8,128)(2,1)}), bf16[8,192,384]{2,1,0:T(8,128)(2,1)S(1)}, u32[]{:S(2)}, u32[]{:S(2)}) async-start(bf16[8,192,384]{2,1,0:T(8,128)(2,1)} %bitcast.37), calls=%async_computation | async-start | bytes 2359296 | tf_op jit(solution)/shard_map/all_to_all | solution.py:170
  55.4 0.1 collective-permute-done.5
  55.6 1.6 %pad_maximum_fusion.3 = bf16[2,128,384]{2,1,0:T(8,128)(2,1)} fusion(bf16[2,64,384]{2,1,0:T(8,128)(2,1)} %collective-permute-done.5, bf16[2,32,384]{2,1,0:T(8,128)(2,1)} %copy-done.4, bf16[2,32,384]{2,1,0:T(8,128)(2,1)} %copy-done.3), kind=kLoop, calls=%fused_computation.6 | loop fusion | flops 589824 | bytes 393216 | tf_op jit(solution)/shard_map/concatenate | solution.py:199
  57.2 2.5 %collective-permute-start.6 = (bf16[2,128,384]{2,1,0:T(8,128)(2,1)}, bf16[2,128,384]{2,1,0:T(8,128)(2,1)}, u32[]{:S(2)}, u32[]{:S(2)}) collective-permute-start(bf16[2,128,384]{2,1,0:T(8,128)(2,1)} %pad_maximum_fusion.3), channel_id=1, source_target_pairs={{0,16},{1,17},{2,18},{3,19},{4,20},{5,21},{6,22},{7,23},{8,24},{9,... | collective-permute-start | bytes 589832 | tf_op jit(solution)/shard_map/ppermute | solution.py:163
  59.7 1.2 fusion.7
  60.8 0.2 collective-permute-start.3
  61.1 3.6 %collective-permute-start.4 = (bf16[4,192,384]{2,1,0:T(8,128)(2,1)}, bf16[4,192,384]{2,1,0:T(8,128)(2,1)}, u32[]{:S(2)}, u32[]{:S(2)}) collective-permute-start(bf16[4,192,384]{2,1,0:T(8,128)(2,1)} %get-tuple-element.13), channel_id=1, source_target_pairs={{0,24},{1,25},{2,26},{3,27},{4,28},{5,29},{6,30},{7,31},{8,0},{9,1... | collective-permute-start | bytes 1769480 | tf_op jit(solution)/shard_map/ppermute | solution.py:163
  64.7 1.2 fusion.8
  65.8 0.0 collective-permute-start.2
  65.8 2.0 %collective-permute-start.1 = (bf16[4,192,384]{2,1,0:T(8,128)(2,1)}, bf16[4,192,384]{2,1,0:T(8,128)(2,1)}, u32[]{:S(2)}, u32[]{:S(2)}) collective-permute-start(bf16[4,192,384]{2,1,0:T(8,128)(2,1)} %get-tuple-element.14), channel_id=1, source_target_pairs={{0,8},{1,9},{2,10},{3,11},{4,12},{5,13},{6,14},{7,15},{8,16},{9,17... | collective-permute-start | bytes 1769480 | tf_op jit(solution)/shard_map/ppermute | solution.py:163
  67.9 0.1 select_n.129.bias
  67.9 15.1 %collective-permute-done.6 = bf16[2,128,384]{2,1,0:T(8,128)(2,1)} collective-permute-done((bf16[2,128,384]{2,1,0:T(8,128)(2,1)}, bf16[2,128,384]{2,1,0:T(8,128)(2,1)}, u32[]{:S(2)}, u32[]{:S(2)}) %collective-permute-start.6) | collective-permute-done | bytes 196640 | tf_op jit(solution)/shard_map/ppermute | solution.py:163
  83.0 1.0 pad_maximum_fusion.2
  84.0 0.8 slice_bitcast_fusion
  84.8 0.0 all-to-all-done
  84.8 0.8 broadcast_in_dim.20.tb_ref
  85.6 0.9 copy-done
  86.5 0.9 copy-done.1
  87.5 15.7 %shard_map.82 = (f32[3,2,128,768]{3,2,1,0:T(8,128)}, f32[3,2,2,768]{3,2,1,0:T(2,128)S(1)}) custom-call(f32[216]{0:T(256)S(1)} %select_n.129.bias, bf16[1536,384]{1,0:T(8,128)(2,1)S(1)} %bitcast.32, bf16[1536,384]{1,0:T(8,128)(2,1)S(1)} %bitcast.34, bf16[1536,384]{1,0:T(8,128)(2,1)S(1)} %bitcast.35, bf16[256,384]{1,0:T(8,128)(2,1)S(1)} %copy-done.1, ...), custom_call_target="tpu_custom_call" | custom-call | tf_op jit(solution)/shard_map/pallas_call | solution.py:101
  103.2 0.0 collective-permute-done.3
  103.2 0.0 collective-permute-done.4
  103.2 1.4 pad_maximum_fusion.1.v_ref
  104.6 12.9 %collective-permute-done.2 = bf16[4,192,384]{2,1,0:T(8,128)(2,1)} collective-permute-done((bf16[4,192,384]{2,1,0:T(8,128)(2,1)}, bf16[4,192,384]{2,1,0:T(8,128)(2,1)}, u32[]{:S(2)}, u32[]{:S(2)}) %collective-permute-start.2) | collective-permute-done | bytes 589856 | tf_op jit(solution)/shard_map/ppermute | solution.py:163
  117.5 0.0 collective-permute-done.1
  117.5 1.4 pad_maximum_fusion.k_ref
  118.9 9.2 %shard_map.83 = bf16[1536,384]{1,0:T(8,128)(2,1)S(1)} custom-call(f32[216]{0:T(256)S(1)} %select_n.129.bias, bf16[1536,384]{1,0:T(8,128)(2,1)S(1)} %bitcast.33, bf16[2,768,384]{2,1,0:T(8,128)(2,1)S(1)} %pad_maximum_fusion.k_ref, bf16[2,768,384]{2,1,0:T(8,128)(2,1)S(1)} %pad_maximum_fusion.1.v_ref, f32[3,2,128,768]{3,2,1,0:T(8,128)} %get-tuple-element.7.sum_ref, ...), custom_call_target="tpu_custom_call" | custom-call | tf_op jit(solution)/shard_map/pallas_call | solution.py:129
  128.1 20.3 %all_to_all.20 = bf16[8,192,384]{2,1,0:T(8,128)(2,1)S(1)} all-to-all(bf16[8,192,384]{2,1,0:T(8,128)(2,1)S(1)} %bitcast.36), channel_id=1, replica_groups={{0,1,2,3,4,5,6,7},{8,9,10,11,12,13,14,15},{16,17,18,19,20,21,22,23},{24..., dimensions={0} | all-to-all | bytes 2359296 | tf_op jit(solution)/shard_map/all_to_all | solution.py:170
  148.4 1.2 copy.30
  149.6 1.7 %reshape.217 = bf16[192,3072]{1,0:T(8,128)(2,1)} reshape(bf16[192,4,2,384]{3,2,1,0:T(2,128)(2,1)S(1)} %bitcast.39) | data formatting | bytes 2359296 | tf_op jit(solution)/shard_map/reshape | solution.py:221
  (22 shorter events, 0.1 us)
Async XLA Ops:
  4.5 5.4 %copy-start.8 = (bf16[32,768]{1,0:T(8,128)(2,1)S(1)}, bf16[32,768]{1,0:T(8,128)(2,1)}, u32[]{:S(2)}) copy-start(bf16[32,768]{1,0:T(8,128)(2,1)} %param.11) | copy-start | bytes 147460
  4.5 6.0 %copy-start.9 = (bf16[32,768]{1,0:T(8,128)(2,1)S(1)}, bf16[32,768]{1,0:T(8,128)(2,1)}, u32[]{:S(2)}) copy-start(bf16[32,768]{1,0:T(8,128)(2,1)} %param.12) | copy-start | bytes 147460
  4.5 6.6 %copy-start.12 = (s32[6]{0:T(128)S(1)}, s32[6]{0:T(128)}, u32[]{:S(2)}) copy-start(s32[6]{0:T(128)} %param.14) | copy-start | bytes 76
  4.5 6.7 %copy-start.11 = (s32[6,12]{1,0:T(8,128)S(1)}, s32[6,12]{1,0:T(8,128)}, u32[]{:S(2)}) copy-start(s32[6,12]{1,0:T(8,128)} %param.13) | copy-start | bytes 868
  4.5 7.3 %copy-start.2 = (bf16[192,3072]{1,0:T(8,128)(2,1)S(1)}, bf16[192,3072]{1,0:T(8,128)(2,1)}, u32[]{:S(2)}) copy-start(bf16[192,3072]{1,0:T(8,128)(2,1)} %param.10) | copy-start | bytes 3538948
  4.5 21.2 %all-to-all-start.1 = ((bf16[8,192,384]{2,1,0:T(8,128)(2,1)}), bf16[8,192,384]{2,1,0:T(8,128)(2,1)S(1)}, u32[]{:S(2)}, u32[]{:S(2)}) async-start(bf16[8,192,384]{2,1,0:T(8,128)(2,1)} %bitcast.8), calls=%async_computation.1 | async-start | bytes 2359296 | tf_op jit(solution)/shard_map/all_to_all | solution.py:170
  12.8 1.2 copy-start.7
  12.8 1.2 copy-start.6
  14.0 15.3 %copy-start.5 = (bf16[2,32,2,384]{3,1,0,2:T(8,128)(2,1)}, bf16[2,32,2,384]{3,1,0,2:T(8,128)(2,1)S(1)}, u32[]{:S(2)}) copy-start(bf16[2,32,2,384]{3,1,0,2:T(8,128)(2,1)S(1)} %copy_dynamic-update-slice_fusion) | copy-start | bytes 294916
  25.7 26.2 %all-to-all-start.2 = ((bf16[8,192,384]{2,1,0:T(8,128)(2,1)}), bf16[8,192,384]{2,1,0:T(8,128)(2,1)S(1)}, u32[]{:S(2)}, u32[]{:S(2)}) async-start(bf16[8,192,384]{2,1,0:T(8,128)(2,1)} %bitcast.12), calls=%async_computation.2 | async-start | bytes 2359296 | tf_op jit(solution)/shard_map/all_to_all | solution.py:170
  30.0 16.8 %collective-permute-start = (bf16[3,32,384]{2,1,0:T(8,128)(2,1)}, bf16[3,32,384]{2,1,0:T(8,128)(2,1)}, u32[]{:S(2)}, u32[]{:S(2)}) collective-permute-start(bf16[3,32,384]{2,1,0:T(8,128)(2,1)} %pad_maximum_fusion.5), channel_id=1, source_target_pairs={{0,4},{1,5},{2,6},{3,7},{4,0},{5,1},{6,2},{7,3},{8,12},{9,13},{10,... | collective-permute-start | bytes 221192 | tf_op jit(solution)/shard_map/ppermute | solution.py:167
  47.6 0.6 copy-start.3
  47.6 1.2 copy-start.4
  48.8 6.7 %collective-permute-start.5 = (bf16[2,64,384]{2,1,0:T(8,128)(2,1)}, bf16[2,64,384]{2,1,0:T(8,128)(2,1)}, u32[]{:S(2)}, u32[]{:S(2)}) collective-permute-start(bf16[2,64,384]{2,1,0:T(8,128)(2,1)} %pad_maximum_fusion.4), channel_id=1, source_target_pairs={{0,8},{1,9},{2,10},{3,11},{4,12},{5,13},{6,14},{7,15},{8,16},{9,17... | collective-permute-start | bytes 294920 | tf_op jit(solution)/shard_map/ppermute | solution.py:163
  51.9 33.0 %all-to-all-start = ((bf16[8,192,384]{2,1,0:T(8,128)(2,1)}), bf16[8,192,384]{2,1,0:T(8,128)(2,1)S(1)}, u32[]{:S(2)}, u32[]{:S(2)}) async-start(bf16[8,192,384]{2,1,0:T(8,128)(2,1)} %bitcast.37), calls=%async_computation | async-start | bytes 2359296 | tf_op jit(solution)/shard_map/all_to_all | solution.py:170
  57.2 25.8 %collective-permute-start.6 = (bf16[2,128,384]{2,1,0:T(8,128)(2,1)}, bf16[2,128,384]{2,1,0:T(8,128)(2,1)}, u32[]{:S(2)}, u32[]{:S(2)}) collective-permute-start(bf16[2,128,384]{2,1,0:T(8,128)(2,1)} %pad_maximum_fusion.3), channel_id=1, source_target_pairs={{0,16},{1,17},{2,18},{3,19},{4,20},{5,21},{6,22},{7,23},{8,24},{9,... | collective-permute-start | bytes 589832 | tf_op jit(solution)/shard_map/ppermute | solution.py:163
  60.8 42.4 %collective-permute-start.3 = (bf16[4,192,384]{2,1,0:T(8,128)(2,1)}, bf16[4,192,384]{2,1,0:T(8,128)(2,1)}, u32[]{:S(2)}, u32[]{:S(2)}) collective-permute-start(bf16[4,192,384]{2,1,0:T(8,128)(2,1)} %get-tuple-element.12), channel_id=1, source_target_pairs={{0,8},{1,9},{2,10},{3,11},{4,12},{5,13},{6,14},{7,15},{8,16},{9,17... | collective-permute-start | bytes 1769480 | tf_op jit(solution)/shard_map/ppermute | solution.py:163
  61.1 6.8 %copy-start.10 = (bf16[1,6,18]{2,1,0:T(8,128)(2,1)S(1)}, bf16[1,6,18]{2,1,0:T(8,128)(2,1)}, u32[]{:S(2)}) copy-start(bf16[1,6,18]{2,1,0:T(8,128)(2,1)} %get-tuple-element.21) | copy-start | bytes 652
  61.1 42.1 %collective-permute-start.4 = (bf16[4,192,384]{2,1,0:T(8,128)(2,1)}, bf16[4,192,384]{2,1,0:T(8,128)(2,1)}, u32[]{:S(2)}, u32[]{:S(2)}) collective-permute-start(bf16[4,192,384]{2,1,0:T(8,128)(2,1)} %get-tuple-element.13), channel_id=1, source_target_pairs={{0,24},{1,25},{2,26},{3,27},{4,28},{5,29},{6,30},{7,31},{8,0},{9,1... | collective-permute-start | bytes 1769480 | tf_op jit(solution)/shard_map/ppermute | solution.py:163
  65.8 51.7 %collective-permute-start.2 = (bf16[4,192,384]{2,1,0:T(8,128)(2,1)}, bf16[4,192,384]{2,1,0:T(8,128)(2,1)}, u32[]{:S(2)}, u32[]{:S(2)}) collective-permute-start(bf16[4,192,384]{2,1,0:T(8,128)(2,1)} %get-tuple-element.15), channel_id=1, source_target_pairs={{0,24},{1,25},{2,26},{3,27},{4,28},{5,29},{6,30},{7,31},{8,0},{9,1... | collective-permute-start | bytes 1769480 | tf_op jit(solution)/shard_map/ppermute | solution.py:163
  65.8 51.7 %collective-permute-start.1 = (bf16[4,192,384]{2,1,0:T(8,128)(2,1)}, bf16[4,192,384]{2,1,0:T(8,128)(2,1)}, u32[]{:S(2)}, u32[]{:S(2)}) collective-permute-start(bf16[4,192,384]{2,1,0:T(8,128)(2,1)} %get-tuple-element.14), channel_id=1, source_target_pairs={{0,8},{1,9},{2,10},{3,11},{4,12},{5,13},{6,14},{7,15},{8,16},{9,17... | collective-permute-start | bytes 1769480 | tf_op jit(solution)/shard_map/ppermute | solution.py:163
  85.6 0.9 copy-start
  86.5 0.9 copy-start.1

commit v2 on v1

v2 whole, which is shorter than its diff:
```python
import functools
import math

import jax
import jax.numpy as jnp
from jax import lax
from jax.experimental import pallas as pl
from jax.experimental.pallas import tpu as pltpu
from jax.sharding import PartitionSpec as P

HD = 128
TILE = 128
AXES = ("frame", "head")
SCALE = math.log2(math.e) / math.sqrt(HD)
LOW = -1e30
NT = (((1,), (1,)), ((), ()))
SMEM = pl.BlockSpec(memory_space=pltpu.SMEM)
ANY = pl.BlockSpec(memory_space=pl.ANY)
SMALL = pltpu.CompilerParams(vmem_limit_bytes=12 << 20)
LARGE = pltpu.CompilerParams(vmem_limit_bytes=24 << 20)


def weigh(queries, keys, biases):
    scores = lax.dot_general(keys, queries, NT, preferred_element_type=jnp.float32)
    key_tiles, query_tiles = keys.shape[0] // TILE, queries.shape[0] // TILE
    tops, totals, weights = [], [], []
    for t in range(query_tiles):
        blocks = [
            scores[u * TILE : (u + 1) * TILE, t * TILE : (t + 1) * TILE] + biases[u][t]
            for u in range(key_tiles)
        ]
        top = functools.reduce(jnp.maximum, blocks)
        top = jnp.max(top, axis=0, keepdims=True)
        parts = [jnp.exp2((block - top) * SCALE) for block in blocks]
        total = functools.reduce(jnp.add, parts)
        tops.append(top)
        totals.append(jnp.sum(total, axis=0, keepdims=True))
        weights.append(jnp.concatenate([p.astype(jnp.bfloat16) for p in parts], axis=0))
    join = lambda parts: jnp.concatenate(parts, axis=1)
    return join(weights), join(tops), join(totals)


def group(queries, keys, values_t, biases):
    weights, top, total = weigh(queries, keys, biases)
    return jnp.dot(values_t, weights, preferred_element_type=jnp.float32), top, total


def merge(one, two):
    top = jnp.maximum(one[1], two[1])
    first, second = jnp.exp2((one[1] - top) * SCALE), jnp.exp2((two[1] - top) * SCALE)
    return one[0] * first + two[0] * second, top, one[2] * first + two[2] * second


def flat(block):
    return block.reshape(-1, block.shape[-1])


def near_kernel(
    tiles,
    bias,
    q_ref,
    v_ref,
    k_ref,
    before_ref,
    after_ref,
    keep_ref,
    got_ref,
    text_ref,
    near_ref,
    far_ref,
    scale_ref,
):
    side = pl.program_id(1)
    half, rows = k_ref.shape[0] // 2, keep_ref.shape[1]
    own, other = pl.ds(side * half, half), pl.ds((1 - side) * half, half)
    queries = flat(q_ref[:, 0])
    at = lambda t, u: bias[side * 8 + t, u]
    span = range(tiles)
    own_bias = [[at(t, u) for t in span] for u in span]
    own_bias += [
        [text_ref[j * TILE : (j + 1) * TILE, :]] * tiles for j in range(text_ref.shape[0] // TILE)
    ]
    mine = group(
        queries,
        jnp.concatenate([flat(k_ref[own]), keep_ref[0], got_ref[0, :rows]], axis=0),
        jnp.concatenate([flat(v_ref[own, 0]), keep_ref[1], got_ref[1, :rows]], axis=0).T,
        own_bias,
    )
    near = group(
        queries,
        flat(k_ref[other]),
        flat(v_ref[other, 0]).T,
        [[at(t, tiles + u) for t in span] for u in span],
    )
    weights, far_top, far_total = weigh(
        queries,
        jnp.where(side == 0, flat(before_ref[...]), flat(after_ref[...])),
        [[at(t, 2 * tiles + u) for t in span] for u in span],
    )
    weighted, top, total = merge(mine, near)
    best = jnp.maximum(top, far_top)
    near_scale, far_scale = jnp.exp2((top - best) * SCALE), jnp.exp2((far_top - best) * SCALE)
    total = total * near_scale + far_total * far_scale
    near_ref[0, 0] = weighted * (near_scale / total)
    far_ref[0, 0] = weights
    scale_ref[0, 0] = far_scale / total


def far_kernel(before_ref, after_ref, near_ref, far_ref, scale_ref, out_ref):
    side = pl.program_id(1)
    values = jnp.where(side == 0, flat(before_ref[...]), flat(after_ref[...])).T
    far = jnp.dot(values, far_ref[0, 0], preferred_element_type=jnp.float32)
    out = near_ref[0, 0] + far * scale_ref[0, 0]
    out_ref[...] = out.T.astype(out_ref.dtype).reshape(out_ref.shape)


def near_attention(tiles, bias, vq, k, k_before, k_after, keep, got, text_bias):
    ways, _, rows, part = vq.shape
    heads, half, length = part // HD, ways // 2, tiles * TILE
    far = pl.BlockSpec((half, rows, HD), lambda h, s: (0, 0, h))
    at = lambda h, s: (h, s, 0, 0)
    return pl.pallas_call(
        functools.partial(near_kernel, tiles),
        grid=(heads, 2),
        in_specs=[
            SMEM,
            pl.BlockSpec((half, 1, rows, HD), lambda h, s: (s, 1, 0, h)),
            pl.BlockSpec((ways, 1, rows, HD), lambda h, s: (0, 0, 0, h)),
            pl.BlockSpec((ways, rows, HD), lambda h, s: (0, 0, h)),
            far,
            far,
            pl.BlockSpec((2, keep.shape[1], HD), lambda h, s: (0, 0, h)),
            pl.BlockSpec((2, got.shape[1], HD), lambda h, s: (0, 0, h)),
            pl.BlockSpec(text_bias.shape, lambda h, s: (0, 0)),
        ],
        out_specs=[
            pl.BlockSpec((1, 1, HD, length), at),
            pl.BlockSpec((1, 1, length, length), at),
            pl.BlockSpec((1, 1, 1, length), at),
        ],
        out_shape=[
            jax.ShapeDtypeStruct((heads, 2, HD, length), jnp.float32),
            jax.ShapeDtypeStruct((heads, 2, length, length), jnp.bfloat16),
            jax.ShapeDtypeStruct((heads, 2, 1, length), jnp.float32),
        ],
        compiler_params=LARGE,
    )(bias, vq, vq, k, k_before, k_after, keep, got, text_bias)


def far_attention(v_before, v_after, near, weights, scales):
    half, rows, part = v_before.shape
    heads, length = part // HD, half * rows
    far = pl.BlockSpec((half, rows, HD), lambda h, s: (0, 0, h))
    at = lambda h, s: (h, s, 0, 0)
    return pl.pallas_call(
        far_kernel,
        grid=(heads, 2),
        in_specs=[
            far,
            far,
            pl.BlockSpec((1, 1, HD, length), at),
            pl.BlockSpec((1, 1, length, length), at),
            pl.BlockSpec((1, 1, 1, length), at),
        ],
        out_specs=pl.BlockSpec((half, rows, HD), lambda h, s: (s, 0, h)),
        out_shape=jax.ShapeDtypeStruct((2 * half, rows, part), jnp.bfloat16),
        compiler_params=LARGE,
    )(v_before, v_after, near, weights, scales)


def split_kernel(order, count, *refs):
    out_ref = refs[-1]
    part = out_ref.shape[-1]
    for i, x_ref in enumerate(refs[:count]):
        for p, g in enumerate(order):
            if count == 1:
                out_ref[p] = x_ref[:, g * part : (g + 1) * part]
            else:
                out_ref[p, i] = x_ref[:, g * part : (g + 1) * part]


def join_kernel(order, x_ref, out_ref):
    part = x_ref.shape[2]
    for p, g in enumerate(order):
        out_ref[:, g * part : (g + 1) * part] = x_ref[p]


def split_heads(order, arrays, first=()):
    rows, width = arrays[0].shape
    ways, count = len(order), len(arrays)
    shape = (ways, count, rows, width // ways) if count > 1 else (ways, rows, width // ways)
    return pl.pallas_call(
        functools.partial(split_kernel, order, count),
        in_specs=[pl.BlockSpec()] * count + [ANY] * len(first),
        out_shape=jax.ShapeDtypeStruct(shape, jnp.bfloat16),
        compiler_params=SMALL,
    )(*arrays, *first)


def join_heads(x, order):
    ways, rows, part = x.shape
    return pl.pallas_call(
        functools.partial(join_kernel, order),
        out_shape=jax.ShapeDtypeStruct((rows, ways * part), x.dtype),
        compiler_params=SMALL,
    )(x)


def mask_kernel(tiles, place, list_ref, count_ref, k_ref, v_ref, mask_ref, text_ref):
    text_ref[0] = k_ref[...]
    text_ref[1] = v_ref[...]
    lane = lax.broadcasted_iota(jnp.int32, (tiles, TILE), 1)
    ids = jnp.where(lane < tiles, place[0] * tiles + lane, place[1] * tiles + lane - tiles)
    ids = jnp.where(lane < 2 * tiles, ids, place[2] * tiles + lane - 2 * tiles)
    mask = jnp.zeros((tiles, TILE), jnp.float32)
    for i in range(list_ref.shape[1]):
        hit = (list_ref[:, i : i + 1] == ids) & (count_ref[...] > i)
        mask = jnp.where(hit, 1.0, mask)
    spare = jnp.zeros((mask_ref.shape[0] - tiles, TILE), jnp.float32)
    mask_ref[...] = jnp.concatenate([mask, spare], axis=0).astype(jnp.bfloat16)


def turn_kernel(pieces, place, mask_ref, *refs):
    texts, (offer_ref, keep_ref) = refs[:pieces], refs[-2:]
    low = place[3] == 0
    part = offer_ref.shape[2]
    for i in range(2):
        one = jnp.concatenate([t[i, :, :part] for t in texts], axis=0)
        two = jnp.concatenate([t[i, :, part:] for t in texts], axis=0)
        offer_ref[i, : one.shape[0]] = jnp.where(low, two, one)
        keep_ref[i] = jnp.where(low, one, two)
    offer_ref[0, keep_ref.shape[1] :, 0:TILE] = mask_ref[...]


def halves_kernel(vq_ref, _, __, ___, low_ref, high_ref):
    half = low_ref.shape[0]
    low_ref[...] = vq_ref[:half, 0]
    high_ref[...] = vq_ref[half:, 0]


def bias_kernel(pairs, rows, place, mask_ref, got_ref, bias_ref, text_ref):
    low = place[3] == 0
    start = got_ref.shape[1] - mask_ref.shape[0]
    mine, theirs = mask_ref[...], got_ref[0, start:, 0:TILE]
    for i, block in enumerate((jnp.where(low, mine, theirs), jnp.where(low, theirs, mine))):
        block = block.astype(jnp.float32)[0:8]
        bias_ref[8 * i : 8 * i + 8, :] = jnp.where(block > 0.5, 0.0, LOW)
    spot = lax.broadcasted_iota(jnp.int32, text_ref.shape, 0)
    spread = pairs * rows
    side = jnp.where(spot < spread, place[3], 1 - place[3])
    spot = jnp.where(spot < spread, spot, spot - spread)
    pair = place[4] - spot // rows
    pair = jnp.where(pair < 0, pair + pairs, pair)
    token = (2 * pair + side) * rows + spot % rows
    text_ref[...] = jnp.where(token < place[5], 0.0, LOW)


def body(queries, keys, values, text_keys, text_values, lists, counts, text_len):
    slabs, heads = lax.axis_size("frame"), lax.axis_size("head")
    slab = lax.axis_index("frame")
    pair, side = slab // 2, slab % 2
    ways, pairs = 2 * heads, slabs // 2
    tiles = lists.shape[0]
    rows, width = queries.shape
    part = width // ways
    count = slabs * heads
    groups = [list(range(ways * i, ways * (i + 1))) for i in range(pairs)]
    order = [2 * h + x for x in range(2) for h in range(heads)]

    def shifted(x, by):
        return lax.ppermute(x, AXES, [(i, (i + by * ways) % count) for i in range(count)])

    def swapped(x):
        flip = lambda i: i // ways * ways + (i + heads) % ways
        return lax.ppermute(x, AXES, [(i, flip(i)) for i in range(count)])

    def exchange(x):
        return lax.all_to_all(
            x, AXES, split_axis=0, concat_axis=0, tiled=True, axis_index_groups=groups
        )

    k = exchange(split_heads(order, (keys,)))
    ahead, behind = (slab + 1) % slabs, (slab + slabs - 1) % slabs
    toward, away = jnp.where(side == 0, ahead, behind), jnp.where(side == 0, behind, ahead)
    place = jnp.stack([slab, toward, away, side, pair, text_len[0]]).astype(jnp.int32)
    text_rows = text_keys.shape[0]
    mask, text = pl.pallas_call(
        functools.partial(mask_kernel, tiles),
        in_specs=[SMEM] + [pl.BlockSpec()] * 4,
        out_shape=[
            jax.ShapeDtypeStruct((16, TILE), jnp.bfloat16),
            jax.ShapeDtypeStruct((2, *text_keys.shape), jnp.bfloat16),
        ],
        compiler_params=SMALL,
    )(place, lists, counts[:, None], text_keys, text_values)
    if pairs <= 4:
        texts = [text] + [shifted(text, by) for by in range(1, pairs)]
    else:
        have = 1
        while have < pairs:
            take = min(have, pairs - have)
            more = shifted(text[:, : take * text_rows], have)
            text, have = jnp.concatenate([text, more], axis=1), have + take
        texts = [text]
    all_text = pairs * text_rows
    offer, keep = pl.pallas_call(
        functools.partial(turn_kernel, len(texts)),
        in_specs=[SMEM] + [pl.BlockSpec()] * (1 + len(texts)),
        out_shape=[
            jax.ShapeDtypeStruct((2, all_text + mask.shape[0], part), jnp.bfloat16),
            jax.ShapeDtypeStruct((2, all_text, part), jnp.bfloat16),
        ],
        compiler_params=SMALL,
    )(place, mask, *texts)
    got = swapped(offer)

    bias, text_bias = pl.pallas_call(
        functools.partial(bias_kernel, pairs, text_rows),
        in_specs=[SMEM] + [pl.BlockSpec()] * 2,
        out_shape=[
            jax.ShapeDtypeStruct((16, TILE), jnp.float32),
            jax.ShapeDtypeStruct((2 * all_text, TILE), jnp.float32),
        ],
        compiler_params=SMALL,
    )(place, mask, got)

    k_before, k_after = shifted(k[heads:], 1), shifted(k[:heads], -1)
    vq = exchange(split_heads(order, (values, queries), (k, keep)))

    half = jax.ShapeDtypeStruct((heads, rows, part), jnp.bfloat16)
    v_low, v_high = pl.pallas_call(
        halves_kernel,
        in_specs=[pl.BlockSpec(), ANY, ANY, ANY],
        out_shape=[half, half],
        compiler_params=SMALL,
    )(vq, text_bias, k_before, k_after)
    v_before, v_after = shifted(v_high, 1), shifted(v_low, -1)
    partial = near_attention(tiles, bias, vq, k, k_before, k_after, keep, got, text_bias)
    out = far_attention(v_before, v_after, *partial)
    return join_heads(exchange(out), order)


def solution(mesh):
    in_specs = (
        P(AXES, None),
        P(AXES, None),
        P(AXES, None),
        P("frame", "head"),
        P("frame", "head"),
        P("frame", None),
        P("frame"),
        P(),
    )
    return jax.shard_map(
        body, mesh=mesh, in_specs=in_specs, out_specs=P(AXES, None), check_vma=False
    )
```

time: 152 us -> 124 us (0.82)
  waiting for transfers between devices: 48.9 us -> 38.7 us
  local copies, waits for them, and re-layouts: 22.6 us -> 12.8 us
  other arithmetic: 9.38 us -> 0 us
  Pallas kernels: 25 us -> 27.2 us
    ppermute x1, waiting for transfers between devices: 9.1 us -> 27.2 us  [swapped(): return lax.ppermute(x, AXES, [(i, flip(i)) for i in range(count)])]
    ppermute x6 -> x7, waiting for transfers between devices: 28.1 us -> 11.5 us  [shifted(): lax.ppermute(x, AXES, [(i, (i + by * ways) % count) for i in range(count)])]
    all_to_all x3 -> x2, waiting for transfers between devices: 11.7 us -> 0.01 us  [exchange(): lax.all_to_all(x, AXES, split_axis=0, concat_axis=0, tiled=True, axis_ind...]
    reshape x5 -> x0, local copies, waits for them, and re-layouts: 10.4 us -> none  [the longest x3 7.54 us: spread(): x = x.reshape(rows, heads, 2, part).transpose(2, 1, 0, 3)]
    unnamed x27 -> x52, local copies, waits for them, and re-layouts: 2.49 us -> 12.5 us
    concatenate x5 -> x0, other arithmetic: 3.99 us -> none  [the longest x2 2.63 us: body(): pieces, have = (jnp.concatenate([pieces, more], axis=1), have + take)]
    transpose x3 -> x0, local copies, waits for them, and re-layouts: 3.52 us -> none  [spread(): x = x.reshape(rows, heads, 2, part).transpose(2, 1, 0, 3)]
    ppermute x6 -> x7, starting transfers between devices: 9.94 us -> 13.3 us  [shifted(): lax.ppermute(x, AXES, [(i, (i + by * ways) % count) for i in range(count)])]
  transfers between devices with their start and end apart: 10 -> 10, of which waited for: 5 -> 4; matrix products, arithmetic and copies ran while one was open for 14% -> 0% of each run, Pallas kernels for 10% -> 18%
where the time goes in v2:
time: 124 us; the launch traced here: 123 us
  waiting for transfers between devices  38.7 us (31%)
  Pallas kernels  27.2 us (22%)
  starting transfers between devices  24.6 us (20%)
  blocking collectives  19.1 us (15%)
  local copies, waits for them, and re-layouts  12.8 us (10%)
    ppermute x1, waiting for transfers between devices, swapped(): return lax.ppermute(x, AXES, [(i, flip(i)) for i in range(count)])  27.2 us
    pallas_call x1, Pallas kernels, near_attention(): pl.pallas_call(functools.partial(near_kernel, tiles), grid=(heads, 2), in...  19.8 us
    all_to_all x1, blocking collectives, exchange(): lax.all_to_all(x, AXES, split_axis=0, concat_axis=0, tiled=True, axis_ind...  19.1 us
    ppermute x7, starting transfers between devices, shifted(): lax.ppermute(x, AXES, [(i, (i + by * ways) % count) for i in range(count)])  13.3 us
    unnamed x52, local copies, waits for them, and re-layouts  12.5 us
    ppermute x7, waiting for transfers between devices, shifted(): lax.ppermute(x, AXES, [(i, (i + by * ways) % count) for i in range(count)])  11.5 us
    all_to_all x2, starting transfers between devices, exchange(): lax.all_to_all(x, AXES, split_axis=0, concat_axis=0, tiled=True, axis_ind...  9.23 us
    pallas_call x1, Pallas kernels, far_attention(): pl.pallas_call(far_kernel, grid=(heads, 2), in_specs=[far, far, pl.BlockS...  3.03 us
  transfers between devices with their start and end apart: 10, of which 4 were waited for; matrix products, arithmetic and copies ran while one was open for 0% of the time, Pallas kernels for 18%

profile of v2, /device:TPU:0, one launch (start us, length us, event | category | flops | bytes accessed | tf_op | source)
XLA Modules:
  0.0 123.3 jit_solution(12795261810893851026)
XLA Ops:
  0.0 1.3 %copy-done.7 = bf16[192,3072]{1,0:T(8,128)(2,1)S(1)} copy-done((bf16[192,3072]{1,0:T(8,128)(2,1)S(1)}, bf16[192,3072]{1,0:T(8,128)(2,1)}, u32[]{:S(2)}) %copy-start.7) | copy-done | bytes 1179672
  1.3 1.1 shard_map.82
  2.4 5.3 %all-to-all-start = ((bf16[8,192,384]{2,1,0:T(8,128)(2,1)}), bf16[8,192,384]{2,1,0:T(8,128)(2,1)S(1)}, u32[]{:S(2)}, u32[]{:S(2)}) async-start(bf16[8,192,384]{2,1,0:T(8,128)(2,1)} %shard_map.82), calls=%async_computation | async-start | bytes 2359296 | tf_op jit(solution)/shard_map/all_to_all | solution.py:278
  8.4 0.0 copy-done.25
  8.4 0.1 copy.9.count_ref
  8.5 0.1 stack.23.place
  8.6 0.0 copy-done.22
  8.6 0.8 copy-done.18
  9.4 0.8 copy-done.19
  10.2 0.6 shard_map.83
  10.8 1.6 %collective-permute-start = (bf16[2,32,768]{2,1,0:T(8,128)(2,1)S(1)}, bf16[2,32,768]{2,1,0:T(8,128)(2,1)S(1)}, u32[]{:S(2)}, u32[]{:S(2)}) collective-permute-start(bf16[2,32,768]{2,1,0:T(8,128)(2,1)S(1)} %get-tuple-element.17.refs_0_), channel_id=1, source_target_pairs={{0,8},{1,9},{2,10},{3,11},{4,12},{5,13},{6,14},{7,15},{8,16},{9,17... | collective-permute-start | bytes 294920 | tf_op jit(solution)/shard_map/ppermute | solution.py:271
  12.4 2.6 %collective-permute-start.1 = (bf16[2,32,768]{2,1,0:T(8,128)(2,1)S(1)}, bf16[2,32,768]{2,1,0:T(8,128)(2,1)S(1)}, u32[]{:S(2)}, u32[]{:S(2)}) collective-permute-start(bf16[2,32,768]{2,1,0:T(8,128)(2,1)S(1)} %get-tuple-element.17.refs_0_), channel_id=1, source_target_pairs={{0,16},{1,17},{2,18},{3,19},{4,20},{5,21},{6,22},{7,23},{8,24},{9,... | collective-permute-start | bytes 294920 | tf_op jit(solution)/shard_map/ppermute | solution.py:271
  15.0 1.3 %collective-permute-start.2 = (bf16[2,32,768]{2,1,0:T(8,128)(2,1)S(1)}, bf16[2,32,768]{2,1,0:T(8,128)(2,1)S(1)}, u32[]{:S(2)}, u32[]{:S(2)}) collective-permute-start(bf16[2,32,768]{2,1,0:T(8,128)(2,1)S(1)} %get-tuple-element.17.refs_0_), channel_id=1, source_target_pairs={{0,24},{1,25},{2,26},{3,27},{4,28},{5,29},{6,30},{7,31},{8,0},{9,1... | collective-permute-start | bytes 294920 | tf_op jit(solution)/shard_map/ppermute | solution.py:271
  16.4 2.0 %collective-permute-done.refs_1_ = bf16[2,32,768]{2,1,0:T(8,128)(2,1)S(1)} collective-permute-done((bf16[2,32,768]{2,1,0:T(8,128)(2,1)S(1)}, bf16[2,32,768]{2,1,0:T(8,128)(2,1)S(1)}, u32[]{:S(2)}, u32[]{:S(2)}) %collective-permute-start) | collective-permute-done | bytes 98336 | tf_op jit(solution)/shard_map/ppermute | solution.py:271
  18.3 3.9 %collective-permute-done.1.refs_2_ = bf16[2,32,768]{2,1,0:T(8,128)(2,1)S(1)} collective-permute-done((bf16[2,32,768]{2,1,0:T(8,128)(2,1)S(1)}, bf16[2,32,768]{2,1,0:T(8,128)(2,1)S(1)}, u32[]{:S(2)}, u32[]{:S(2)}) %collective-permute-start.1) | collective-permute-done | bytes 98336 | tf_op jit(solution)/shard_map/ppermute | solution.py:271
  22.2 0.0 collective-permute-done.2.refs_3_
  22.2 0.6 shard_map.84
  22.8 0.0 copy-start.12
  22.8 0.7 copy-done.12
  23.5 0.7 copy-done.23
  24.2 0.0 all-to-all-done.refs_2_.k_ref
  24.2 0.0 copy-done.8
  24.2 0.0 copy-done.9
  24.2 0.0 copy-start.13
  24.2 0.9 copy-done.13
  25.1 0.2 shard_map.85
  25.3 0.0 copy-start
  25.3 1.4 %copy-done = bf16[8,2,192,384]{3,2,1,0:T(8,128)(2,1)} copy-done((bf16[8,2,192,384]{3,2,1,0:T(8,128)(2,1)}, bf16[8,2,192,384]{3,2,1,0:T(8,128)(2,1)S(1)}, u32[]{:S(2)}) %copy-start) | copy-done | bytes 2359320
  26.8 3.9 %all-to-all-start.1 = ((bf16[8,2,192,384]{3,2,1,0:T(8,128)(2,1)}), bf16[8,2,192,384]{3,2,1,0:T(8,128)(2,1)S(1)}, u32[]{:S(2)}, u32[]{:S(2)}) async-start(bf16[8,2,192,384]{3,2,1,0:T(8,128)(2,1)} %copy-done), calls=%async_computation.1 | async-start | bytes 4718592 | tf_op jit(solution)/shard_map/all_to_all | solution.py:278
  30.7 0.1 fusion
  30.8 2.6 %collective-permute-start.4 = (bf16[4,192,384]{2,1,0:T(8,128)(2,1)S(1)}, bf16[4,192,384]{2,1,0:T(8,128)(2,1)S(1)}, u32[]{:S(2)}, u32[]{:S(2)}) collective-permute-start(bf16[4,192,384]{2,1,0:T(8,128)(2,1)S(1)} %get-tuple-element.28), channel_id=1, source_target_pairs={{0,8},{1,9},{2,10},{3,11},{4,12},{5,13},{6,14},{7,15},{8,16},{9,17... | collective-permute-start | bytes 1769480 | tf_op jit(solution)/shard_map/ppermute | solution.py:271
  33.4 1.3 %collective-permute-start.5 = (bf16[4,192,384]{2,1,0:T(8,128)(2,1)S(1)}, bf16[4,192,384]{2,1,0:T(8,128)(2,1)S(1)}, u32[]{:S(2)}, u32[]{:S(2)}) collective-permute-start(bf16[4,192,384]{2,1,0:T(8,128)(2,1)S(1)} %get-tuple-element.27), channel_id=1, source_target_pairs={{0,24},{1,25},{2,26},{3,27},{4,28},{5,29},{6,30},{7,31},{8,0},{9,1... | collective-permute-start | bytes 1769480 | tf_op jit(solution)/shard_map/ppermute | solution.py:271
  34.7 0.0 copy-done.24
  34.7 2.0 %collective-permute-start.3 = (bf16[2,144,384]{2,1,0:T(8,128)(2,1)S(1)}, bf16[2,144,384]{2,1,0:T(8,128)(2,1)S(1)}, u32[]{:S(2)}, u32[]{:S(2)}) collective-permute-start(bf16[2,144,384]{2,1,0:T(8,128)(2,1)S(1)} %copy-done.24), channel_id=1, source_target_pairs={{0,4},{1,5},{2,6},{3,7},{4,0},{5,1},{6,2},{7,3},{8,12},{9,13},{10,... | collective-permute-start | bytes 663560 | tf_op jit(solution)/shard_map/ppermute | solution.py:275
  36.7 27.2 %collective-permute-done.3.got_ref = bf16[2,144,384]{2,1,0:T(8,128)(2,1)S(1)} collective-permute-done((bf16[2,144,384]{2,1,0:T(8,128)(2,1)S(1)}, bf16[2,144,384]{2,1,0:T(8,128)(2,1)S(1)}, u32[]{:S(2)}, u32[]{:S(2)}) %collective-permute-start.3) | collective-permute-done | bytes 221216 | tf_op jit(solution)/shard_map/ppermute | solution.py:275
  63.9 0.6 shard_map.86
  64.5 0.0 copy-start.15
  64.5 0.6 copy-done.15
  65.2 0.6 copy-done.20
  65.8 0.0 collective-permute-done.4.__.before_ref
  65.8 0.0 copy-done.10
  65.8 0.8 copy-done.1
  66.6 0.0 collective-permute-done.5.___.after_ref
  66.6 0.8 copy-done.4
  67.4 0.0 all-to-all-done.1.vq_ref.q_ref.v_ref
  67.4 1.1 copy-done.2
  68.5 1.1 copy-done.5
  69.5 0.9 copy-done.16
  70.5 0.0 copy-start.17
  70.5 0.0 copy-start.21
  70.5 0.1 shard_map.87
  70.6 2.6 %collective-permute-start.6 = (bf16[4,192,384]{2,1,0:T(8,128)(2,1)S(1)}, bf16[4,192,384]{2,1,0:T(8,128)(2,1)S(1)}, u32[]{:S(2)}, u32[]{:S(2)}) collective-permute-start(bf16[4,192,384]{2,1,0:T(8,128)(2,1)S(1)} %get-tuple-element.21), channel_id=1, source_target_pairs={{0,8},{1,9},{2,10},{3,11},{4,12},{5,13},{6,14},{7,15},{8,16},{9,17... | collective-permute-start | bytes 1769480 | tf_op jit(solution)/shard_map/ppermute | solution.py:271
  73.2 1.3 %collective-permute-start.7 = (bf16[4,192,384]{2,1,0:T(8,128)(2,1)S(1)}, bf16[4,192,384]{2,1,0:T(8,128)(2,1)S(1)}, u32[]{:S(2)}, u32[]{:S(2)}) collective-permute-start(bf16[4,192,384]{2,1,0:T(8,128)(2,1)S(1)} %get-tuple-element.22), channel_id=1, source_target_pairs={{0,24},{1,25},{2,26},{3,27},{4,28},{5,29},{6,30},{7,31},{8,0},{9,1... | collective-permute-start | bytes 1769480 | tf_op jit(solution)/shard_map/ppermute | solution.py:271
  74.5 0.0 copy-done.3
  74.5 0.0 copy-done.6
  74.5 0.0 copy-done.14
  74.5 0.0 copy-done.17
  74.5 0.0 copy-done.21
  74.5 19.8 %shard_map.88 = (f32[3,2,128,768]{3,2,1,0:T(8,128)S(1)}, bf16[3,2,768,768]{3,2,1,0:T(8,128)(2,1)S(1)}, f32[3,2,1,768]{3,2,1,0:T(1,128)S(1)}) custom-call(f32[16,128]{1,0:T(8,128)S(1)} %copy-done.21, bf16[8,2,192,384]{3,2,1,0:T(8,128)(2,1)S(1)} %all-to-all-done.1.vq_ref.q_ref.v_ref, bf16[8,2,192,384]{3,2,1,0:T(8,128)(2,1)S(1)} %all-to-all-done.1.vq_ref.q_ref.v_ref, ...), custom_call_target="tpu_custom_call" | custom-call | tf_op jit(solution)/shard_map/pallas_call | solution.py:122
  94.3 0.0 collective-permute-done.6.before_ref
  94.3 5.7 %collective-permute-done.7.after_ref = bf16[4,192,384]{2,1,0:T(8,128)(2,1)S(1)} collective-permute-done((bf16[4,192,384]{2,1,0:T(8,128)(2,1)S(1)}, bf16[4,192,384]{2,1,0:T(8,128)(2,1)S(1)}, u32[]{:S(2)}, u32[]{:S(2)}) %collective-permute-start.7) | collective-permute-done | bytes 589856 | tf_op jit(solution)/shard_map/ppermute | solution.py:271
  100.0 3.0 %shard_map.89 = bf16[8,192,384]{2,1,0:T(8,128)(2,1)S(1)} custom-call(bf16[4,192,384]{2,1,0:T(8,128)(2,1)S(1)} %collective-permute-done.6.before_ref, bf16[4,192,384]{2,1,0:T(8,128)(2,1)S(1)} %collective-permute-done.7.after_ref, f32[3,2,128,768]{3,2,1,0:T(8,128)S(1)} %get-tuple-element.24.near_ref, bf16[3,2,768,768]{3,2,1,0:T(8,128)(2,1)S(1)} %get-tuple-element.25.far_ref, ...), custom_call_target="tpu_custom_call" | custom-call | tf_op jit(solution)/shard_map/pallas_call | solution.py:155
  103.1 19.1 %all_to_all.15.x_ref = bf16[8,192,384]{2,1,0:T(8,128)(2,1)S(1)} all-to-all(bf16[8,192,384]{2,1,0:T(8,128)(2,1)S(1)} %shard_map.89), channel_id=1, replica_groups={{0,1,2,3,4,5,6,7},{8,9,10,11,12,13,14,15},{16,17,18,19,20,21,22,23},{24..., dimensions={0} | all-to-all | bytes 2359296 | tf_op jit(solution)/shard_map/all_to_all | solution.py:278
  122.2 1.1 shard_map.90
  (21 shorter events, 0.0 us)
Async XLA Ops:
  0.0 1.3 %copy-start.7 = (bf16[192,3072]{1,0:T(8,128)(2,1)S(1)}, bf16[192,3072]{1,0:T(8,128)(2,1)}, u32[]{:S(2)}) copy-start(bf16[192,3072]{1,0:T(8,128)(2,1)} %refs_0_.2) | copy-start | bytes 3538948
  2.4 6.0 %copy-start.25 = (s32[6]{0:T(128)S(1)}, s32[6]{0:T(128)}, u32[]{:S(2)}) copy-start(s32[6]{0:T(128)} %param.14) | copy-start | bytes 76
  2.4 6.2 %copy-start.22 = (s32[6,12]{1,0:T(8,128)S(1)}, s32[6,12]{1,0:T(8,128)}, u32[]{:S(2)}) copy-start(s32[6,12]{1,0:T(8,128)} %list_ref.1) | copy-start | bytes 868
  2.4 21.8 %copy-start.8 = (bf16[192,3072]{1,0:T(8,128)(2,1)S(1)}, bf16[192,3072]{1,0:T(8,128)(2,1)}, u32[]{:S(2)}) copy-start(bf16[192,3072]{1,0:T(8,128)(2,1)} %refs_0_.3) | copy-start | bytes 3538948
  2.4 21.8 %copy-start.9 = (bf16[192,3072]{1,0:T(8,128)(2,1)S(1)}, bf16[192,3072]{1,0:T(8,128)(2,1)}, u32[]{:S(2)}) copy-start(bf16[192,3072]{1,0:T(8,128)(2,1)} %refs_1_.1) | copy-start | bytes 3538948
  2.4 21.8 %all-to-all-start = ((bf16[8,192,384]{2,1,0:T(8,128)(2,1)}), bf16[8,192,384]{2,1,0:T(8,128)(2,1)S(1)}, u32[]{:S(2)}, u32[]{:S(2)}) async-start(bf16[8,192,384]{2,1,0:T(8,128)(2,1)} %shard_map.82), calls=%async_computation | async-start | bytes 2359296 | tf_op jit(solution)/shard_map/all_to_all | solution.py:278
  8.6 0.8 copy-start.18
  9.4 0.8 copy-start.19
  10.8 7.5 %collective-permute-start = (bf16[2,32,768]{2,1,0:T(8,128)(2,1)S(1)}, bf16[2,32,768]{2,1,0:T(8,128)(2,1)S(1)}, u32[]{:S(2)}, u32[]{:S(2)}) collective-permute-start(bf16[2,32,768]{2,1,0:T(8,128)(2,1)S(1)} %get-tuple-element.17.refs_0_), channel_id=1, source_target_pairs={{0,8},{1,9},{2,10},{3,11},{4,12},{5,13},{6,14},{7,15},{8,16},{9,17... | collective-permute-start | bytes 294920 | tf_op jit(solution)/shard_map/ppermute | solution.py:271
  12.4 9.8 %collective-permute-start.1 = (bf16[2,32,768]{2,1,0:T(8,128)(2,1)S(1)}, bf16[2,32,768]{2,1,0:T(8,128)(2,1)S(1)}, u32[]{:S(2)}, u32[]{:S(2)}) collective-permute-start(bf16[2,32,768]{2,1,0:T(8,128)(2,1)S(1)} %get-tuple-element.17.refs_0_), channel_id=1, source_target_pairs={{0,16},{1,17},{2,18},{3,19},{4,20},{5,21},{6,22},{7,23},{8,24},{9,... | collective-permute-start | bytes 294920 | tf_op jit(solution)/shard_map/ppermute | solution.py:271
  15.0 7.2 %collective-permute-start.2 = (bf16[2,32,768]{2,1,0:T(8,128)(2,1)S(1)}, bf16[2,32,768]{2,1,0:T(8,128)(2,1)S(1)}, u32[]{:S(2)}, u32[]{:S(2)}) collective-permute-start(bf16[2,32,768]{2,1,0:T(8,128)(2,1)S(1)} %get-tuple-element.17.refs_0_), channel_id=1, source_target_pairs={{0,24},{1,25},{2,26},{3,27},{4,28},{5,29},{6,30},{7,31},{8,0},{9,1... | collective-permute-start | bytes 294920 | tf_op jit(solution)/shard_map/ppermute | solution.py:271
  22.8 0.7 copy-start.12
  23.5 0.7 copy-start.23
  24.2 0.9 copy-start.13
  25.3 1.4 %copy-start = (bf16[8,2,192,384]{3,2,1,0:T(8,128)(2,1)}, bf16[8,2,192,384]{3,2,1,0:T(8,128)(2,1)S(1)}, u32[]{:S(2)}) copy-start(bf16[8,2,192,384]{3,2,1,0:T(8,128)(2,1)S(1)} %shard_map.85) | copy-start | bytes 7077892
  26.8 40.7 %all-to-all-start.1 = ((bf16[8,2,192,384]{3,2,1,0:T(8,128)(2,1)}), bf16[8,2,192,384]{3,2,1,0:T(8,128)(2,1)S(1)}, u32[]{:S(2)}, u32[]{:S(2)}) async-start(bf16[8,2,192,384]{3,2,1,0:T(8,128)(2,1)} %copy-done), calls=%async_computation.1 | async-start | bytes 4718592 | tf_op jit(solution)/shard_map/all_to_all | solution.py:278
  30.7 4.0 %copy-start.24 = (bf16[2,144,384]{2,1,0:T(8,128)(2,1)S(1)}, bf16[2,144,384]{2,1,0:T(8,128)(2,1)}, u32[]{:S(2)}) copy-start(bf16[2,144,384]{2,1,0:T(8,128)(2,1)} %copy-done.23) | copy-start | bytes 663556
  30.8 35.0 %collective-permute-start.4 = (bf16[4,192,384]{2,1,0:T(8,128)(2,1)S(1)}, bf16[4,192,384]{2,1,0:T(8,128)(2,1)S(1)}, u32[]{:S(2)}, u32[]{:S(2)}) collective-permute-start(bf16[4,192,384]{2,1,0:T(8,128)(2,1)S(1)} %get-tuple-element.28), channel_id=1, source_target_pairs={{0,8},{1,9},{2,10},{3,11},{4,12},{5,13},{6,14},{7,15},{8,16},{9,17... | collective-permute-start | bytes 1769480 | tf_op jit(solution)/shard_map/ppermute | solution.py:271
  33.4 33.2 %collective-permute-start.5 = (bf16[4,192,384]{2,1,0:T(8,128)(2,1)S(1)}, bf16[4,192,384]{2,1,0:T(8,128)(2,1)S(1)}, u32[]{:S(2)}, u32[]{:S(2)}) collective-permute-start(bf16[4,192,384]{2,1,0:T(8,128)(2,1)S(1)} %get-tuple-element.27), channel_id=1, source_target_pairs={{0,24},{1,25},{2,26},{3,27},{4,28},{5,29},{6,30},{7,31},{8,0},{9,1... | collective-permute-start | bytes 1769480 | tf_op jit(solution)/shard_map/ppermute | solution.py:271
  34.7 29.2 %collective-permute-start.3 = (bf16[2,144,384]{2,1,0:T(8,128)(2,1)S(1)}, bf16[2,144,384]{2,1,0:T(8,128)(2,1)S(1)}, u32[]{:S(2)}, u32[]{:S(2)}) collective-permute-start(bf16[2,144,384]{2,1,0:T(8,128)(2,1)S(1)} %copy-done.24), channel_id=1, source_target_pairs={{0,4},{1,5},{2,6},{3,7},{4,0},{5,1},{6,2},{7,3},{8,12},{9,13},{10,... | collective-permute-start | bytes 663560 | tf_op jit(solution)/shard_map/ppermute | solution.py:275
  63.9 1.9 %copy-start.10 = (bf16[2,144,384]{2,1,0:T(8,128)(2,1)}, bf16[2,144,384]{2,1,0:T(8,128)(2,1)S(1)}, u32[]{:S(2)}) copy-start(bf16[2,144,384]{2,1,0:T(8,128)(2,1)S(1)} %collective-permute-done.3.got_ref) | copy-start | bytes 663556
  64.5 0.6 copy-start.15
  65.2 0.6 copy-start.20
  65.8 0.8 copy-start.1
  66.6 0.8 copy-start.4
  67.4 1.1 copy-start.2
  68.5 1.1 copy-start.5
  69.5 0.9 copy-start.16
  70.4 4.0 %copy-start.3 = (bf16[4,192,384]{2,1,0:T(8,128)(2,1)S(1)}, bf16[4,192,384]{2,1,0:T(8,128)(2,1)}, u32[]{:S(2)}) copy-start(bf16[4,192,384]{2,1,0:T(8,128)(2,1)} %copy-done.1) | copy-start | bytes 1769476
  70.4 4.0 %copy-start.6 = (bf16[4,192,384]{2,1,0:T(8,128)(2,1)S(1)}, bf16[4,192,384]{2,1,0:T(8,128)(2,1)}, u32[]{:S(2)}) copy-start(bf16[4,192,384]{2,1,0:T(8,128)(2,1)} %copy-done.4) | copy-start | bytes 1769476
  70.5 4.0 %copy-start.11 = (bf16[2,144,384]{2,1,0:T(8,128)(2,1)S(1)}, bf16[2,144,384]{2,1,0:T(8,128)(2,1)}, u32[]{:S(2)}) copy-start(bf16[2,144,384]{2,1,0:T(8,128)(2,1)} %copy-done.10) | copy-start | bytes 663556
  70.5 4.0 %copy-start.14 = (bf16[2,128,384]{2,1,0:T(8,128)(2,1)S(1)}, bf16[2,128,384]{2,1,0:T(8,128)(2,1)}, u32[]{:S(2)}) copy-start(bf16[2,128,384]{2,1,0:T(8,128)(2,1)} %copy-done.12) | copy-start | bytes 589828
  70.5 4.0 %copy-start.17 = (f32[256,128]{1,0:T(8,128)S(1)}, f32[256,128]{1,0:T(8,128)}, u32[]{:S(2)}) copy-start(f32[256,128]{1,0:T(8,128)} %copy-done.15) | copy-start | bytes 393220
  70.5 4.0 %copy-start.21 = (f32[16,128]{1,0:T(8,128)S(1)}, f32[16,128]{1,0:T(8,128)}, u32[]{:S(2)}) copy-start(f32[16,128]{1,0:T(8,128)} %copy-done.20) | copy-start | bytes 24580
  70.6 23.7 %collective-permute-start.6 = (bf16[4,192,384]{2,1,0:T(8,128)(2,1)S(1)}, bf16[4,192,384]{2,1,0:T(8,128)(2,1)S(1)}, u32[]{:S(2)}, u32[]{:S(2)}) collective-permute-start(bf16[4,192,384]{2,1,0:T(8,128)(2,1)S(1)} %get-tuple-element.21), channel_id=1, source_target_pairs={{0,8},{1,9},{2,10},{3,11},{4,12},{5,13},{6,14},{7,15},{8,16},{9,17... | collective-permute-start | bytes 1769480 | tf_op jit(solution)/shard_map/ppermute | solution.py:271
  73.2 26.8 %collective-permute-start.7 = (bf16[4,192,384]{2,1,0:T(8,128)(2,1)S(1)}, bf16[4,192,384]{2,1,0:T(8,128)(2,1)S(1)}, u32[]{:S(2)}, u32[]{:S(2)}) collective-permute-start(bf16[4,192,384]{2,1,0:T(8,128)(2,1)S(1)} %get-tuple-element.22), channel_id=1, source_target_pairs={{0,24},{1,25},{2,26},{3,27},{4,28},{5,29},{6,30},{7,31},{8,0},{9,1... | collective-permute-start | bytes 1769480 | tf_op jit(solution)/shard_map/ppermute | solution.py:271

commit v3 on v2

--- a/solution.py
+++ b/solution.py
@@ -18,6 +18,10 @@
 ANY = pl.BlockSpec(memory_space=pl.ANY)
 SMALL = pltpu.CompilerParams(vmem_limit_bytes=12 << 20)
 LARGE = pltpu.CompilerParams(vmem_limit_bytes=24 << 20)
+
+
+def far_memory(x):
+    return pltpu.with_memory_space_constraint(x, pltpu.HBM)
 
 
 def weigh(queries, keys, biases):
@@ -63,27 +67,27 @@
     k_ref,
     before_ref,
     after_ref,
-    keep_ref,
-    got_ref,
     text_ref,
+    text_bias_ref,
     near_ref,
     far_ref,
     scale_ref,
 ):
     side = pl.program_id(1)
-    half, rows = k_ref.shape[0] // 2, keep_ref.shape[1]
+    half = k_ref.shape[0] // 2
     own, other = pl.ds(side * half, half), pl.ds((1 - side) * half, half)
     queries = flat(q_ref[:, 0])
     at = lambda t, u: bias[side * 8 + t, u]
     span = range(tiles)
     own_bias = [[at(t, u) for t in span] for u in span]
     own_bias += [
-        [text_ref[j * TILE : (j + 1) * TILE, :]] * tiles for j in range(text_ref.shape[0] // TILE)
+        [text_bias_ref[j * TILE : (j + 1) * TILE, :]] * tiles
+        for j in range(text_bias_ref.shape[0] // TILE)
     ]
     mine = group(
         queries,
-        jnp.concatenate([flat(k_ref[own]), keep_ref[0], got_ref[0, :rows]], axis=0),
-        jnp.concatenate([flat(v_ref[own, 0]), keep_ref[1], got_ref[1, :rows]], axis=0).T,
+        jnp.concatenate([flat(k_ref[own]), text_ref[0]], axis=0),
+        jnp.concatenate([flat(v_ref[own, 0]), text_ref[1]], axis=0).T,
         own_bias,
     )
     near = group(
@@ -114,7 +118,7 @@
     out_ref[...] = out.T.astype(out_ref.dtype).reshape(out_ref.shape)
 
 
-def near_attention(tiles, bias, vq, k, k_before, k_after, keep, got, text_bias):
+def near_attention(tiles, bias, vq, k, k_before, k_after, text, text_bias):
     ways, _, rows, part = vq.shape
     heads, half, length = part // HD, ways // 2, tiles * TILE
     far = pl.BlockSpec((half, rows, HD), lambda h, s: (0, 0, h))
@@ -129,8 +133,7 @@
             pl.BlockSpec((ways, rows, HD), lambda h, s: (0, 0, h)),
             far,
             far,
-            pl.BlockSpec((2, keep.shape[1], HD), lambda h, s: (0, 0, h)),
-            pl.BlockSpec((2, got.shape[1], HD), lambda h, s: (0, 0, h)),
+            pl.BlockSpec((2, text.shape[1], HD), lambda h, s: (0, 0, h)),
             pl.BlockSpec(text_bias.shape, lambda h, s: (0, 0)),
         ],
         out_specs=[
@@ -144,7 +147,7 @@
             jax.ShapeDtypeStruct((heads, 2, 1, length), jnp.float32),
         ],
         compiler_params=LARGE,
-    )(bias, vq, vq, k, k_before, k_after, keep, got, text_bias)
+    )(bias, vq, vq, k, k_before, k_after, text, text_bias)
 
 
 def far_attention(v_before, v_after, near, weights, scales):
@@ -169,14 +172,30 @@
 
 
 def split_kernel(order, count, *refs):
-    out_ref = refs[-1]
+    arrays, (out_ref, held, came, left) = refs[:count], refs[count:]
     part = out_ref.shape[-1]
-    for i, x_ref in enumerate(refs[:count]):
-        for p, g in enumerate(order):
-            if count == 1:
-                out_ref[p] = x_ref[:, g * part : (g + 1) * part]
-            else:
-                out_ref[p, i] = x_ref[:, g * part : (g + 1) * part]
+    slot = lambda ref, p, i: ref.at[p] if count == 1 else ref.at[p, i]
+    reads = [
+        [
+            pltpu.make_async_copy(
+                x_ref.at[:, g * part : (g + 1) * part], slot(held, p, i), came.at[p, i]
+            )
+            for i, x_ref in enumerate(arrays)
+        ]
+        for p, g in enumerate(order)
+    ]
+    writes = [
+        pltpu.make_async_copy(held.at[p], out_ref.at[p], left.at[p]) for p in range(len(order))
+    ]
+    for row in reads:
+        for copy in row:
+            copy.start()
+    for row, write in zip(reads, writes):
+        for copy in row:
+            copy.wait()
+        write.start()
+    for write in writes:
+        write.wait()
 
 
 def join_kernel(order, x_ref, out_ref):
@@ -185,16 +204,22 @@
         out_ref[:, g * part : (g + 1) * part] = x_ref[p]
 
 
-def split_heads(order, arrays, first=()):
+def split_heads(order, arrays):
     rows, width = arrays[0].shape
     ways, count = len(order), len(arrays)
     shape = (ways, count, rows, width // ways) if count > 1 else (ways, rows, width // ways)
     return pl.pallas_call(
         functools.partial(split_kernel, order, count),
-        in_specs=[pl.BlockSpec()] * count + [ANY] * len(first),
-        out_shape=jax.ShapeDtypeStruct(shape, jnp.bfloat16),
-        compiler_params=SMALL,
-    )(*arrays, *first)
+        in_specs=[ANY] * count,
+        out_specs=ANY,
+        out_shape=pltpu.HBM(shape, jnp.bfloat16),
+        scratch_shapes=[
+            pltpu.VMEM(shape, jnp.bfloat16),
+            pltpu.SemaphoreType.DMA((ways, count)),
+            pltpu.SemaphoreType.DMA((ways,)),
+        ],
+        compiler_params=SMALL,
+    )(*(far_memory(x) for x in arrays))
 
 
 def join_heads(x, order):
@@ -206,22 +231,31 @@
     )(x)
 
 
-def mask_kernel(tiles, place, list_ref, count_ref, k_ref, v_ref, mask_ref, text_ref):
-    text_ref[0] = k_ref[...]
-    text_ref[1] = v_ref[...]
+def mask_kernel(tiles, place, count, list_hbm, k_ref, v_ref, mask_ref, text_ref, list_ref, sems):
+    pairs = ((list_hbm, list_ref), (k_ref, text_ref.at[0]), (v_ref, text_ref.at[1]))
+    copies = [pltpu.make_async_copy(a, b, sems.at[i]) for i, (a, b) in enumerate(pairs)]
+    for copy in copies:
+        copy.start()
+    for copy in copies:
+        copy.wait()
+    row = lax.broadcasted_iota(jnp.int32, (tiles, TILE), 0)
+    counts = jnp.zeros((tiles, TILE), jnp.int32)
+    for t in range(tiles):
+        counts = jnp.where(row == t, count[t], counts)
     lane = lax.broadcasted_iota(jnp.int32, (tiles, TILE), 1)
     ids = jnp.where(lane < tiles, place[0] * tiles + lane, place[1] * tiles + lane - tiles)
     ids = jnp.where(lane < 2 * tiles, ids, place[2] * tiles + lane - 2 * tiles)
     mask = jnp.zeros((tiles, TILE), jnp.float32)
     for i in range(list_ref.shape[1]):
-        hit = (list_ref[:, i : i + 1] == ids) & (count_ref[...] > i)
+        hit = (list_ref[:, i : i + 1] == ids) & (counts > i)
         mask = jnp.where(hit, 1.0, mask)
     spare = jnp.zeros((mask_ref.shape[0] - tiles, TILE), jnp.float32)
     mask_ref[...] = jnp.concatenate([mask, spare], axis=0).astype(jnp.bfloat16)
 
 
 def turn_kernel(pieces, place, mask_ref, *refs):
-    texts, (offer_ref, keep_ref) = refs[:pieces], refs[-2:]
+    texts, (offer_ref, keep_ref, done_ref) = refs[:pieces], refs[-3:]
+    done_ref[...] = jnp.zeros_like(done_ref)
     low = place[3] == 0
     part = offer_ref.shape[2]
     for i in range(2):
@@ -232,14 +266,33 @@
     offer_ref[0, keep_ref.shape[1] :, 0:TILE] = mask_ref[...]
 
 
-def halves_kernel(vq_ref, _, __, ___, low_ref, high_ref):
+def halves_kernel(vq_ref, _, __, low_ref, high_ref):
     half = low_ref.shape[0]
     low_ref[...] = vq_ref[:half, 0]
     high_ref[...] = vq_ref[half:, 0]
 
 
-def bias_kernel(pairs, rows, place, mask_ref, got_ref, bias_ref, text_ref):
+def gate_kernel(*_):
+    pass
+
+
+def gated(x, *first):
+    return pl.pallas_call(
+        gate_kernel,
+        in_specs=[ANY] * (1 + len(first)),
+        out_specs=ANY,
+        out_shape=pltpu.HBM(x.shape, x.dtype),
+        input_output_aliases={0: 0},
+        compiler_params=SMALL,
+    )(far_memory(x), *first)
+
+
+def bias_kernel(
+    pairs, rows, place, mask_ref, keep_ref, got_ref, bias_ref, text_ref, all_ref
+):
     low = place[3] == 0
+    for i in range(2):
+        all_ref[i] = jnp.concatenate([keep_ref[i], got_ref[i, : keep_ref.shape[1]]], axis=0)
     start = got_ref.shape[1] - mask_ref.shape[0]
     mine, theirs = mask_ref[...], got_ref[0, start:, 0:TILE]
     for i, block in enumerate((jnp.where(low, mine, theirs), jnp.where(low, theirs, mine))):
@@ -286,13 +339,14 @@
     text_rows = text_keys.shape[0]
     mask, text = pl.pallas_call(
         functools.partial(mask_kernel, tiles),
-        in_specs=[SMEM] + [pl.BlockSpec()] * 4,
+        in_specs=[SMEM, SMEM] + [ANY] * 3,
         out_shape=[
             jax.ShapeDtypeStruct((16, TILE), jnp.bfloat16),
             jax.ShapeDtypeStruct((2, *text_keys.shape), jnp.bfloat16),
         ],
-        compiler_params=SMALL,
-    )(place, lists, counts[:, None], text_keys, text_values)
+        scratch_shapes=[pltpu.VMEM(lists.shape, jnp.int32), pltpu.SemaphoreType.DMA((3,))],
+        compiler_params=SMALL,
+    )(place, counts, far_memory(lists), far_memory(text_keys), far_memory(text_values))
     if pairs <= 4:
         texts = [text] + [shifted(text, by) for by in range(1, pairs)]
     else:
@@ -303,39 +357,42 @@
             text, have = jnp.concatenate([text, more], axis=1), have + take
         texts = [text]
     all_text = pairs * text_rows
-    offer, keep = pl.pallas_call(
+    offer, keep, turned = pl.pallas_call(
         functools.partial(turn_kernel, len(texts)),
         in_specs=[SMEM] + [pl.BlockSpec()] * (1 + len(texts)),
         out_shape=[
-            jax.ShapeDtypeStruct((2, all_text + mask.shape[0], part), jnp.bfloat16),
-            jax.ShapeDtypeStruct((2, all_text, part), jnp.bfloat16),
+            pltpu.HBM((2, all_text + mask.shape[0], part), jnp.bfloat16),
+            pltpu.HBM((2, all_text, part), jnp.bfloat16),
+            pltpu.HBM((8, TILE), jnp.float32),
         ],
         compiler_params=SMALL,
     )(place, mask, *texts)
     got = swapped(offer)
 
-    bias, text_bias = pl.pallas_call(
+    bias, text_bias, text = pl.pallas_call(
         functools.partial(bias_kernel, pairs, text_rows),
-        in_specs=[SMEM] + [pl.BlockSpec()] * 2,
+        in_specs=[SMEM] + [pl.BlockSpec()] * 3,
         out_shape=[
-            jax.ShapeDtypeStruct((16, TILE), jnp.float32),
-            jax.ShapeDtypeStruct((2 * all_text, TILE), jnp.float32),
-        ],
-        compiler_params=SMALL,
-    )(place, mask, got)
-
-    k_before, k_after = shifted(k[heads:], 1), shifted(k[:heads], -1)
-    vq = exchange(split_heads(order, (values, queries), (k, keep)))
+            pltpu.HBM((16, TILE), jnp.float32),
+            pltpu.HBM((2 * all_text, TILE), jnp.float32),
+            pltpu.HBM((2, 2 * all_text, part), jnp.bfloat16),
+        ],
+        compiler_params=SMALL,
+    )(place, mask, keep, got)
+
+    k_before, k_after = far_memory(shifted(k[heads:], 1)), far_memory(shifted(k[:heads], -1))
+    vq = exchange(gated(split_heads(order, (values, queries)), k, turned))
 
     half = jax.ShapeDtypeStruct((heads, rows, part), jnp.bfloat16)
     v_low, v_high = pl.pallas_call(
         halves_kernel,
-        in_specs=[pl.BlockSpec(), ANY, ANY, ANY],
+        in_specs=[pl.BlockSpec()] + [ANY] * 2,
         out_shape=[half, half],
         compiler_params=SMALL,
-    )(vq, text_bias, k_before, k_after)
+    )(vq, k_before, k_after)
     v_before, v_after = shifted(v_high, 1), shifted(v_low, -1)
-    partial = near_attention(tiles, bias, vq, k, k_before, k_after, keep, got, text_bias)
+    text, text_bias = far_memory(text), far_memory(text_bias)
+    partial = near_attention(tiles, bias, vq, far_memory(k), k_before, k_after, text, text_bias)
     out = far_attention(v_before, v_after, *partial)
     return join_heads(exchange(out), order)
 

time: 124 us -> 116 us (0.935)
  local copies, waits for them, and re-layouts: 12.8 us -> 1.6 us
  Pallas kernels: 27.2 us -> 33.3 us
  waiting for transfers between devices: 38.7 us -> 35.4 us
    ppermute x1, waiting for transfers between devices: 27.2 us -> 5.08 us  [swapped(): return lax.ppermute(x, AXES, [(i, flip(i)) for i in range(count)])]
    ppermute x7, waiting for transfers between devices: 11.5 us -> 29.4 us  [shifted(): lax.ppermute(x, AXES, [(i, (i + by * ways) % count) for i in range(count)])]
    unnamed x52 -> x14, local copies, waits for them, and re-layouts: 12.5 us -> 1.4 us
    pallas_call x4 -> x5, Pallas kernels: 2.06 us -> 6.47 us  [the longest x2 4.87 us: split_heads(): pl.pallas_call(functools.partial(split_kernel, order, count), in_specs=[A...]
  transfers between devices with their start and end apart: 10 -> 10, of which waited for: 4 -> 5; matrix products, arithmetic and copies ran while one was open for 0% -> 0% of each run, Pallas kernels for 18% -> 23%
where the time goes in v3:
time: 116 us; the launch traced here: 115 us
  waiting for transfers between devices  35.4 us (31%)
  Pallas kernels  33.3 us (29%)
  starting transfers between devices  23.8 us (21%)
  blocking collectives  20.2 us (17%)
  local copies, waits for them, and re-layouts  1.6 us (1%)
    ppermute x7, waiting for transfers between devices, shifted(): lax.ppermute(x, AXES, [(i, (i + by * ways) % count) for i in range(count)])  29.4 us
    all_to_all x1, blocking collectives, exchange(): lax.all_to_all(x, AXES, split_axis=0, concat_axis=0, tiled=True, axis_ind...  20.2 us
    pallas_call x1, Pallas kernels, near_attention(): pl.pallas_call(functools.partial(near_kernel, tiles), grid=(heads, 2), in...  19.8 us
    ppermute x7, starting transfers between devices, shifted(): lax.ppermute(x, AXES, [(i, (i + by * ways) % count) for i in range(count)])  13.3 us
    all_to_all x2, starting transfers between devices, exchange(): lax.all_to_all(x, AXES, split_axis=0, concat_axis=0, tiled=True, axis_ind...  8.8 us
    ppermute x1, waiting for transfers between devices, swapped(): return lax.ppermute(x, AXES, [(i, flip(i)) for i in range(count)])  5.08 us
    pallas_call x2, Pallas kernels, split_heads(): pl.pallas_call(functools.partial(split_kernel, order, count), in_specs=[A...  4.87 us
    pallas_call x1, Pallas kernels, far_attention(): pl.pallas_call(far_kernel, grid=(heads, 2), in_specs=[far, far, pl.BlockS...  3.07 us
  transfers between devices with their start and end apart: 10, of which 5 were waited for; matrix products, arithmetic and copies ran while one was open for 0% of the time, Pallas kernels for 23%

profile of v3, /device:TPU:0, one launch (start us, length us, event | category | flops | bytes accessed | tf_op | source)
XLA Modules:
  0.0 115.1 jit_solution(12908092435801400100)
XLA Ops:
  0.0 2.2 %shard_map.83 = bf16[8,192,384]{2,1,0:T(8,128)(2,1)} custom-call(bf16[192,3072]{1,0:T(8,128)(2,1)} %refs_0_.3), custom_call_target="tpu_custom_call" | custom-call | tf_op jit(solution)/shard_map/pallas_call | solution.py:211
  2.2 0.0 copy-start.4
  2.2 5.2 %all-to-all-start = ((bf16[8,192,384]{2,1,0:T(8,128)(2,1)}), bf16[8,192,384]{2,1,0:T(8,128)(2,1)S(1)}, u32[]{:S(2)}, u32[]{:S(2)}) async-start(bf16[8,192,384]{2,1,0:T(8,128)(2,1)} %shard_map.83), calls=%async_computation | async-start | bytes 2359296 | tf_op jit(solution)/shard_map/all_to_all | solution.py:331
  8.0 0.1 stack.23.place
  8.1 0.0 copy-done.4
  8.1 1.5 %shard_map.84 = (bf16[16,128]{1,0:T(8,128)(2,1)S(1)}, bf16[2,32,768]{2,1,0:T(8,128)(2,1)S(1)}) custom-call(s32[6]{0:T(128)S(1)} %stack.23.place, s32[6]{0:T(128)S(1)} %copy-done.4, s32[6,12]{1,0:T(8,128)} %list_hbm.1, bf16[32,768]{1,0:T(8,128)(2,1)} %k_ref.1, bf16[32,768]{1,0:T(8,128)(2,1)} %v_ref.1), custom_call_target="tpu_custom_call" | custom-call | tf_op jit(solution)/shard_map/pallas_call | solution.py:340
  9.6 1.6 %collective-permute-start = (bf16[2,32,768]{2,1,0:T(8,128)(2,1)S(1)}, bf16[2,32,768]{2,1,0:T(8,128)(2,1)S(1)}, u32[]{:S(2)}, u32[]{:S(2)}) collective-permute-start(bf16[2,32,768]{2,1,0:T(8,128)(2,1)S(1)} %get-tuple-element.19.refs_0_), channel_id=1, source_target_pairs={{0,8},{1,9},{2,10},{3,11},{4,12},{5,13},{6,14},{7,15},{8,16},{9,17... | collective-permute-start | bytes 294920 | tf_op jit(solution)/shard_map/ppermute | solution.py:324
  11.2 2.6 %collective-permute-start.1 = (bf16[2,32,768]{2,1,0:T(8,128)(2,1)S(1)}, bf16[2,32,768]{2,1,0:T(8,128)(2,1)S(1)}, u32[]{:S(2)}, u32[]{:S(2)}) collective-permute-start(bf16[2,32,768]{2,1,0:T(8,128)(2,1)S(1)} %get-tuple-element.19.refs_0_), channel_id=1, source_target_pairs={{0,16},{1,17},{2,18},{3,19},{4,20},{5,21},{6,22},{7,23},{8,24},{9,... | collective-permute-start | bytes 294920 | tf_op jit(solution)/shard_map/ppermute | solution.py:324
  13.8 1.3 %collective-permute-start.2 = (bf16[2,32,768]{2,1,0:T(8,128)(2,1)S(1)}, bf16[2,32,768]{2,1,0:T(8,128)(2,1)S(1)}, u32[]{:S(2)}, u32[]{:S(2)}) collective-permute-start(bf16[2,32,768]{2,1,0:T(8,128)(2,1)S(1)} %get-tuple-element.19.refs_0_), channel_id=1, source_target_pairs={{0,24},{1,25},{2,26},{3,27},{4,28},{5,29},{6,30},{7,31},{8,0},{9,1... | collective-permute-start | bytes 294920 | tf_op jit(solution)/shard_map/ppermute | solution.py:324
  15.2 2.7 %shard_map.82.__0_ = bf16[8,2,192,384]{3,2,1,0:T(8,128)(2,1)} custom-call(bf16[192,3072]{1,0:T(8,128)(2,1)} %refs_0_.2, bf16[192,3072]{1,0:T(8,128)(2,1)} %refs_1_.1), custom_call_target="tpu_custom_call" | custom-call | tf_op jit(solution)/shard_map/pallas_call | solution.py:211
  17.9 0.0 collective-permute-done.refs_1_
  17.9 3.1 %collective-permute-done.1.refs_2_ = bf16[2,32,768]{2,1,0:T(8,128)(2,1)S(1)} collective-permute-done((bf16[2,32,768]{2,1,0:T(8,128)(2,1)S(1)}, bf16[2,32,768]{2,1,0:T(8,128)(2,1)S(1)}, u32[]{:S(2)}, u32[]{:S(2)}) %collective-permute-start.1) | collective-permute-done | bytes 98336 | tf_op jit(solution)/shard_map/ppermute | solution.py:324
  21.0 0.0 collective-permute-done.2.refs_3_
  21.0 1.3 %shard_map.85 = (bf16[2,144,384]{2,1,0:T(8,128)(2,1)}, bf16[2,128,384]{2,1,0:T(8,128)(2,1)}, f32[8,128]{1,0:T(8,128)}) custom-call(s32[6]{0:T(128)S(1)} %stack.23.place, bf16[16,128]{1,0:T(8,128)(2,1)S(1)} %get-tuple-element.18.mask_ref, bf16[2,32,768]{2,1,0:T(8,128)(2,1)S(1)} %get-tuple-element.19.refs_0_, ...), custom_call_target="tpu_custom_call" | custom-call | tf_op jit(solution)/shard_map/pallas_call | solution.py:360
  22.4 0.9 all-to-all-done.__1_.k_ref
  23.2 0.0 copy-start
  23.2 0.0 copy-start.3
  23.2 0.7 copy-done.3
  23.9 3.6 %all-to-all-start.1 = ((bf16[8,2,192,384]{3,2,1,0:T(8,128)(2,1)}), bf16[8,2,192,384]{3,2,1,0:T(8,128)(2,1)S(1)}, u32[]{:S(2)}, u32[]{:S(2)}) async-start(bf16[8,2,192,384]{3,2,1,0:T(8,128)(2,1)} %shard_map.86), calls=%async_computation.1 | async-start | bytes 4718592 | tf_op jit(solution)/shard_map/all_to_all | solution.py:331
  27.5 0.0 copy-done
  27.5 0.1 fusion
  27.7 2.0 %collective-permute-start.3 = (bf16[4,192,384]{2,1,0:T(8,128)(2,1)S(1)}, bf16[4,192,384]{2,1,0:T(8,128)(2,1)S(1)}, u32[]{:S(2)}, u32[]{:S(2)}) collective-permute-start(bf16[4,192,384]{2,1,0:T(8,128)(2,1)S(1)} %get-tuple-element.32), channel_id=1, source_target_pairs={{0,8},{1,9},{2,10},{3,11},{4,12},{5,13},{6,14},{7,15},{8,16},{9,17... | collective-permute-start | bytes 1769480 | tf_op jit(solution)/shard_map/ppermute | solution.py:324
  29.7 0.0 copy-start.6
  29.7 0.0 copy-start.1
  29.7 1.9 %collective-permute-start.4 = (bf16[4,192,384]{2,1,0:T(8,128)(2,1)S(1)}, bf16[4,192,384]{2,1,0:T(8,128)(2,1)}, u32[]{:S(2)}, u32[]{:S(2)}) collective-permute-start(bf16[4,192,384]{2,1,0:T(8,128)(2,1)S(1)} %get-tuple-element.31), channel_id=1, source_target_pairs={{0,24},{1,25},{2,26},{3,27},{4,28},{5,29},{6,30},{7,31},{8,0},{9,1... | collective-permute-start | bytes 1769480 | tf_op jit(solution)/shard_map/ppermute | solution.py:324
  31.6 14.2 %collective-permute-done.3._.before_ref = bf16[4,192,384]{2,1,0:T(8,128)(2,1)S(1)} collective-permute-done((bf16[4,192,384]{2,1,0:T(8,128)(2,1)S(1)}, bf16[4,192,384]{2,1,0:T(8,128)(2,1)S(1)}, u32[]{:S(2)}, u32[]{:S(2)}) %collective-permute-start.3) | collective-permute-done | bytes 589856 | tf_op jit(solution)/shard_map/ppermute | solution.py:324
  45.7 0.0 copy-start.5
  45.7 12.2 %collective-permute-done.4.__.after_ref = bf16[4,192,384]{2,1,0:T(8,128)(2,1)} collective-permute-done((bf16[4,192,384]{2,1,0:T(8,128)(2,1)S(1)}, bf16[4,192,384]{2,1,0:T(8,128)(2,1)}, u32[]{:S(2)}, u32[]{:S(2)}) %collective-permute-start.4) | collective-permute-done | bytes 589856 | tf_op jit(solution)/shard_map/ppermute | solution.py:324
  57.9 0.0 copy-done.5
  57.9 0.0 all-to-all-done.1.vq_ref.q_ref.v_ref
  57.9 0.1 shard_map.87
  58.0 0.7 collective-permute-start.5
  58.7 3.2 %collective-permute-start.6 = (bf16[4,192,384]{2,1,0:T(8,128)(2,1)S(1)}, bf16[4,192,384]{2,1,0:T(8,128)(2,1)S(1)}, u32[]{:S(2)}, u32[]{:S(2)}) collective-permute-start(bf16[4,192,384]{2,1,0:T(8,128)(2,1)S(1)} %get-tuple-element.22), channel_id=1, source_target_pairs={{0,24},{1,25},{2,26},{3,27},{4,28},{5,29},{6,30},{7,31},{8,0},{9,1... | collective-permute-start | bytes 1769480 | tf_op jit(solution)/shard_map/ppermute | solution.py:324
  61.9 0.0 copy-done.6
  61.9 1.7 %collective-permute-start.7 = (bf16[2,144,384]{2,1,0:T(8,128)(2,1)S(1)}, bf16[2,144,384]{2,1,0:T(8,128)(2,1)S(1)}, u32[]{:S(2)}, u32[]{:S(2)}) collective-permute-start(bf16[2,144,384]{2,1,0:T(8,128)(2,1)S(1)} %copy-done.6), channel_id=1, source_target_pairs={{0,4},{1,5},{2,6},{3,7},{4,0},{5,1},{6,2},{7,3},{8,12},{9,13},{10,... | collective-permute-start | bytes 663560 | tf_op jit(solution)/shard_map/ppermute | solution.py:328
  63.6 5.1 %collective-permute-done.7.got_ref = bf16[2,144,384]{2,1,0:T(8,128)(2,1)S(1)} collective-permute-done((bf16[2,144,384]{2,1,0:T(8,128)(2,1)S(1)}, bf16[2,144,384]{2,1,0:T(8,128)(2,1)S(1)}, u32[]{:S(2)}, u32[]{:S(2)}) %collective-permute-start.7) | collective-permute-done | bytes 221216 | tf_op jit(solution)/shard_map/ppermute | solution.py:328
  68.7 0.0 copy-done.1
  68.7 1.4 %shard_map.88 = (f32[16,128]{1,0:T(8,128)}, f32[256,128]{1,0:T(8,128)}, bf16[2,256,384]{2,1,0:T(8,128)(2,1)}) custom-call(s32[6]{0:T(128)S(1)} %stack.23.place, bf16[16,128]{1,0:T(8,128)(2,1)S(1)} %get-tuple-element.18.mask_ref, bf16[2,128,384]{2,1,0:T(8,128)(2,1)S(1)} %copy-done.1, bf16[2,144,384]{2,1,0:T(8,128)(2,1)S(1)} %collective-permute-done.7.got_ref), custom_call_target="tpu_custom_call" | custom-call | tf_op jit(solution)/shard_map/pallas_call | solution.py:372
  70.1 0.0 copy-start.2
  70.1 0.7 copy-done.2
  70.8 19.8 %shard_map.89 = (f32[3,2,128,768]{3,2,1,0:T(8,128)S(1)}, bf16[3,2,768,768]{3,2,1,0:T(8,128)(2,1)S(1)}, f32[3,2,1,768]{3,2,1,0:T(1,128)S(1)}) custom-call(f32[16,128]{1,0:T(8,128)S(1)} %copy-done.2, bf16[8,2,192,384]{3,2,1,0:T(8,128)(2,1)S(1)} %all-to-all-done.1.vq_ref.q_ref.v_ref, bf16[8,2,192,384]{3,2,1,0:T(8,128)(2,1)S(1)} %all-to-all-done.1.vq_ref.q_ref.v_ref, ...), custom_call_target="tpu_custom_call" | custom-call | tf_op jit(solution)/shard_map/pallas_call | solution.py:126
  90.6 0.0 collective-permute-done.5.before_ref
  90.6 0.0 collective-permute-done.6.after_ref
  90.7 3.1 %shard_map.90 = bf16[8,192,384]{2,1,0:T(8,128)(2,1)S(1)} custom-call(bf16[4,192,384]{2,1,0:T(8,128)(2,1)S(1)} %collective-permute-done.5.before_ref, bf16[4,192,384]{2,1,0:T(8,128)(2,1)S(1)} %collective-permute-done.6.after_ref, f32[3,2,128,768]{3,2,1,0:T(8,128)S(1)} %get-tuple-element.28.near_ref, bf16[3,2,768,768]{3,2,1,0:T(8,128)(2,1)S(1)} %get-tuple-element.29.far_ref, ...), custom_call_target="tpu_custom_call" | custom-call | tf_op jit(solution)/shard_map/pallas_call | solution.py:158
  93.7 20.2 %all_to_all.15.x_ref = bf16[8,192,384]{2,1,0:T(8,128)(2,1)S(1)} all-to-all(bf16[8,192,384]{2,1,0:T(8,128)(2,1)S(1)} %shard_map.90), channel_id=1, replica_groups={{0,1,2,3,4,5,6,7},{8,9,10,11,12,13,14,15},{16,17,18,19,20,21,22,23},{24..., dimensions={0} | all-to-all | bytes 2359296 | tf_op jit(solution)/shard_map/all_to_all | solution.py:331
  113.9 1.1 shard_map.91
  (1 shorter events, 0.0 us)
Async XLA Ops:
  2.2 5.9 %copy-start.4 = (s32[6]{0:T(128)S(1)}, s32[6]{0:T(128)}, u32[]{:S(2)}) copy-start(s32[6]{0:T(128)} %count.1) | copy-start | bytes 76
  2.2 21.0 %all-to-all-start = ((bf16[8,192,384]{2,1,0:T(8,128)(2,1)}), bf16[8,192,384]{2,1,0:T(8,128)(2,1)S(1)}, u32[]{:S(2)}, u32[]{:S(2)}) async-start(bf16[8,192,384]{2,1,0:T(8,128)(2,1)} %shard_map.83), calls=%async_computation | async-start | bytes 2359296 | tf_op jit(solution)/shard_map/all_to_all | solution.py:331
  9.6 8.3 %collective-permute-start = (bf16[2,32,768]{2,1,0:T(8,128)(2,1)S(1)}, bf16[2,32,768]{2,1,0:T(8,128)(2,1)S(1)}, u32[]{:S(2)}, u32[]{:S(2)}) collective-permute-start(bf16[2,32,768]{2,1,0:T(8,128)(2,1)S(1)} %get-tuple-element.19.refs_0_), channel_id=1, source_target_pairs={{0,8},{1,9},{2,10},{3,11},{4,12},{5,13},{6,14},{7,15},{8,16},{9,17... | collective-permute-start | bytes 294920 | tf_op jit(solution)/shard_map/ppermute | solution.py:324
  11.2 9.8 %collective-permute-start.1 = (bf16[2,32,768]{2,1,0:T(8,128)(2,1)S(1)}, bf16[2,32,768]{2,1,0:T(8,128)(2,1)S(1)}, u32[]{:S(2)}, u32[]{:S(2)}) collective-permute-start(bf16[2,32,768]{2,1,0:T(8,128)(2,1)S(1)} %get-tuple-element.19.refs_0_), channel_id=1, source_target_pairs={{0,16},{1,17},{2,18},{3,19},{4,20},{5,21},{6,22},{7,23},{8,24},{9,... | collective-permute-start | bytes 294920 | tf_op jit(solution)/shard_map/ppermute | solution.py:324
  13.8 7.2 %collective-permute-start.2 = (bf16[2,32,768]{2,1,0:T(8,128)(2,1)S(1)}, bf16[2,32,768]{2,1,0:T(8,128)(2,1)S(1)}, u32[]{:S(2)}, u32[]{:S(2)}) collective-permute-start(bf16[2,32,768]{2,1,0:T(8,128)(2,1)S(1)} %get-tuple-element.19.refs_0_), channel_id=1, source_target_pairs={{0,24},{1,25},{2,26},{3,27},{4,28},{5,29},{6,30},{7,31},{8,0},{9,1... | collective-permute-start | bytes 294920 | tf_op jit(solution)/shard_map/ppermute | solution.py:324
  23.2 4.3 %copy-start = (bf16[8,192,384]{2,1,0:T(8,128)(2,1)}, bf16[8,192,384]{2,1,0:T(8,128)(2,1)S(1)}, u32[]{:S(2)}) copy-start(bf16[8,192,384]{2,1,0:T(8,128)(2,1)S(1)} %all-to-all-done.__1_.k_ref) | copy-start | bytes 3538948
  23.2 0.7 copy-start.3
  23.9 34.0 %all-to-all-start.1 = ((bf16[8,2,192,384]{3,2,1,0:T(8,128)(2,1)}), bf16[8,2,192,384]{3,2,1,0:T(8,128)(2,1)S(1)}, u32[]{:S(2)}, u32[]{:S(2)}) async-start(bf16[8,2,192,384]{3,2,1,0:T(8,128)(2,1)} %shard_map.86), calls=%async_computation.1 | async-start | bytes 4718592 | tf_op jit(solution)/shard_map/all_to_all | solution.py:331
  27.7 18.1 %collective-permute-start.3 = (bf16[4,192,384]{2,1,0:T(8,128)(2,1)S(1)}, bf16[4,192,384]{2,1,0:T(8,128)(2,1)S(1)}, u32[]{:S(2)}, u32[]{:S(2)}) collective-permute-start(bf16[4,192,384]{2,1,0:T(8,128)(2,1)S(1)} %get-tuple-element.32), channel_id=1, source_target_pairs={{0,8},{1,9},{2,10},{3,11},{4,12},{5,13},{6,14},{7,15},{8,16},{9,17... | collective-permute-start | bytes 1769480 | tf_op jit(solution)/shard_map/ppermute | solution.py:324
  29.7 32.2 %copy-start.6 = (bf16[2,144,384]{2,1,0:T(8,128)(2,1)S(1)}, bf16[2,144,384]{2,1,0:T(8,128)(2,1)}, u32[]{:S(2)}) copy-start(bf16[2,144,384]{2,1,0:T(8,128)(2,1)} %get-tuple-element.24) | copy-start | bytes 663556
  29.7 38.9 %copy-start.1 = (bf16[2,128,384]{2,1,0:T(8,128)(2,1)S(1)}, bf16[2,128,384]{2,1,0:T(8,128)(2,1)}, u32[]{:S(2)}) copy-start(bf16[2,128,384]{2,1,0:T(8,128)(2,1)} %get-tuple-element.23.keep_ref) | copy-start | bytes 589828
  29.7 28.2 %collective-permute-start.4 = (bf16[4,192,384]{2,1,0:T(8,128)(2,1)S(1)}, bf16[4,192,384]{2,1,0:T(8,128)(2,1)}, u32[]{:S(2)}, u32[]{:S(2)}) collective-permute-start(bf16[4,192,384]{2,1,0:T(8,128)(2,1)S(1)} %get-tuple-element.31), channel_id=1, source_target_pairs={{0,24},{1,25},{2,26},{3,27},{4,28},{5,29},{6,30},{7,31},{8,0},{9,1... | collective-permute-start | bytes 1769480 | tf_op jit(solution)/shard_map/ppermute | solution.py:324
  45.7 12.2 %copy-start.5 = (bf16[4,192,384]{2,1,0:T(8,128)(2,1)}, bf16[4,192,384]{2,1,0:T(8,128)(2,1)S(1)}, u32[]{:S(2)}) copy-start(bf16[4,192,384]{2,1,0:T(8,128)(2,1)S(1)} %collective-permute-done.3._.before_ref) | copy-start | bytes 1769476
  58.0 32.6 %collective-permute-start.5 = (bf16[4,192,384]{2,1,0:T(8,128)(2,1)S(1)}, bf16[4,192,384]{2,1,0:T(8,128)(2,1)S(1)}, u32[]{:S(2)}, u32[]{:S(2)}) collective-permute-start(bf16[4,192,384]{2,1,0:T(8,128)(2,1)S(1)} %get-tuple-element.21), channel_id=1, source_target_pairs={{0,8},{1,9},{2,10},{3,11},{4,12},{5,13},{6,14},{7,15},{8,16},{9,17... | collective-permute-start | bytes 1769480 | tf_op jit(solution)/shard_map/ppermute | solution.py:324
  58.7 32.0 %collective-permute-start.6 = (bf16[4,192,384]{2,1,0:T(8,128)(2,1)S(1)}, bf16[4,192,384]{2,1,0:T(8,128)(2,1)S(1)}, u32[]{:S(2)}, u32[]{:S(2)}) collective-permute-start(bf16[4,192,384]{2,1,0:T(8,128)(2,1)S(1)} %get-tuple-element.22), channel_id=1, source_target_pairs={{0,24},{1,25},{2,26},{3,27},{4,28},{5,29},{6,30},{7,31},{8,0},{9,1... | collective-permute-start | bytes 1769480 | tf_op jit(solution)/shard_map/ppermute | solution.py:324
  61.9 6.7 %collective-permute-start.7 = (bf16[2,144,384]{2,1,0:T(8,128)(2,1)S(1)}, bf16[2,144,384]{2,1,0:T(8,128)(2,1)S(1)}, u32[]{:S(2)}, u32[]{:S(2)}) collective-permute-start(bf16[2,144,384]{2,1,0:T(8,128)(2,1)S(1)} %copy-done.6), channel_id=1, source_target_pairs={{0,4},{1,5},{2,6},{3,7},{4,0},{5,1},{6,2},{7,3},{8,12},{9,13},{10,... | collective-permute-start | bytes 663560 | tf_op jit(solution)/shard_map/ppermute | solution.py:328
  70.1 0.7 copy-start.2

commit v4 on v3

--- a/solution.py
+++ b/solution.py
@@ -13,6 +13,8 @@
 AXES = ("frame", "head")
 SCALE = math.log2(math.e) / math.sqrt(HD)
 LOW = -1e30
+FLOOR = -1e29
+CHUNK = 3
 NT = (((1,), (1,)), ((), ()))
 SMEM = pl.BlockSpec(memory_space=pltpu.SMEM)
 ANY = pl.BlockSpec(memory_space=pl.ANY)
@@ -24,18 +26,23 @@
     return pltpu.with_memory_space_constraint(x, pltpu.HBM)
 
 
-def weigh(queries, keys, biases):
-    scores = lax.dot_general(keys, queries, NT, preferred_element_type=jnp.float32)
-    key_tiles, query_tiles = keys.shape[0] // TILE, queries.shape[0] // TILE
+def weigh(scores, biases):
+    key_tiles, query_tiles = scores.shape[0] // TILE, scores.shape[1] // TILE
     tops, totals, weights = [], [], []
     for t in range(query_tiles):
         blocks = [
-            scores[u * TILE : (u + 1) * TILE, t * TILE : (t + 1) * TILE] + biases[u][t]
-            for u in range(key_tiles)
+            scores[u * TILE : (u + 1) * TILE, t * TILE : (t + 1) * TILE] for u in range(key_tiles)
         ]
-        top = functools.reduce(jnp.maximum, blocks)
-        top = jnp.max(top, axis=0, keepdims=True)
-        parts = [jnp.exp2((block - top) * SCALE) for block in blocks]
+        tops_of = [
+            jnp.max(block + bias[t], axis=0, keepdims=True)
+            if bias[t].ndim
+            else jnp.max(block, axis=0, keepdims=True) + bias[t]
+            for block, bias in zip(blocks, biases)
+        ]
+        top = jnp.maximum(functools.reduce(jnp.maximum, tops_of), FLOOR)
+        parts = [
+            jnp.exp2((block - (top - bias[t])) * SCALE) for block, bias in zip(blocks, biases)
+        ]
         total = functools.reduce(jnp.add, parts)
         tops.append(top)
         totals.append(jnp.sum(total, axis=0, keepdims=True))
@@ -44,11 +51,6 @@
     return join(weights), join(tops), join(totals)
 
 
-def group(queries, keys, values_t, biases):
-    weights, top, total = weigh(queries, keys, biases)
-    return jnp.dot(values_t, weights, preferred_element_type=jnp.float32), top, total
-
-
 def merge(one, two):
     top = jnp.maximum(one[1], two[1])
     first, second = jnp.exp2((one[1] - top) * SCALE), jnp.exp2((two[1] - top) * SCALE)
@@ -61,14 +63,16 @@
 
 def near_kernel(
     tiles,
+    chunk,
     bias,
     q_ref,
     v_ref,
     k_ref,
     before_ref,
     after_ref,
-    text_ref,
-    text_bias_ref,
+    keep_ref,
+    got_ref,
+    add_ref,
     near_ref,
     far_ref,
     scale_ref,
@@ -78,36 +82,45 @@
     own, other = pl.ds(side * half, half), pl.ds((1 - side) * half, half)
     queries = flat(q_ref[:, 0])
     at = lambda t, u: bias[side * 8 + t, u]
-    span = range(tiles)
-    own_bias = [[at(t, u) for t in span] for u in span]
-    own_bias += [
-        [text_bias_ref[j * TILE : (j + 1) * TILE, :]] * tiles
-        for j in range(text_bias_ref.shape[0] // TILE)
-    ]
-    mine = group(
-        queries,
-        jnp.concatenate([flat(k_ref[own]), text_ref[0]], axis=0),
-        jnp.concatenate([flat(v_ref[own, 0]), text_ref[1]], axis=0).T,
-        own_bias,
+    adds = [add_ref[j * TILE : (j + 1) * TILE, :] for j in range(add_ref.shape[0] // TILE)]
+    keys = (
+        jnp.concatenate([flat(k_ref[own]), keep_ref[0], got_ref[0]], axis=0),
+        flat(k_ref[other]),
+        jnp.where(side == 0, flat(before_ref[...]), flat(after_ref[...])),
     )
-    near = group(
-        queries,
-        flat(k_ref[other]),
+    values = (
+        jnp.concatenate([flat(v_ref[own, 0]), keep_ref[1], got_ref[1]], axis=0).T,
         flat(v_ref[other, 0]).T,
-        [[at(t, tiles + u) for t in span] for u in span],
     )
-    weights, far_top, far_total = weigh(
-        queries,
-        jnp.where(side == 0, flat(before_ref[...]), flat(after_ref[...])),
-        [[at(t, 2 * tiles + u) for t in span] for u in span],
-    )
-    weighted, top, total = merge(mine, near)
-    best = jnp.maximum(top, far_top)
-    near_scale, far_scale = jnp.exp2((top - best) * SCALE), jnp.exp2((far_top - best) * SCALE)
-    total = total * near_scale + far_total * far_scale
-    near_ref[0, 0] = weighted * (near_scale / total)
-    far_ref[0, 0] = weights
-    scale_ref[0, 0] = far_scale / total
+    works = [(c, g) for c in range(0, tiles, chunk) for g in range(3)]
+
+    def scores_of(c, g):
+        some = queries[c * TILE : (c + chunk) * TILE]
+        return lax.dot_general(keys[g], some, NT, preferred_element_type=jnp.float32)
+
+    ahead, done = scores_of(*works[0]), []
+    for i, (c, g) in enumerate(works):
+        scores = ahead
+        if i + 1 < len(works):
+            ahead = scores_of(*works[i + 1])
+        biases = [[at(t, g * tiles + u) for t in range(c, c + chunk)] for u in range(tiles)]
+        if g == 0:
+            biases += [[add] * chunk for add in adds]
+        weights, top, total = weigh(scores, biases)
+        lanes = slice(c * TILE, (c + chunk) * TILE)
+        if g < 2:
+            weighted = jnp.dot(values[g], weights, preferred_element_type=jnp.float32)
+            done.append((weighted, top, total))
+        else:
+            far_ref[0, 0, :, lanes] = weights
+            weighted, near_top, near_total = merge(*done)
+            best = jnp.maximum(near_top, top)
+            near_scale = jnp.exp2((near_top - best) * SCALE)
+            far_scale = jnp.exp2((top - best) * SCALE)
+            whole = near_total * near_scale + total * far_scale
+            near_ref[0, 0, :, lanes] = weighted * (near_scale / whole)
+            scale_ref[0, 0, :, lanes] = far_scale / whole
+            done = []
 
 
 def far_kernel(before_ref, after_ref, near_ref, far_ref, scale_ref, out_ref):
@@ -118,13 +131,14 @@
     out_ref[...] = out.T.astype(out_ref.dtype).reshape(out_ref.shape)
 
 
-def near_attention(tiles, bias, vq, k, k_before, k_after, text, text_bias):
+def near_attention(tiles, bias, vq, k, k_before, k_after, keep, got, add):
     ways, _, rows, part = vq.shape
     heads, half, length = part // HD, ways // 2, tiles * TILE
     far = pl.BlockSpec((half, rows, HD), lambda h, s: (0, 0, h))
+    text = pl.BlockSpec((2, keep.shape[1], HD), lambda h, s: (0, 0, h))
     at = lambda h, s: (h, s, 0, 0)
     return pl.pallas_call(
-        functools.partial(near_kernel, tiles),
+        functools.partial(near_kernel, tiles, CHUNK if tiles % CHUNK == 0 else 1),
         grid=(heads, 2),
         in_specs=[
             SMEM,
@@ -133,8 +147,9 @@
             pl.BlockSpec((ways, rows, HD), lambda h, s: (0, 0, h)),
             far,
             far,
-            pl.BlockSpec((2, text.shape[1], HD), lambda h, s: (0, 0, h)),
-            pl.BlockSpec(text_bias.shape, lambda h, s: (0, 0)),
+            text,
+            text,
+            pl.BlockSpec(add.shape, lambda h, s: (0, 0)),
         ],
         out_specs=[
             pl.BlockSpec((1, 1, HD, length), at),
@@ -147,7 +162,7 @@
             jax.ShapeDtypeStruct((heads, 2, 1, length), jnp.float32),
         ],
         compiler_params=LARGE,
-    )(bias, vq, vq, k, k_before, k_after, text, text_bias)
+    )(bias, vq, vq, k, k_before, k_after, keep, got, add)
 
 
 def far_attention(v_before, v_after, near, weights, scales):
@@ -198,10 +213,14 @@
         write.wait()
 
 
-def join_kernel(order, x_ref, out_ref):
-    part = x_ref.shape[2]
+def join_kernel(order, *refs):
+    parts, out_ref = refs[:-1], refs[-1]
+    width = out_ref.shape[1] // len(order)
     for p, g in enumerate(order):
-        out_ref[:, g * part : (g + 1) * part] = x_ref[p]
+        at = g * width
+        for ref in parts:
+            out_ref[:, at : at + ref.shape[2]] = ref[p]
+            at += ref.shape[2]
 
 
 def split_heads(order, arrays):
@@ -222,13 +241,14 @@
     )(*(far_memory(x) for x in arrays))
 
 
-def join_heads(x, order):
-    ways, rows, part = x.shape
+def join_heads(order, *parts):
+    ways, rows, _ = parts[0].shape
+    width = sum(x.shape[2] for x in parts)
     return pl.pallas_call(
         functools.partial(join_kernel, order),
-        out_shape=jax.ShapeDtypeStruct((rows, ways * part), x.dtype),
-        compiler_params=SMALL,
-    )(x)
+        out_shape=jax.ShapeDtypeStruct((rows, ways * width), jnp.bfloat16),
+        compiler_params=SMALL,
+    )(*parts)
 
 
 def mask_kernel(tiles, place, count, list_hbm, k_ref, v_ref, mask_ref, text_ref, list_ref, sems):
@@ -253,17 +273,28 @@
     mask_ref[...] = jnp.concatenate([mask, spare], axis=0).astype(jnp.bfloat16)
 
 
-def turn_kernel(pieces, place, mask_ref, *refs):
-    texts, (offer_ref, keep_ref, done_ref) = refs[:pieces], refs[-3:]
-    done_ref[...] = jnp.zeros_like(done_ref)
+def turn_kernel(pairs, pieces, place, mask_ref, their_ref, *refs):
+    texts, (offer_ref, keep_ref, bias_ref, add_ref) = refs[:pieces], refs[pieces:]
     low = place[3] == 0
     part = offer_ref.shape[2]
     for i in range(2):
         one = jnp.concatenate([t[i, :, :part] for t in texts], axis=0)
         two = jnp.concatenate([t[i, :, part:] for t in texts], axis=0)
-        offer_ref[i, : one.shape[0]] = jnp.where(low, two, one)
+        offer_ref[i] = jnp.where(low, two, one)
         keep_ref[i] = jnp.where(low, one, two)
-    offer_ref[0, keep_ref.shape[1] :, 0:TILE] = mask_ref[...]
+    mine, theirs = mask_ref[...], their_ref[...]
+    for i, block in enumerate((jnp.where(low, mine, theirs), jnp.where(low, theirs, mine))):
+        block = block.astype(jnp.float32)[0:8]
+        bias_ref[8 * i : 8 * i + 8, :] = jnp.where(block > 0.5, 0.0, LOW)
+    spread = keep_ref.shape[1]
+    rows = spread // pairs
+    spot = lax.broadcasted_iota(jnp.int32, add_ref.shape, 0)
+    side = jnp.where(spot < spread, place[3], 1 - place[3])
+    spot = jnp.where(spot < spread, spot, spot - spread)
+    pair = place[4] - spot // rows
+    pair = jnp.where(pair < 0, pair + pairs, pair)
+    token = (2 * pair + side) * rows + spot % rows
+    add_ref[...] = jnp.where(token < place[5], 0.0, LOW)
 
 
 def halves_kernel(vq_ref, _, __, low_ref, high_ref):
@@ -285,27 +316,6 @@
         input_output_aliases={0: 0},
         compiler_params=SMALL,
     )(far_memory(x), *first)
-
-
-def bias_kernel(
-    pairs, rows, place, mask_ref, keep_ref, got_ref, bias_ref, text_ref, all_ref
-):
-    low = place[3] == 0
-    for i in range(2):
-        all_ref[i] = jnp.concatenate([keep_ref[i], got_ref[i, : keep_ref.shape[1]]], axis=0)
-    start = got_ref.shape[1] - mask_ref.shape[0]
-    mine, theirs = mask_ref[...], got_ref[0, start:, 0:TILE]
-    for i, block in enumerate((jnp.where(low, mine, theirs), jnp.where(low, theirs, mine))):
-        block = block.astype(jnp.float32)[0:8]
-        bias_ref[8 * i : 8 * i + 8, :] = jnp.where(block > 0.5, 0.0, LOW)
-    spot = lax.broadcasted_iota(jnp.int32, text_ref.shape, 0)
-    spread = pairs * rows
-    side = jnp.where(spot < spread, place[3], 1 - place[3])
-    spot = jnp.where(spot < spread, spot, spot - spread)
-    pair = place[4] - spot // rows
-    pair = jnp.where(pair < 0, pair + pairs, pair)
-    token = (2 * pair + side) * rows + spot % rows
-    text_ref[...] = jnp.where(token < place[5], 0.0, LOW)
 
 
 def body(queries, keys, values, text_keys, text_values, lists, counts, text_len):
@@ -357,44 +367,31 @@
             text, have = jnp.concatenate([text, more], axis=1), have + take
         texts = [text]
     all_text = pairs * text_rows
-    offer, keep, turned = pl.pallas_call(
-        functools.partial(turn_kernel, len(texts)),
-        in_specs=[SMEM] + [pl.BlockSpec()] * (1 + len(texts)),
+    offer, keep, bias, add = pl.pallas_call(
+        functools.partial(turn_kernel, pairs, len(texts)),
+        in_specs=[SMEM] + [pl.BlockSpec()] * (2 + len(texts)),
         out_shape=[
-            pltpu.HBM((2, all_text + mask.shape[0], part), jnp.bfloat16),
             pltpu.HBM((2, all_text, part), jnp.bfloat16),
-            pltpu.HBM((8, TILE), jnp.float32),
-        ],
-        compiler_params=SMALL,
-    )(place, mask, *texts)
-    got = swapped(offer)
-
-    bias, text_bias, text = pl.pallas_call(
-        functools.partial(bias_kernel, pairs, text_rows),
-        in_specs=[SMEM] + [pl.BlockSpec()] * 3,
-        out_shape=[
+            pltpu.HBM((2, all_text, part), jnp.bfloat16),
             pltpu.HBM((16, TILE), jnp.float32),
             pltpu.HBM((2 * all_text, TILE), jnp.float32),
-            pltpu.HBM((2, 2 * all_text, part), jnp.bfloat16),
-        ],
-        compiler_params=SMALL,
-    )(place, mask, keep, got)
+        ],
+        compiler_params=SMALL,
+    )(place, mask, swapped(mask), *texts)
+    got, keep, add = far_memory(swapped(offer)), far_memory(keep), far_memory(add)
 
     k_before, k_after = far_memory(shifted(k[heads:], 1)), far_memory(shifted(k[:heads], -1))
-    vq = exchange(gated(split_heads(order, (values, queries)), k, turned))
-
-    half = jax.ShapeDtypeStruct((heads, rows, part), jnp.bfloat16)
+    vq = exchange(gated(split_heads(order, (values, queries)), k, add))
+
     v_low, v_high = pl.pallas_call(
         halves_kernel,
         in_specs=[pl.BlockSpec()] + [ANY] * 2,
-        out_shape=[half, half],
+        out_shape=[jax.ShapeDtypeStruct((heads, rows, part), jnp.bfloat16)] * 2,
         compiler_params=SMALL,
     )(vq, k_before, k_after)
     v_before, v_after = shifted(v_high, 1), shifted(v_low, -1)
-    text, text_bias = far_memory(text), far_memory(text_bias)
-    partial = near_attention(tiles, bias, vq, far_memory(k), k_before, k_after, text, text_bias)
-    out = far_attention(v_before, v_after, *partial)
-    return join_heads(exchange(out), order)
+    partial = near_attention(tiles, bias, vq, far_memory(k), k_before, k_after, keep, got, add)
+    return join_heads(order, exchange(far_attention(v_before, v_after, *partial)))
 
 
 def solution(mesh):

time: 116 us -> 112 us (0.966)
  Pallas kernels: 33.3 us -> 30.1 us
  starting transfers between devices: 23.8 us -> 25.8 us
  waiting for transfers between devices: 35.4 us -> 33.7 us
    ppermute x7, waiting for transfers between devices: 29.4 us -> 26.2 us  [shifted(): lax.ppermute(x, AXES, [(i, (i + by * ways) % count) for i in range(count)])]
    pallas_call x3 -> x2, Pallas kernels: 22.6 us -> 19.5 us  [the longest x1 18.1 us: near_attention(): pl.pallas_call(functools.partial(near_kernel, tiles, CHUNK if tiles % CHU...]
    ppermute x1 -> x2, waiting for transfers between devices: 5.08 us -> 7.49 us  [swapped(): return lax.ppermute(x, AXES, [(i, flip(i)) for i in range(count)])]
    ppermute x1 -> x2, starting transfers between devices: 1.67 us -> 3.67 us  [swapped(): return lax.ppermute(x, AXES, [(i, flip(i)) for i in range(count)])]
  transfers between devices with their start and end apart: 10 -> 11, of which waited for: 5 -> 5; matrix products, arithmetic and copies ran while one was open for 0% -> 0% of each run, Pallas kernels for 23% -> 21%
where the time goes in v4:
time: 112 us
  waiting for transfers between devices  33.7 us (30%)
  Pallas kernels  30.1 us (27%)
  starting transfers between devices  25.8 us (23%)
  blocking collectives  20.2 us (18%)
    ppermute x7, waiting for transfers between devices, shifted(): lax.ppermute(x, AXES, [(i, (i + by * ways) % count) for i in range(count)])  26.2 us
    all_to_all x1, blocking collectives, exchange(): lax.all_to_all(x, AXES, split_axis=0, concat_axis=0, tiled=True, axis_ind...  20.2 us
    pallas_call x1, Pallas kernels, near_attention(): pl.pallas_call(functools.partial(near_kernel, tiles, CHUNK if tiles % CHU...  18.1 us
    ppermute x7, starting transfers between devices, shifted(): lax.ppermute(x, AXES, [(i, (i + by * ways) % count) for i in range(count)])  13.3 us
    all_to_all x2, starting transfers between devices, exchange(): lax.all_to_all(x, AXES, split_axis=0, concat_axis=0, tiled=True, axis_ind...  8.8 us
    ppermute x2, waiting for transfers between devices, swapped(): return lax.ppermute(x, AXES, [(i, flip(i)) for i in range(count)])  7.49 us
    pallas_call x2, Pallas kernels, split_heads(): pl.pallas_call(functools.partial(split_kernel, order, count), in_specs=[A...  4.88 us
    ppermute x2, starting transfers between devices, swapped(): return lax.ppermute(x, AXES, [(i, flip(i)) for i in range(count)])  3.67 us
  transfers between devices with their start and end apart: 11, of which 5 were waited for; matrix products, arithmetic and copies ran while one was open for 0% of the time, Pallas kernels for 21%

profile of v4, /device:TPU:0, one launch (start us, length us, event | category | flops | bytes accessed | tf_op | source)
XLA Modules:
  0.0 111.5 jit_solution(8096473813865066388)
XLA Ops:
  0.0 2.2 %shard_map.83 = bf16[8,192,384]{2,1,0:T(8,128)(2,1)} custom-call(bf16[192,3072]{1,0:T(8,128)(2,1)} %refs_0_.3), custom_call_target="tpu_custom_call" | custom-call | tf_op jit(solution)/shard_map/pallas_call | solution.py:230
  2.2 0.0 copy-start.2
  2.2 5.2 %all-to-all-start = ((bf16[8,192,384]{2,1,0:T(8,128)(2,1)}), bf16[8,192,384]{2,1,0:T(8,128)(2,1)S(1)}, u32[]{:S(2)}, u32[]{:S(2)}) async-start(bf16[8,192,384]{2,1,0:T(8,128)(2,1)} %shard_map.83), calls=%async_computation | async-start | bytes 2359296 | tf_op jit(solution)/shard_map/all_to_all | solution.py:341
  8.0 0.1 stack.23.place
  8.1 0.0 copy-done.2
  8.1 1.5 %shard_map.84 = (bf16[16,128]{1,0:T(8,128)(2,1)S(1)}, bf16[2,32,768]{2,1,0:T(8,128)(2,1)S(1)}) custom-call(s32[6]{0:T(128)S(1)} %stack.23.place, s32[6]{0:T(128)S(1)} %copy-done.2, s32[6,12]{1,0:T(8,128)} %list_hbm.1, bf16[32,768]{1,0:T(8,128)(2,1)} %k_ref.1, bf16[32,768]{1,0:T(8,128)(2,1)} %v_ref.1), custom_call_target="tpu_custom_call" | custom-call | tf_op jit(solution)/shard_map/pallas_call | solution.py:350
  9.6 1.6 %collective-permute-start.1 = (bf16[2,32,768]{2,1,0:T(8,128)(2,1)S(1)}, bf16[2,32,768]{2,1,0:T(8,128)(2,1)S(1)}, u32[]{:S(2)}, u32[]{:S(2)}) collective-permute-start(bf16[2,32,768]{2,1,0:T(8,128)(2,1)S(1)} %get-tuple-element.17.refs_0_), channel_id=1, source_target_pairs={{0,8},{1,9},{2,10},{3,11},{4,12},{5,13},{6,14},{7,15},{8,16},{9,17... | collective-permute-start | bytes 294920 | tf_op jit(solution)/shard_map/ppermute | solution.py:334
  11.2 2.6 %collective-permute-start.2 = (bf16[2,32,768]{2,1,0:T(8,128)(2,1)S(1)}, bf16[2,32,768]{2,1,0:T(8,128)(2,1)S(1)}, u32[]{:S(2)}, u32[]{:S(2)}) collective-permute-start(bf16[2,32,768]{2,1,0:T(8,128)(2,1)S(1)} %get-tuple-element.17.refs_0_), channel_id=1, source_target_pairs={{0,16},{1,17},{2,18},{3,19},{4,20},{5,21},{6,22},{7,23},{8,24},{9,... | collective-permute-start | bytes 294920 | tf_op jit(solution)/shard_map/ppermute | solution.py:334
  13.8 1.3 %collective-permute-start.3 = (bf16[2,32,768]{2,1,0:T(8,128)(2,1)S(1)}, bf16[2,32,768]{2,1,0:T(8,128)(2,1)S(1)}, u32[]{:S(2)}, u32[]{:S(2)}) collective-permute-start(bf16[2,32,768]{2,1,0:T(8,128)(2,1)S(1)} %get-tuple-element.17.refs_0_), channel_id=1, source_target_pairs={{0,24},{1,25},{2,26},{3,27},{4,28},{5,29},{6,30},{7,31},{8,0},{9,1... | collective-permute-start | bytes 294920 | tf_op jit(solution)/shard_map/ppermute | solution.py:334
  15.2 2.0 %collective-permute-start = (bf16[16,128]{1,0:T(8,128)(2,1)S(1)}, bf16[16,128]{1,0:T(8,128)(2,1)S(1)}, u32[]{:S(2)}, u32[]{:S(2)}) collective-permute-start(bf16[16,128]{1,0:T(8,128)(2,1)S(1)} %get-tuple-element.16.mask_ref), channel_id=1, source_target_pairs={{0,4},{1,5},{2,6},{3,7},{4,0},{5,1},{6,2},{7,3},{8,12},{9,13},{10,... | collective-permute-start | bytes 12296 | tf_op jit(solution)/shard_map/ppermute | solution.py:338
  17.2 2.7 %shard_map.82.__0_ = bf16[8,2,192,384]{3,2,1,0:T(8,128)(2,1)} custom-call(bf16[192,3072]{1,0:T(8,128)(2,1)} %refs_0_.2, bf16[192,3072]{1,0:T(8,128)(2,1)} %refs_1_.1), custom_call_target="tpu_custom_call" | custom-call | tf_op jit(solution)/shard_map/pallas_call | solution.py:230
  19.9 3.4 %collective-permute-done.their_ref = bf16[16,128]{1,0:T(8,128)(2,1)S(1)} collective-permute-done((bf16[16,128]{1,0:T(8,128)(2,1)S(1)}, bf16[16,128]{1,0:T(8,128)(2,1)S(1)}, u32[]{:S(2)}, u32[]{:S(2)}) %collective-permute-start) | collective-permute-done | bytes 4128 | tf_op jit(solution)/shard_map/ppermute | solution.py:338
  23.3 0.0 collective-permute-done.1.refs_1_
  23.3 0.0 collective-permute-done.2.refs_2_
  23.3 0.0 collective-permute-done.3.refs_3_
  23.3 1.4 %shard_map.85 = (bf16[2,128,384]{2,1,0:T(8,128)(2,1)}, bf16[2,128,384]{2,1,0:T(8,128)(2,1)}, f32[16,128]{1,0:T(8,128)}, f32[256,128]{1,0:T(8,128)}) custom-call(s32[6]{0:T(128)S(1)} %stack.23.place, bf16[16,128]{1,0:T(8,128)(2,1)S(1)} %get-tuple-element.16.mask_ref, bf16[16,128]{1,0:T(8,128)(2,1)S(1)} %collective-permute-done.their_ref, ...), custom_call_target="tpu_custom_call" | custom-call | tf_op jit(solution)/shard_map/pallas_call | solution.py:370
  24.7 0.0 all-to-all-done.__1_.k_ref
  24.7 0.0 copy-start
  24.7 3.6 %all-to-all-start.1 = ((bf16[8,2,192,384]{3,2,1,0:T(8,128)(2,1)}), bf16[8,2,192,384]{3,2,1,0:T(8,128)(2,1)S(1)}, u32[]{:S(2)}, u32[]{:S(2)}) async-start(bf16[8,2,192,384]{3,2,1,0:T(8,128)(2,1)} %shard_map.86), calls=%async_computation.1 | async-start | bytes 4718592 | tf_op jit(solution)/shard_map/all_to_all | solution.py:341
  28.3 0.0 copy-done
  28.4 0.1 fusion
  28.5 1.6 %collective-permute-start.4 = (bf16[4,192,384]{2,1,0:T(8,128)(2,1)S(1)}, bf16[4,192,384]{2,1,0:T(8,128)(2,1)S(1)}, u32[]{:S(2)}, u32[]{:S(2)}) collective-permute-start(bf16[4,192,384]{2,1,0:T(8,128)(2,1)S(1)} %get-tuple-element.28), channel_id=1, source_target_pairs={{0,8},{1,9},{2,10},{3,11},{4,12},{5,13},{6,14},{7,15},{8,16},{9,17... | collective-permute-start | bytes 1769480 | tf_op jit(solution)/shard_map/ppermute | solution.py:334
  30.1 0.0 copy-start.5
  30.1 0.0 copy-start.1
  30.1 2.2 %collective-permute-start.5 = (bf16[4,192,384]{2,1,0:T(8,128)(2,1)S(1)}, bf16[4,192,384]{2,1,0:T(8,128)(2,1)}, u32[]{:S(2)}, u32[]{:S(2)}) collective-permute-start(bf16[4,192,384]{2,1,0:T(8,128)(2,1)S(1)} %get-tuple-element.27), channel_id=1, source_target_pairs={{0,24},{1,25},{2,26},{3,27},{4,28},{5,29},{6,30},{7,31},{8,0},{9,1... | collective-permute-start | bytes 1769480 | tf_op jit(solution)/shard_map/ppermute | solution.py:334
  32.4 14.1 %collective-permute-done.4._.before_ref = bf16[4,192,384]{2,1,0:T(8,128)(2,1)S(1)} collective-permute-done((bf16[4,192,384]{2,1,0:T(8,128)(2,1)S(1)}, bf16[4,192,384]{2,1,0:T(8,128)(2,1)S(1)}, u32[]{:S(2)}, u32[]{:S(2)}) %collective-permute-start.4) | collective-permute-done | bytes 589856 | tf_op jit(solution)/shard_map/ppermute | solution.py:334
  46.5 0.0 copy-start.3
  46.5 11.7 %collective-permute-done.5.__.after_ref = bf16[4,192,384]{2,1,0:T(8,128)(2,1)} collective-permute-done((bf16[4,192,384]{2,1,0:T(8,128)(2,1)S(1)}, bf16[4,192,384]{2,1,0:T(8,128)(2,1)}, u32[]{:S(2)}, u32[]{:S(2)}) %collective-permute-start.5) | collective-permute-done | bytes 589856 | tf_op jit(solution)/shard_map/ppermute | solution.py:334
  58.2 0.0 all-to-all-done.1.vq_ref.q_ref.v_ref
  58.3 0.0 copy-done.3
  58.3 0.1 shard_map.87
  58.4 1.1 %collective-permute-start.6 = (bf16[4,192,384]{2,1,0:T(8,128)(2,1)S(1)}, bf16[4,192,384]{2,1,0:T(8,128)(2,1)S(1)}, u32[]{:S(2)}, u32[]{:S(2)}) collective-permute-start(bf16[4,192,384]{2,1,0:T(8,128)(2,1)S(1)} %get-tuple-element.19), channel_id=1, source_target_pairs={{0,8},{1,9},{2,10},{3,11},{4,12},{5,13},{6,14},{7,15},{8,16},{9,17... | collective-permute-start | bytes 1769480 | tf_op jit(solution)/shard_map/ppermute | solution.py:334
  59.5 2.7 %collective-permute-start.7 = (bf16[4,192,384]{2,1,0:T(8,128)(2,1)S(1)}, bf16[4,192,384]{2,1,0:T(8,128)(2,1)S(1)}, u32[]{:S(2)}, u32[]{:S(2)}) collective-permute-start(bf16[4,192,384]{2,1,0:T(8,128)(2,1)S(1)} %get-tuple-element.20), channel_id=1, source_target_pairs={{0,24},{1,25},{2,26},{3,27},{4,28},{5,29},{6,30},{7,31},{8,0},{9,1... | collective-permute-start | bytes 1769480 | tf_op jit(solution)/shard_map/ppermute | solution.py:334
  62.2 0.0 copy-done.5
  62.2 1.7 %collective-permute-start.8 = (bf16[2,128,384]{2,1,0:T(8,128)(2,1)S(1)}, bf16[2,128,384]{2,1,0:T(8,128)(2,1)S(1)}, u32[]{:S(2)}, u32[]{:S(2)}) collective-permute-start(bf16[2,128,384]{2,1,0:T(8,128)(2,1)S(1)} %copy-done.5), channel_id=1, source_target_pairs={{0,4},{1,5},{2,6},{3,7},{4,0},{5,1},{6,2},{7,3},{8,12},{9,13},{10,... | collective-permute-start | bytes 589832 | tf_op jit(solution)/shard_map/ppermute | solution.py:338
  63.9 4.1 %collective-permute-done.8.got_ref = bf16[2,128,384]{2,1,0:T(8,128)(2,1)S(1)} collective-permute-done((bf16[2,128,384]{2,1,0:T(8,128)(2,1)S(1)}, bf16[2,128,384]{2,1,0:T(8,128)(2,1)S(1)}, u32[]{:S(2)}, u32[]{:S(2)}) %collective-permute-start.8) | collective-permute-done | bytes 196640 | tf_op jit(solution)/shard_map/ppermute | solution.py:338
  68.0 0.0 copy-start.4
  68.0 0.7 copy-done.4
  68.7 0.0 copy-done.1
  68.7 18.1 %shard_map.88 = (f32[3,2,128,768]{3,2,1,0:T(8,128)S(1)}, bf16[3,2,768,768]{3,2,1,0:T(8,128)(2,1)S(1)}, f32[3,2,1,768]{3,2,1,0:T(1,128)S(1)}) custom-call(f32[16,128]{1,0:T(8,128)S(1)} %copy-done.1, bf16[8,2,192,384]{3,2,1,0:T(8,128)(2,1)S(1)} %all-to-all-done.1.vq_ref.q_ref.v_ref, bf16[8,2,192,384]{3,2,1,0:T(8,128)(2,1)S(1)} %all-to-all-done.1.vq_ref.q_ref.v_ref, ...), custom_call_target="tpu_custom_call" | custom-call | tf_op jit(solution)/shard_map/pallas_call | solution.py:140
  86.8 0.0 collective-permute-done.6.before_ref
  86.8 0.3 collective-permute-done.7.after_ref
  87.1 3.0 %shard_map.89 = bf16[8,192,384]{2,1,0:T(8,128)(2,1)S(1)} custom-call(bf16[4,192,384]{2,1,0:T(8,128)(2,1)S(1)} %collective-permute-done.6.before_ref, bf16[4,192,384]{2,1,0:T(8,128)(2,1)S(1)} %collective-permute-done.7.after_ref, f32[3,2,128,768]{3,2,1,0:T(8,128)S(1)} %get-tuple-element.24.near_ref, bf16[3,2,768,768]{3,2,1,0:T(8,128)(2,1)S(1)} %get-tuple-element.25.far_ref, ...), custom_call_target="tpu_custom_call" | custom-call | tf_op jit(solution)/shard_map/pallas_call | solution.py:173
  90.2 20.2 %all_to_all.15.refs_0_ = bf16[8,192,384]{2,1,0:T(8,128)(2,1)S(1)} all-to-all(bf16[8,192,384]{2,1,0:T(8,128)(2,1)S(1)} %shard_map.89), channel_id=1, replica_groups={{0,1,2,3,4,5,6,7},{8,9,10,11,12,13,14,15},{16,17,18,19,20,21,22,23},{24..., dimensions={0} | all-to-all | bytes 2359296 | tf_op jit(solution)/shard_map/all_to_all | solution.py:341
  110.4 1.1 %shard_map.90 = bf16[192,3072]{1,0:T(8,128)(2,1)} custom-call(bf16[8,192,384]{2,1,0:T(8,128)(2,1)S(1)} %all_to_all.15.refs_0_), custom_call_target="tpu_custom_call" | custom-call | tf_op jit(solution)/shard_map/pallas_call | solution.py:247
  (1 shorter events, 0.0 us)
Async XLA Ops:
  2.2 5.9 %copy-start.2 = (s32[6]{0:T(128)S(1)}, s32[6]{0:T(128)}, u32[]{:S(2)}) copy-start(s32[6]{0:T(128)} %count.1) | copy-start | bytes 76
  2.2 22.5 %all-to-all-start = ((bf16[8,192,384]{2,1,0:T(8,128)(2,1)}), bf16[8,192,384]{2,1,0:T(8,128)(2,1)S(1)}, u32[]{:S(2)}, u32[]{:S(2)}) async-start(bf16[8,192,384]{2,1,0:T(8,128)(2,1)} %shard_map.83), calls=%async_computation | async-start | bytes 2359296 | tf_op jit(solution)/shard_map/all_to_all | solution.py:341
  9.6 13.7 %collective-permute-start.1 = (bf16[2,32,768]{2,1,0:T(8,128)(2,1)S(1)}, bf16[2,32,768]{2,1,0:T(8,128)(2,1)S(1)}, u32[]{:S(2)}, u32[]{:S(2)}) collective-permute-start(bf16[2,32,768]{2,1,0:T(8,128)(2,1)S(1)} %get-tuple-element.17.refs_0_), channel_id=1, source_target_pairs={{0,8},{1,9},{2,10},{3,11},{4,12},{5,13},{6,14},{7,15},{8,16},{9,17... | collective-permute-start | bytes 294920 | tf_op jit(solution)/shard_map/ppermute | solution.py:334
  11.2 12.1 %collective-permute-start.2 = (bf16[2,32,768]{2,1,0:T(8,128)(2,1)S(1)}, bf16[2,32,768]{2,1,0:T(8,128)(2,1)S(1)}, u32[]{:S(2)}, u32[]{:S(2)}) collective-permute-start(bf16[2,32,768]{2,1,0:T(8,128)(2,1)S(1)} %get-tuple-element.17.refs_0_), channel_id=1, source_target_pairs={{0,16},{1,17},{2,18},{3,19},{4,20},{5,21},{6,22},{7,23},{8,24},{9,... | collective-permute-start | bytes 294920 | tf_op jit(solution)/shard_map/ppermute | solution.py:334
  13.8 9.5 %collective-permute-start.3 = (bf16[2,32,768]{2,1,0:T(8,128)(2,1)S(1)}, bf16[2,32,768]{2,1,0:T(8,128)(2,1)S(1)}, u32[]{:S(2)}, u32[]{:S(2)}) collective-permute-start(bf16[2,32,768]{2,1,0:T(8,128)(2,1)S(1)} %get-tuple-element.17.refs_0_), channel_id=1, source_target_pairs={{0,24},{1,25},{2,26},{3,27},{4,28},{5,29},{6,30},{7,31},{8,0},{9,1... | collective-permute-start | bytes 294920 | tf_op jit(solution)/shard_map/ppermute | solution.py:334
  15.2 8.1 %collective-permute-start = (bf16[16,128]{1,0:T(8,128)(2,1)S(1)}, bf16[16,128]{1,0:T(8,128)(2,1)S(1)}, u32[]{:S(2)}, u32[]{:S(2)}) collective-permute-start(bf16[16,128]{1,0:T(8,128)(2,1)S(1)} %get-tuple-element.16.mask_ref), channel_id=1, source_target_pairs={{0,4},{1,5},{2,6},{3,7},{4,0},{5,1},{6,2},{7,3},{8,12},{9,13},{10,... | collective-permute-start | bytes 12296 | tf_op jit(solution)/shard_map/ppermute | solution.py:338
  24.7 3.6 %copy-start = (bf16[8,192,384]{2,1,0:T(8,128)(2,1)}, bf16[8,192,384]{2,1,0:T(8,128)(2,1)S(1)}, u32[]{:S(2)}) copy-start(bf16[8,192,384]{2,1,0:T(8,128)(2,1)S(1)} %all-to-all-done.__1_.k_ref) | copy-start | bytes 3538948
  24.7 33.5 %all-to-all-start.1 = ((bf16[8,2,192,384]{3,2,1,0:T(8,128)(2,1)}), bf16[8,2,192,384]{3,2,1,0:T(8,128)(2,1)S(1)}, u32[]{:S(2)}, u32[]{:S(2)}) async-start(bf16[8,2,192,384]{3,2,1,0:T(8,128)(2,1)} %shard_map.86), calls=%async_computation.1 | async-start | bytes 4718592 | tf_op jit(solution)/shard_map/all_to_all | solution.py:341
  28.5 18.0 %collective-permute-start.4 = (bf16[4,192,384]{2,1,0:T(8,128)(2,1)S(1)}, bf16[4,192,384]{2,1,0:T(8,128)(2,1)S(1)}, u32[]{:S(2)}, u32[]{:S(2)}) collective-permute-start(bf16[4,192,384]{2,1,0:T(8,128)(2,1)S(1)} %get-tuple-element.28), channel_id=1, source_target_pairs={{0,8},{1,9},{2,10},{3,11},{4,12},{5,13},{6,14},{7,15},{8,16},{9,17... | collective-permute-start | bytes 1769480 | tf_op jit(solution)/shard_map/ppermute | solution.py:334
  30.1 32.1 %copy-start.5 = (bf16[2,128,384]{2,1,0:T(8,128)(2,1)S(1)}, bf16[2,128,384]{2,1,0:T(8,128)(2,1)}, u32[]{:S(2)}) copy-start(bf16[2,128,384]{2,1,0:T(8,128)(2,1)} %get-tuple-element.23) | copy-start | bytes 589828
  30.1 38.6 %copy-start.1 = (f32[16,128]{1,0:T(8,128)S(1)}, f32[16,128]{1,0:T(8,128)}, u32[]{:S(2)}) copy-start(f32[16,128]{1,0:T(8,128)} %get-tuple-element.21.bias) | copy-start | bytes 24580
  30.1 28.1 %collective-permute-start.5 = (bf16[4,192,384]{2,1,0:T(8,128)(2,1)S(1)}, bf16[4,192,384]{2,1,0:T(8,128)(2,1)}, u32[]{:S(2)}, u32[]{:S(2)}) collective-permute-start(bf16[4,192,384]{2,1,0:T(8,128)(2,1)S(1)} %get-tuple-element.27), channel_id=1, source_target_pairs={{0,24},{1,25},{2,26},{3,27},{4,28},{5,29},{6,30},{7,31},{8,0},{9,1... | collective-permute-start | bytes 1769480 | tf_op jit(solution)/shard_map/ppermute | solution.py:334
  46.5 11.7 %copy-start.3 = (bf16[4,192,384]{2,1,0:T(8,128)(2,1)}, bf16[4,192,384]{2,1,0:T(8,128)(2,1)S(1)}, u32[]{:S(2)}) copy-start(bf16[4,192,384]{2,1,0:T(8,128)(2,1)S(1)} %collective-permute-done.4._.before_ref) | copy-start | bytes 1769476
  58.4 28.4 %collective-permute-start.6 = (bf16[4,192,384]{2,1,0:T(8,128)(2,1)S(1)}, bf16[4,192,384]{2,1,0:T(8,128)(2,1)S(1)}, u32[]{:S(2)}, u32[]{:S(2)}) collective-permute-start(bf16[4,192,384]{2,1,0:T(8,128)(2,1)S(1)} %get-tuple-element.19), channel_id=1, source_target_pairs={{0,8},{1,9},{2,10},{3,11},{4,12},{5,13},{6,14},{7,15},{8,16},{9,17... | collective-permute-start | bytes 1769480 | tf_op jit(solution)/shard_map/ppermute | solution.py:334
  59.5 27.6 %collective-permute-start.7 = (bf16[4,192,384]{2,1,0:T(8,128)(2,1)S(1)}, bf16[4,192,384]{2,1,0:T(8,128)(2,1)S(1)}, u32[]{:S(2)}, u32[]{:S(2)}) collective-permute-start(bf16[4,192,384]{2,1,0:T(8,128)(2,1)S(1)} %get-tuple-element.20), channel_id=1, source_target_pairs={{0,24},{1,25},{2,26},{3,27},{4,28},{5,29},{6,30},{7,31},{8,0},{9,1... | collective-permute-start | bytes 1769480 | tf_op jit(solution)/shard_map/ppermute | solution.py:334
  62.2 5.8 %collective-permute-start.8 = (bf16[2,128,384]{2,1,0:T(8,128)(2,1)S(1)}, bf16[2,128,384]{2,1,0:T(8,128)(2,1)S(1)}, u32[]{:S(2)}, u32[]{:S(2)}) collective-permute-start(bf16[2,128,384]{2,1,0:T(8,128)(2,1)S(1)} %copy-done.5), channel_id=1, source_target_pairs={{0,4},{1,5},{2,6},{3,7},{4,0},{5,1},{6,2},{7,3},{8,12},{9,13},{10,... | collective-permute-start | bytes 589832 | tf_op jit(solution)/shard_map/ppermute | solution.py:338
  68.0 0.7 copy-start.4

commit v5 on v4

--- a/solution.py
+++ b/solution.py
@@ -123,12 +123,16 @@
             done = []
 
 
-def far_kernel(before_ref, after_ref, near_ref, far_ref, scale_ref, out_ref):
-    side = pl.program_id(1)
-    values = jnp.where(side == 0, flat(before_ref[...]), flat(after_ref[...])).T
-    far = jnp.dot(values, far_ref[0, 0], preferred_element_type=jnp.float32)
-    out = near_ref[0, 0] + far * scale_ref[0, 0]
-    out_ref[...] = out.T.astype(out_ref.dtype).reshape(out_ref.shape)
+def far_kernel(place, before_ref, after_ref, near_ref, far_ref, scale_ref, *rest):
+    outs, held = rest[:-1], rest[-1]
+    half = len(outs) // 2
+    for side, ref in enumerate((before_ref, after_ref)):
+        far = jnp.dot(flat(ref[...]).T, far_ref[0, side], preferred_element_type=jnp.float32)
+        out = near_ref[0, side] + far * scale_ref[0, side]
+        out = out.T.astype(held.dtype)
+        held[side * half : (side + 1) * half] = out.reshape(half, *held.shape[1:])
+    for d, out_ref in enumerate(outs):
+        out_ref[...] = held[place[6] ^ d]
 
 
 def near_attention(tiles, bias, vq, k, k_before, k_after, keep, got, add):
@@ -165,25 +169,27 @@
     )(bias, vq, vq, k, k_before, k_after, keep, got, add)
 
 
-def far_attention(v_before, v_after, near, weights, scales):
+def far_attention(place, v_before, v_after, near, weights, scales):
     half, rows, part = v_before.shape
     heads, length = part // HD, half * rows
-    far = pl.BlockSpec((half, rows, HD), lambda h, s: (0, 0, h))
-    at = lambda h, s: (h, s, 0, 0)
+    far = pl.BlockSpec((half, rows, HD), lambda h: (0, 0, h))
+    at = lambda h: (h, 0, 0, 0)
     return pl.pallas_call(
         far_kernel,
-        grid=(heads, 2),
+        grid=(heads,),
         in_specs=[
+            SMEM,
             far,
             far,
-            pl.BlockSpec((1, 1, HD, length), at),
-            pl.BlockSpec((1, 1, length, length), at),
-            pl.BlockSpec((1, 1, 1, length), at),
-        ],
-        out_specs=pl.BlockSpec((half, rows, HD), lambda h, s: (s, 0, h)),
-        out_shape=jax.ShapeDtypeStruct((2 * half, rows, part), jnp.bfloat16),
+            pl.BlockSpec((1, 2, HD, length), at),
+            pl.BlockSpec((1, 2, length, length), at),
+            pl.BlockSpec((1, 2, 1, length), at),
+        ],
+        out_specs=[pl.BlockSpec((rows, HD), lambda h: (0, h))] * (2 * half),
+        out_shape=[jax.ShapeDtypeStruct((rows, part), jnp.bfloat16)] * (2 * half),
+        scratch_shapes=[pltpu.VMEM((2 * half, rows, HD), jnp.bfloat16)],
         compiler_params=LARGE,
-    )(v_before, v_after, near, weights, scales)
+    )(place, v_before, v_after, near, weights, scales)
 
 
 def split_kernel(order, count, *refs):
@@ -213,14 +219,13 @@
         write.wait()
 
 
-def join_kernel(order, *refs):
-    parts, out_ref = refs[:-1], refs[-1]
-    width = out_ref.shape[1] // len(order)
-    for p, g in enumerate(order):
-        at = g * width
-        for ref in parts:
-            out_ref[:, at : at + ref.shape[2]] = ref[p]
-            at += ref.shape[2]
+def join_kernel(heads, which, place, *refs):
+    out_ref = refs[-1]
+    for d, ref in zip(which, refs[:-1]):
+        part = ref.shape[1]
+        owner = place[6] ^ d
+        group_at = 2 * lax.rem(owner, heads) + lax.div(owner, heads)
+        out_ref[:, pl.ds(pl.multiple_of(group_at * part, part), part)] = ref[...]
 
 
 def split_heads(order, arrays):
@@ -241,14 +246,14 @@
     )(*(far_memory(x) for x in arrays))
 
 
-def join_heads(order, *parts):
-    ways, rows, _ = parts[0].shape
-    width = sum(x.shape[2] for x in parts)
+def join_heads(heads, place, which, parts):
+    rows, part = parts[0].shape
     return pl.pallas_call(
-        functools.partial(join_kernel, order),
-        out_shape=jax.ShapeDtypeStruct((rows, ways * width), jnp.bfloat16),
-        compiler_params=SMALL,
-    )(*parts)
+        functools.partial(join_kernel, heads, which),
+        in_specs=[SMEM] + [pl.BlockSpec()] * len(parts),
+        out_shape=jax.ShapeDtypeStruct((rows, len(parts) * part), jnp.bfloat16),
+        compiler_params=SMALL,
+    )(place, *parts)
 
 
 def mask_kernel(tiles, place, count, list_hbm, k_ref, v_ref, mask_ref, text_ref, list_ref, sems):
@@ -337,6 +342,9 @@
         flip = lambda i: i // ways * ways + (i + heads) % ways
         return lax.ppermute(x, AXES, [(i, flip(i)) for i in range(count)])
 
+    def crossed(x, by):
+        return lax.ppermute(x, AXES, [(i, i // ways * ways + (i % ways ^ by)) for i in range(count)])
+
     def exchange(x):
         return lax.all_to_all(
             x, AXES, split_axis=0, concat_axis=0, tiled=True, axis_index_groups=groups
@@ -345,7 +353,8 @@
     k = exchange(split_heads(order, (keys,)))
     ahead, behind = (slab + 1) % slabs, (slab + slabs - 1) % slabs
     toward, away = jnp.where(side == 0, ahead, behind), jnp.where(side == 0, behind, ahead)
-    place = jnp.stack([slab, toward, away, side, pair, text_len[0]]).astype(jnp.int32)
+    me = side * heads + lax.axis_index("head")
+    place = jnp.stack([slab, toward, away, side, pair, text_len[0], me]).astype(jnp.int32)
     text_rows = text_keys.shape[0]
     mask, text = pl.pallas_call(
         functools.partial(mask_kernel, tiles),
@@ -391,7 +400,9 @@
     )(vq, k_before, k_after)
     v_before, v_after = shifted(v_high, 1), shifted(v_low, -1)
     partial = near_attention(tiles, bias, vq, far_memory(k), k_before, k_after, keep, got, add)
-    return join_heads(order, exchange(far_attention(v_before, v_after, *partial)))
+    outs = far_attention(place, v_before, v_after, *partial)
+    sends = sorted(range(1, ways), key=lambda d: (d % 2, -(d // 2).bit_count(), d))
+    return join_heads(heads, place, [0] + sends, [outs[0]] + [crossed(outs[d], d) for d in sends])
 
 
 def solution(mesh):

time: 112 us -> 108 us (0.964)
  blocking collectives: 20.2 us -> 0 us
  waiting for transfers between devices: 33.7 us -> 41.6 us
  starting transfers between devices: 25.8 us -> 33.6 us
    all_to_all x1 -> x0, blocking collectives: 20.2 us -> none  [exchange(): lax.all_to_all(x, AXES, split_axis=0, concat_axis=0, tiled=True, axis_ind...]
    ppermute x0 -> x7, waiting for transfers between devices: none -> 7.89 us  [crossed(): lax.ppermute(x, AXES, [(i, i // ways * ways + (i % ways ^ by)) for i in r...]
    ppermute x0 -> x7, starting transfers between devices: none -> 7.79 us  [crossed(): lax.ppermute(x, AXES, [(i, i // ways * ways + (i % ways ^ by)) for i in r...]
  transfers between devices with their start and end apart: 11 -> 18, of which waited for: 5 -> 11; matrix products, arithmetic and copies ran while one was open for 0% -> 0% of each run, Pallas kernels for 21% -> 22%
where the time goes in v5:
time: 108 us; the launch traced here: 107 us
  waiting for transfers between devices  41.6 us (39%)
  starting transfers between devices  33.6 us (31%)
  Pallas kernels  30.4 us (28%)
    ppermute x7, waiting for transfers between devices, shifted(): lax.ppermute(x, AXES, [(i, (i + by * ways) % count) for i in range(count)])  26.2 us
    pallas_call x1, Pallas kernels, near_attention(): pl.pallas_call(functools.partial(near_kernel, tiles, CHUNK if tiles % CHU...  18.1 us
    ppermute x7, starting transfers between devices, shifted(): lax.ppermute(x, AXES, [(i, (i + by * ways) % count) for i in range(count)])  13.3 us
    all_to_all x2, starting transfers between devices, exchange(): lax.all_to_all(x, AXES, split_axis=0, concat_axis=0, tiled=True, axis_ind...  8.8 us
    ppermute x7, waiting for transfers between devices, crossed(): lax.ppermute(x, AXES, [(i, i // ways * ways + (i % ways ^ by)) for i in r...  7.89 us
    ppermute x7, starting transfers between devices, crossed(): lax.ppermute(x, AXES, [(i, i // ways * ways + (i % ways ^ by)) for i in r...  7.79 us
    ppermute x2, waiting for transfers between devices, swapped(): return lax.ppermute(x, AXES, [(i, flip(i)) for i in range(count)])  7.52 us
    pallas_call x2, Pallas kernels, split_heads(): pl.pallas_call(functools.partial(split_kernel, order, count), in_specs=[A...  4.84 us
  transfers between devices with their start and end apart: 18, of which 11 were waited for; matrix products, arithmetic and copies ran while one was open for 0% of the time, Pallas kernels for 22%

profile of v5, /device:TPU:0, one launch (start us, length us, event | category | flops | bytes accessed | tf_op | source)
XLA Modules:
  0.0 107.3 jit_solution(7709348026217956972)
XLA Ops:
  0.0 2.2 %shard_map.83 = bf16[8,192,384]{2,1,0:T(8,128)(2,1)} custom-call(bf16[192,3072]{1,0:T(8,128)(2,1)} %refs_0_.3), custom_call_target="tpu_custom_call" | custom-call | tf_op jit(solution)/shard_map/pallas_call | solution.py:235
  2.2 0.0 copy-start.2
  2.2 5.2 %all-to-all-start = ((bf16[8,192,384]{2,1,0:T(8,128)(2,1)}), bf16[8,192,384]{2,1,0:T(8,128)(2,1)S(1)}, u32[]{:S(2)}, u32[]{:S(2)}) async-start(bf16[8,192,384]{2,1,0:T(8,128)(2,1)} %shard_map.83), calls=%async_computation | async-start | bytes 2359296 | tf_op jit(solution)/shard_map/all_to_all | solution.py:349
  8.0 0.1 stack.27.place
  8.1 0.0 copy-done.2
  8.1 1.5 %shard_map.84 = (bf16[16,128]{1,0:T(8,128)(2,1)S(1)}, bf16[2,32,768]{2,1,0:T(8,128)(2,1)S(1)}) custom-call(s32[7]{0:T(128)S(1)} %stack.27.place, s32[6]{0:T(128)S(1)} %copy-done.2, s32[6,12]{1,0:T(8,128)} %list_hbm.1, bf16[32,768]{1,0:T(8,128)(2,1)} %k_ref.1, bf16[32,768]{1,0:T(8,128)(2,1)} %v_ref.1), custom_call_target="tpu_custom_call" | custom-call | tf_op jit(solution)/shard_map/pallas_call | solution.py:359
  9.6 1.6 %collective-permute-start.1 = (bf16[2,32,768]{2,1,0:T(8,128)(2,1)S(1)}, bf16[2,32,768]{2,1,0:T(8,128)(2,1)S(1)}, u32[]{:S(2)}, u32[]{:S(2)}) collective-permute-start(bf16[2,32,768]{2,1,0:T(8,128)(2,1)S(1)} %get-tuple-element.25.refs_0_), channel_id=1, source_target_pairs={{0,8},{1,9},{2,10},{3,11},{4,12},{5,13},{6,14},{7,15},{8,16},{9,17... | collective-permute-start | bytes 294920 | tf_op jit(solution)/shard_map/ppermute | solution.py:339
  11.2 2.6 %collective-permute-start.2 = (bf16[2,32,768]{2,1,0:T(8,128)(2,1)S(1)}, bf16[2,32,768]{2,1,0:T(8,128)(2,1)S(1)}, u32[]{:S(2)}, u32[]{:S(2)}) collective-permute-start(bf16[2,32,768]{2,1,0:T(8,128)(2,1)S(1)} %get-tuple-element.25.refs_0_), channel_id=1, source_target_pairs={{0,16},{1,17},{2,18},{3,19},{4,20},{5,21},{6,22},{7,23},{8,24},{9,... | collective-permute-start | bytes 294920 | tf_op jit(solution)/shard_map/ppermute | solution.py:339
  13.8 1.3 %collective-permute-start.3 = (bf16[2,32,768]{2,1,0:T(8,128)(2,1)S(1)}, bf16[2,32,768]{2,1,0:T(8,128)(2,1)S(1)}, u32[]{:S(2)}, u32[]{:S(2)}) collective-permute-start(bf16[2,32,768]{2,1,0:T(8,128)(2,1)S(1)} %get-tuple-element.25.refs_0_), channel_id=1, source_target_pairs={{0,24},{1,25},{2,26},{3,27},{4,28},{5,29},{6,30},{7,31},{8,0},{9,1... | collective-permute-start | bytes 294920 | tf_op jit(solution)/shard_map/ppermute | solution.py:339
  15.2 2.0 %collective-permute-start = (bf16[16,128]{1,0:T(8,128)(2,1)S(1)}, bf16[16,128]{1,0:T(8,128)(2,1)S(1)}, u32[]{:S(2)}, u32[]{:S(2)}) collective-permute-start(bf16[16,128]{1,0:T(8,128)(2,1)S(1)} %get-tuple-element.24.mask_ref), channel_id=1, source_target_pairs={{0,4},{1,5},{2,6},{3,7},{4,0},{5,1},{6,2},{7,3},{8,12},{9,13},{10,... | collective-permute-start | bytes 12296 | tf_op jit(solution)/shard_map/ppermute | solution.py:343
  17.2 2.7 %shard_map.82.__0_ = bf16[8,2,192,384]{3,2,1,0:T(8,128)(2,1)} custom-call(bf16[192,3072]{1,0:T(8,128)(2,1)} %refs_0_.2, bf16[192,3072]{1,0:T(8,128)(2,1)} %refs_1_.1), custom_call_target="tpu_custom_call" | custom-call | tf_op jit(solution)/shard_map/pallas_call | solution.py:235
  19.9 3.4 %collective-permute-done.their_ref = bf16[16,128]{1,0:T(8,128)(2,1)S(1)} collective-permute-done((bf16[16,128]{1,0:T(8,128)(2,1)S(1)}, bf16[16,128]{1,0:T(8,128)(2,1)S(1)}, u32[]{:S(2)}, u32[]{:S(2)}) %collective-permute-start) | collective-permute-done | bytes 4128 | tf_op jit(solution)/shard_map/ppermute | solution.py:343
  23.3 0.0 collective-permute-done.1.refs_1_
  23.3 0.0 collective-permute-done.2.refs_2_
  23.3 0.0 collective-permute-done.3.refs_3_
  23.3 1.4 %shard_map.85 = (bf16[2,128,384]{2,1,0:T(8,128)(2,1)}, bf16[2,128,384]{2,1,0:T(8,128)(2,1)}, f32[16,128]{1,0:T(8,128)}, f32[256,128]{1,0:T(8,128)}) custom-call(s32[7]{0:T(128)S(1)} %stack.27.place, bf16[16,128]{1,0:T(8,128)(2,1)S(1)} %get-tuple-element.24.mask_ref, bf16[16,128]{1,0:T(8,128)(2,1)S(1)} %collective-permute-done.their_ref, ...), custom_call_target="tpu_custom_call" | custom-call | tf_op jit(solution)/shard_map/pallas_call | solution.py:379
  24.7 0.0 all-to-all-done.__1_.k_ref
  24.7 0.0 copy-start
  24.7 3.6 %all-to-all-start.1 = ((bf16[8,2,192,384]{3,2,1,0:T(8,128)(2,1)}), bf16[8,2,192,384]{3,2,1,0:T(8,128)(2,1)S(1)}, u32[]{:S(2)}, u32[]{:S(2)}) async-start(bf16[8,2,192,384]{3,2,1,0:T(8,128)(2,1)} %shard_map.86), calls=%async_computation.1 | async-start | bytes 4718592 | tf_op jit(solution)/shard_map/all_to_all | solution.py:349
  28.3 0.0 copy-done
  28.4 0.1 fusion
  28.5 1.6 %collective-permute-start.4 = (bf16[4,192,384]{2,1,0:T(8,128)(2,1)S(1)}, bf16[4,192,384]{2,1,0:T(8,128)(2,1)S(1)}, u32[]{:S(2)}, u32[]{:S(2)}) collective-permute-start(bf16[4,192,384]{2,1,0:T(8,128)(2,1)S(1)} %get-tuple-element.44), channel_id=1, source_target_pairs={{0,8},{1,9},{2,10},{3,11},{4,12},{5,13},{6,14},{7,15},{8,16},{9,17... | collective-permute-start | bytes 1769480 | tf_op jit(solution)/shard_map/ppermute | solution.py:339
  30.1 0.0 copy-start.5
  30.1 0.0 copy-start.1
  30.1 2.2 %collective-permute-start.5 = (bf16[4,192,384]{2,1,0:T(8,128)(2,1)S(1)}, bf16[4,192,384]{2,1,0:T(8,128)(2,1)}, u32[]{:S(2)}, u32[]{:S(2)}) collective-permute-start(bf16[4,192,384]{2,1,0:T(8,128)(2,1)S(1)} %get-tuple-element.43), channel_id=1, source_target_pairs={{0,24},{1,25},{2,26},{3,27},{4,28},{5,29},{6,30},{7,31},{8,0},{9,1... | collective-permute-start | bytes 1769480 | tf_op jit(solution)/shard_map/ppermute | solution.py:339
  32.4 14.1 %collective-permute-done.4._.before_ref = bf16[4,192,384]{2,1,0:T(8,128)(2,1)S(1)} collective-permute-done((bf16[4,192,384]{2,1,0:T(8,128)(2,1)S(1)}, bf16[4,192,384]{2,1,0:T(8,128)(2,1)S(1)}, u32[]{:S(2)}, u32[]{:S(2)}) %collective-permute-start.4) | collective-permute-done | bytes 589856 | tf_op jit(solution)/shard_map/ppermute | solution.py:339
  46.5 0.0 copy-start.3
  46.5 11.7 %collective-permute-done.5.__.after_ref = bf16[4,192,384]{2,1,0:T(8,128)(2,1)} collective-permute-done((bf16[4,192,384]{2,1,0:T(8,128)(2,1)S(1)}, bf16[4,192,384]{2,1,0:T(8,128)(2,1)}, u32[]{:S(2)}, u32[]{:S(2)}) %collective-permute-start.5) | collective-permute-done | bytes 589856 | tf_op jit(solution)/shard_map/ppermute | solution.py:339
  58.2 0.0 copy-done.3
  58.2 0.0 all-to-all-done.1.vq_ref.q_ref.v_ref
  58.3 0.1 shard_map.87
  58.4 1.1 %collective-permute-start.6 = (bf16[4,192,384]{2,1,0:T(8,128)(2,1)S(1)}, bf16[4,192,384]{2,1,0:T(8,128)(2,1)S(1)}, u32[]{:S(2)}, u32[]{:S(2)}) collective-permute-start(bf16[4,192,384]{2,1,0:T(8,128)(2,1)S(1)} %get-tuple-element.27), channel_id=1, source_target_pairs={{0,8},{1,9},{2,10},{3,11},{4,12},{5,13},{6,14},{7,15},{8,16},{9,17... | collective-permute-start | bytes 1769480 | tf_op jit(solution)/shard_map/ppermute | solution.py:339
  59.5 2.7 %collective-permute-start.7 = (bf16[4,192,384]{2,1,0:T(8,128)(2,1)S(1)}, bf16[4,192,384]{2,1,0:T(8,128)(2,1)S(1)}, u32[]{:S(2)}, u32[]{:S(2)}) collective-permute-start(bf16[4,192,384]{2,1,0:T(8,128)(2,1)S(1)} %get-tuple-element.28), channel_id=1, source_target_pairs={{0,24},{1,25},{2,26},{3,27},{4,28},{5,29},{6,30},{7,31},{8,0},{9,1... | collective-permute-start | bytes 1769480 | tf_op jit(solution)/shard_map/ppermute | solution.py:339
  62.2 0.0 copy-done.5
  62.2 1.7 %collective-permute-start.8 = (bf16[2,128,384]{2,1,0:T(8,128)(2,1)S(1)}, bf16[2,128,384]{2,1,0:T(8,128)(2,1)S(1)}, u32[]{:S(2)}, u32[]{:S(2)}) collective-permute-start(bf16[2,128,384]{2,1,0:T(8,128)(2,1)S(1)} %copy-done.5), channel_id=1, source_target_pairs={{0,4},{1,5},{2,6},{3,7},{4,0},{5,1},{6,2},{7,3},{8,12},{9,13},{10,... | collective-permute-start | bytes 589832 | tf_op jit(solution)/shard_map/ppermute | solution.py:343
  63.9 4.1 %collective-permute-done.8.got_ref = bf16[2,128,384]{2,1,0:T(8,128)(2,1)S(1)} collective-permute-done((bf16[2,128,384]{2,1,0:T(8,128)(2,1)S(1)}, bf16[2,128,384]{2,1,0:T(8,128)(2,1)S(1)}, u32[]{:S(2)}, u32[]{:S(2)}) %collective-permute-start.8) | collective-permute-done | bytes 196640 | tf_op jit(solution)/shard_map/ppermute | solution.py:343
  68.0 0.0 copy-start.4
  68.0 0.7 copy-done.4
  68.7 0.0 copy-done.1
  68.7 18.1 %shard_map.88 = (f32[3,2,128,768]{3,2,1,0:T(8,128)S(1)}, bf16[3,2,768,768]{3,2,1,0:T(8,128)(2,1)S(1)}, f32[3,2,1,768]{3,2,1,0:T(1,128)S(1)}) custom-call(f32[16,128]{1,0:T(8,128)S(1)} %copy-done.1, bf16[8,2,192,384]{3,2,1,0:T(8,128)(2,1)S(1)} %all-to-all-done.1.vq_ref.q_ref.v_ref, bf16[8,2,192,384]{3,2,1,0:T(8,128)(2,1)S(1)} %all-to-all-done.1.vq_ref.q_ref.v_ref, ...), custom_call_target="tpu_custom_call" | custom-call | tf_op jit(solution)/shard_map/pallas_call | solution.py:144
  86.8 0.0 collective-permute-done.6.before_ref
  86.8 0.3 collective-permute-done.7.after_ref
  87.1 2.8 %shard_map.89 = (bf16[192,384]{1,0:T(8,128)(2,1)S(1)}, bf16[192,384]{1,0:T(8,128)(2,1)S(1)}, bf16[192,384]{1,0:T(8,128)(2,1)S(1)}, bf16[192,384]{1,0:T(8,128)(2,...) custom-call(s32[7]{0:T(128)S(1)} %stack.27.place, ...), custom_call_target="tpu_custom_call" | custom-call | tf_op jit(solution)/shard_map/pallas_call | solution.py:177
  89.9 1.7 %collective-permute-start.10 = (bf16[192,384]{1,0:T(8,128)(2,1)S(1)}, bf16[192,384]{1,0:T(8,128)(2,1)S(1)}, u32[]{:S(2)}, u32[]{:S(2)}) collective-permute-start(bf16[192,384]{1,0:T(8,128)(2,1)S(1)} %get-tuple-element.37), channel_id=1, source_target_pairs={{0,2},{1,3},{2,0},{3,1},{4,6},{5,7},{6,4},{7,5},{8,10},{9,11},{10,... | collective-permute-start | bytes 442376 | tf_op jit(solution)/shard_map/ppermute | solution.py:346
  91.7 1.5 %collective-permute-start.11 = (bf16[192,384]{1,0:T(8,128)(2,1)S(1)}, bf16[192,384]{1,0:T(8,128)(2,1)S(1)}, u32[]{:S(2)}, u32[]{:S(2)}) collective-permute-start(bf16[192,384]{1,0:T(8,128)(2,1)S(1)} %get-tuple-element.38), channel_id=1, source_target_pairs={{0,4},{1,5},{2,6},{3,7},{4,0},{5,1},{6,2},{7,3},{8,12},{9,13},{10,... | collective-permute-start | bytes 442376 | tf_op jit(solution)/shard_map/ppermute | solution.py:346
  93.2 0.0 collective-permute-start.12
  93.2 1.7 %collective-permute-start.13 = (bf16[192,384]{1,0:T(8,128)(2,1)S(1)}, bf16[192,384]{1,0:T(8,128)(2,1)S(1)}, u32[]{:S(2)}, u32[]{:S(2)}) collective-permute-start(bf16[192,384]{1,0:T(8,128)(2,1)S(1)} %get-tuple-element.40), channel_id=1, source_target_pairs={{0,3},{1,2},{2,1},{3,0},{4,7},{5,6},{6,5},{7,4},{8,11},{9,10},{10,... | collective-permute-start | bytes 442376 | tf_op jit(solution)/shard_map/ppermute | solution.py:346
  94.9 0.1 collective-permute-start.14
  95.0 0.3 collective-permute-done.10.refs_2_
  95.2 1.3 %collective-permute-start.15 = (bf16[192,384]{1,0:T(8,128)(2,1)S(1)}, bf16[192,384]{1,0:T(8,128)(2,1)S(1)}, u32[]{:S(2)}, u32[]{:S(2)}) collective-permute-start(bf16[192,384]{1,0:T(8,128)(2,1)S(1)} %get-tuple-element.42), channel_id=1, source_target_pairs={{0,1},{1,0},{2,3},{3,2},{4,5},{5,4},{6,7},{7,6},{8,9},{9,8},{10,11... | collective-permute-start | bytes 442376 | tf_op jit(solution)/shard_map/ppermute | solution.py:346
  96.5 1.0 collective-permute-done.11.refs_3_
  97.5 1.5 %collective-permute-start.9 = (bf16[192,384]{1,0:T(8,128)(2,1)S(1)}, bf16[192,384]{1,0:T(8,128)(2,1)S(1)}, u32[]{:S(2)}, u32[]{:S(2)}) collective-permute-start(bf16[192,384]{1,0:T(8,128)(2,1)S(1)} %get-tuple-element.36), channel_id=1, source_target_pairs={{0,6},{1,7},{2,4},{3,5},{4,2},{5,3},{6,0},{7,1},{8,14},{9,15},{10,... | collective-permute-start | bytes 442376 | tf_op jit(solution)/shard_map/ppermute | solution.py:346
  99.0 1.6 %collective-permute-done.12.refs_4_ = bf16[192,384]{1,0:T(8,128)(2,1)S(1)} collective-permute-done((bf16[192,384]{1,0:T(8,128)(2,1)S(1)}, bf16[192,384]{1,0:T(8,128)(2,1)S(1)}, u32[]{:S(2)}, u32[]{:S(2)}) %collective-permute-start.12) | collective-permute-done | bytes 147488 | tf_op jit(solution)/shard_map/ppermute | solution.py:346
  100.6 1.3 %collective-permute-done.13.refs_5_ = bf16[192,384]{1,0:T(8,128)(2,1)S(1)} collective-permute-done((bf16[192,384]{1,0:T(8,128)(2,1)S(1)}, bf16[192,384]{1,0:T(8,128)(2,1)S(1)}, u32[]{:S(2)}, u32[]{:S(2)}) %collective-permute-start.13) | collective-permute-done | bytes 147488 | tf_op jit(solution)/shard_map/ppermute | solution.py:346
  102.0 1.6 %collective-permute-done.14.refs_6_ = bf16[192,384]{1,0:T(8,128)(2,1)S(1)} collective-permute-done((bf16[192,384]{1,0:T(8,128)(2,1)S(1)}, bf16[192,384]{1,0:T(8,128)(2,1)S(1)}, u32[]{:S(2)}, u32[]{:S(2)}) %collective-permute-start.14) | collective-permute-done | bytes 147488 | tf_op jit(solution)/shard_map/ppermute | solution.py:346
  103.6 0.0 collective-permute-done.15.refs_7_
  103.6 2.0 %collective-permute-done.9.refs_1_ = bf16[192,384]{1,0:T(8,128)(2,1)S(1)} collective-permute-done((bf16[192,384]{1,0:T(8,128)(2,1)S(1)}, bf16[192,384]{1,0:T(8,128)(2,1)S(1)}, u32[]{:S(2)}, u32[]{:S(2)}) %collective-permute-start.9) | collective-permute-done | bytes 147488 | tf_op jit(solution)/shard_map/ppermute | solution.py:346
  105.6 1.7 %shard_map.90 = bf16[192,3072]{1,0:T(8,128)(2,1)} custom-call(s32[7]{0:T(128)S(1)} %stack.27.place, bf16[192,384]{1,0:T(8,128)(2,1)S(1)} %get-tuple-element.35.refs_0_, bf16[192,384]{1,0:T(8,128)(2,1)S(1)} %collective-permute-done.9.refs_1_, bf16[192,384]{1,0:T(8,128)(2,1)S(1)} %collective-permute-done.10.refs_2_, ...), custom_call_target="tpu_custom_call" | custom-call | tf_op jit(solution)/shard_map/pallas_call | solution.py:251
  (1 shorter events, 0.0 us)
Async XLA Ops:
  2.2 5.9 %copy-start.2 = (s32[6]{0:T(128)S(1)}, s32[6]{0:T(128)}, u32[]{:S(2)}) copy-start(s32[6]{0:T(128)} %count.1) | copy-start | bytes 76
  2.2 22.5 %all-to-all-start = ((bf16[8,192,384]{2,1,0:T(8,128)(2,1)}), bf16[8,192,384]{2,1,0:T(8,128)(2,1)S(1)}, u32[]{:S(2)}, u32[]{:S(2)}) async-start(bf16[8,192,384]{2,1,0:T(8,128)(2,1)} %shard_map.83), calls=%async_computation | async-start | bytes 2359296 | tf_op jit(solution)/shard_map/all_to_all | solution.py:349
  9.6 13.7 %collective-permute-start.1 = (bf16[2,32,768]{2,1,0:T(8,128)(2,1)S(1)}, bf16[2,32,768]{2,1,0:T(8,128)(2,1)S(1)}, u32[]{:S(2)}, u32[]{:S(2)}) collective-permute-start(bf16[2,32,768]{2,1,0:T(8,128)(2,1)S(1)} %get-tuple-element.25.refs_0_), channel_id=1, source_target_pairs={{0,8},{1,9},{2,10},{3,11},{4,12},{5,13},{6,14},{7,15},{8,16},{9,17... | collective-permute-start | bytes 294920 | tf_op jit(solution)/shard_map/ppermute | solution.py:339
  11.2 12.1 %collective-permute-start.2 = (bf16[2,32,768]{2,1,0:T(8,128)(2,1)S(1)}, bf16[2,32,768]{2,1,0:T(8,128)(2,1)S(1)}, u32[]{:S(2)}, u32[]{:S(2)}) collective-permute-start(bf16[2,32,768]{2,1,0:T(8,128)(2,1)S(1)} %get-tuple-element.25.refs_0_), channel_id=1, source_target_pairs={{0,16},{1,17},{2,18},{3,19},{4,20},{5,21},{6,22},{7,23},{8,24},{9,... | collective-permute-start | bytes 294920 | tf_op jit(solution)/shard_map/ppermute | solution.py:339
  13.8 9.5 %collective-permute-start.3 = (bf16[2,32,768]{2,1,0:T(8,128)(2,1)S(1)}, bf16[2,32,768]{2,1,0:T(8,128)(2,1)S(1)}, u32[]{:S(2)}, u32[]{:S(2)}) collective-permute-start(bf16[2,32,768]{2,1,0:T(8,128)(2,1)S(1)} %get-tuple-element.25.refs_0_), channel_id=1, source_target_pairs={{0,24},{1,25},{2,26},{3,27},{4,28},{5,29},{6,30},{7,31},{8,0},{9,1... | collective-permute-start | bytes 294920 | tf_op jit(solution)/shard_map/ppermute | solution.py:339
  15.2 8.1 %collective-permute-start = (bf16[16,128]{1,0:T(8,128)(2,1)S(1)}, bf16[16,128]{1,0:T(8,128)(2,1)S(1)}, u32[]{:S(2)}, u32[]{:S(2)}) collective-permute-start(bf16[16,128]{1,0:T(8,128)(2,1)S(1)} %get-tuple-element.24.mask_ref), channel_id=1, source_target_pairs={{0,4},{1,5},{2,6},{3,7},{4,0},{5,1},{6,2},{7,3},{8,12},{9,13},{10,... | collective-permute-start | bytes 12296 | tf_op jit(solution)/shard_map/ppermute | solution.py:343
  24.7 3.6 %copy-start = (bf16[8,192,384]{2,1,0:T(8,128)(2,1)}, bf16[8,192,384]{2,1,0:T(8,128)(2,1)S(1)}, u32[]{:S(2)}) copy-start(bf16[8,192,384]{2,1,0:T(8,128)(2,1)S(1)} %all-to-all-done.__1_.k_ref) | copy-start | bytes 3538948
  24.7 33.5 %all-to-all-start.1 = ((bf16[8,2,192,384]{3,2,1,0:T(8,128)(2,1)}), bf16[8,2,192,384]{3,2,1,0:T(8,128)(2,1)S(1)}, u32[]{:S(2)}, u32[]{:S(2)}) async-start(bf16[8,2,192,384]{3,2,1,0:T(8,128)(2,1)} %shard_map.86), calls=%async_computation.1 | async-start | bytes 4718592 | tf_op jit(solution)/shard_map/all_to_all | solution.py:349
  28.5 18.0 %collective-permute-start.4 = (bf16[4,192,384]{2,1,0:T(8,128)(2,1)S(1)}, bf16[4,192,384]{2,1,0:T(8,128)(2,1)S(1)}, u32[]{:S(2)}, u32[]{:S(2)}) collective-permute-start(bf16[4,192,384]{2,1,0:T(8,128)(2,1)S(1)} %get-tuple-element.44), channel_id=1, source_target_pairs={{0,8},{1,9},{2,10},{3,11},{4,12},{5,13},{6,14},{7,15},{8,16},{9,17... | collective-permute-start | bytes 1769480 | tf_op jit(solution)/shard_map/ppermute | solution.py:339
  30.1 32.1 %copy-start.5 = (bf16[2,128,384]{2,1,0:T(8,128)(2,1)S(1)}, bf16[2,128,384]{2,1,0:T(8,128)(2,1)}, u32[]{:S(2)}) copy-start(bf16[2,128,384]{2,1,0:T(8,128)(2,1)} %get-tuple-element.31) | copy-start | bytes 589828
  30.1 38.6 %copy-start.1 = (f32[16,128]{1,0:T(8,128)S(1)}, f32[16,128]{1,0:T(8,128)}, u32[]{:S(2)}) copy-start(f32[16,128]{1,0:T(8,128)} %get-tuple-element.29.bias) | copy-start | bytes 24580
  30.1 28.1 %collective-permute-start.5 = (bf16[4,192,384]{2,1,0:T(8,128)(2,1)S(1)}, bf16[4,192,384]{2,1,0:T(8,128)(2,1)}, u32[]{:S(2)}, u32[]{:S(2)}) collective-permute-start(bf16[4,192,384]{2,1,0:T(8,128)(2,1)S(1)} %get-tuple-element.43), channel_id=1, source_target_pairs={{0,24},{1,25},{2,26},{3,27},{4,28},{5,29},{6,30},{7,31},{8,0},{9,1... | collective-permute-start | bytes 1769480 | tf_op jit(solution)/shard_map/ppermute | solution.py:339
  46.5 11.7 %copy-start.3 = (bf16[4,192,384]{2,1,0:T(8,128)(2,1)}, bf16[4,192,384]{2,1,0:T(8,128)(2,1)S(1)}, u32[]{:S(2)}) copy-start(bf16[4,192,384]{2,1,0:T(8,128)(2,1)S(1)} %collective-permute-done.4._.before_ref) | copy-start | bytes 1769476
  58.4 28.4 %collective-permute-start.6 = (bf16[4,192,384]{2,1,0:T(8,128)(2,1)S(1)}, bf16[4,192,384]{2,1,0:T(8,128)(2,1)S(1)}, u32[]{:S(2)}, u32[]{:S(2)}) collective-permute-start(bf16[4,192,384]{2,1,0:T(8,128)(2,1)S(1)} %get-tuple-element.27), channel_id=1, source_target_pairs={{0,8},{1,9},{2,10},{3,11},{4,12},{5,13},{6,14},{7,15},{8,16},{9,17... | collective-permute-start | bytes 1769480 | tf_op jit(solution)/shard_map/ppermute | solution.py:339
  59.5 27.6 %collective-permute-start.7 = (bf16[4,192,384]{2,1,0:T(8,128)(2,1)S(1)}, bf16[4,192,384]{2,1,0:T(8,128)(2,1)S(1)}, u32[]{:S(2)}, u32[]{:S(2)}) collective-permute-start(bf16[4,192,384]{2,1,0:T(8,128)(2,1)S(1)} %get-tuple-element.28), channel_id=1, source_target_pairs={{0,24},{1,25},{2,26},{3,27},{4,28},{5,29},{6,30},{7,31},{8,0},{9,1... | collective-permute-start | bytes 1769480 | tf_op jit(solution)/shard_map/ppermute | solution.py:339
  62.2 5.8 %collective-permute-start.8 = (bf16[2,128,384]{2,1,0:T(8,128)(2,1)S(1)}, bf16[2,128,384]{2,1,0:T(8,128)(2,1)S(1)}, u32[]{:S(2)}, u32[]{:S(2)}) collective-permute-start(bf16[2,128,384]{2,1,0:T(8,128)(2,1)S(1)} %copy-done.5), channel_id=1, source_target_pairs={{0,4},{1,5},{2,6},{3,7},{4,0},{5,1},{6,2},{7,3},{8,12},{9,13},{10,... | collective-permute-start | bytes 589832 | tf_op jit(solution)/shard_map/ppermute | solution.py:343
  68.0 0.7 copy-start.4
  89.9 5.3 %collective-permute-start.10 = (bf16[192,384]{1,0:T(8,128)(2,1)S(1)}, bf16[192,384]{1,0:T(8,128)(2,1)S(1)}, u32[]{:S(2)}, u32[]{:S(2)}) collective-permute-start(bf16[192,384]{1,0:T(8,128)(2,1)S(1)} %get-tuple-element.37), channel_id=1, source_target_pairs={{0,2},{1,3},{2,0},{3,1},{4,6},{5,7},{6,4},{7,5},{8,10},{9,11},{10,... | collective-permute-start | bytes 442376 | tf_op jit(solution)/shard_map/ppermute | solution.py:346
  91.7 5.8 %collective-permute-start.11 = (bf16[192,384]{1,0:T(8,128)(2,1)S(1)}, bf16[192,384]{1,0:T(8,128)(2,1)S(1)}, u32[]{:S(2)}, u32[]{:S(2)}) collective-permute-start(bf16[192,384]{1,0:T(8,128)(2,1)S(1)} %get-tuple-element.38), channel_id=1, source_target_pairs={{0,4},{1,5},{2,6},{3,7},{4,0},{5,1},{6,2},{7,3},{8,12},{9,13},{10,... | collective-permute-start | bytes 442376 | tf_op jit(solution)/shard_map/ppermute | solution.py:346
  93.2 7.5 %collective-permute-start.12 = (bf16[192,384]{1,0:T(8,128)(2,1)S(1)}, bf16[192,384]{1,0:T(8,128)(2,1)S(1)}, u32[]{:S(2)}, u32[]{:S(2)}) collective-permute-start(bf16[192,384]{1,0:T(8,128)(2,1)S(1)} %get-tuple-element.39), channel_id=1, source_target_pairs={{0,7},{1,6},{2,5},{3,4},{4,3},{5,2},{6,1},{7,0},{8,15},{9,14},{10,... | collective-permute-start | bytes 442376 | tf_op jit(solution)/shard_map/ppermute | solution.py:346
  93.2 8.8 %collective-permute-start.13 = (bf16[192,384]{1,0:T(8,128)(2,1)S(1)}, bf16[192,384]{1,0:T(8,128)(2,1)S(1)}, u32[]{:S(2)}, u32[]{:S(2)}) collective-permute-start(bf16[192,384]{1,0:T(8,128)(2,1)S(1)} %get-tuple-element.40), channel_id=1, source_target_pairs={{0,3},{1,2},{2,1},{3,0},{4,7},{5,6},{6,5},{7,4},{8,11},{9,10},{10,... | collective-permute-start | bytes 442376 | tf_op jit(solution)/shard_map/ppermute | solution.py:346
  94.9 8.7 %collective-permute-start.14 = (bf16[192,384]{1,0:T(8,128)(2,1)S(1)}, bf16[192,384]{1,0:T(8,128)(2,1)S(1)}, u32[]{:S(2)}, u32[]{:S(2)}) collective-permute-start(bf16[192,384]{1,0:T(8,128)(2,1)S(1)} %get-tuple-element.41), channel_id=1, source_target_pairs={{0,5},{1,4},{2,7},{3,6},{4,1},{5,0},{6,3},{7,2},{8,13},{9,12},{10,... | collective-permute-start | bytes 442376 | tf_op jit(solution)/shard_map/ppermute | solution.py:346
  95.2 8.4 %collective-permute-start.15 = (bf16[192,384]{1,0:T(8,128)(2,1)S(1)}, bf16[192,384]{1,0:T(8,128)(2,1)S(1)}, u32[]{:S(2)}, u32[]{:S(2)}) collective-permute-start(bf16[192,384]{1,0:T(8,128)(2,1)S(1)} %get-tuple-element.42), channel_id=1, source_target_pairs={{0,1},{1,0},{2,3},{3,2},{4,5},{5,4},{6,7},{7,6},{8,9},{9,8},{10,11... | collective-permute-start | bytes 442376 | tf_op jit(solution)/shard_map/ppermute | solution.py:346
  97.5 8.1 %collective-permute-start.9 = (bf16[192,384]{1,0:T(8,128)(2,1)S(1)}, bf16[192,384]{1,0:T(8,128)(2,1)S(1)}, u32[]{:S(2)}, u32[]{:S(2)}) collective-permute-start(bf16[192,384]{1,0:T(8,128)(2,1)S(1)} %get-tuple-element.36), channel_id=1, source_target_pairs={{0,6},{1,7},{2,4},{3,5},{4,2},{5,3},{6,0},{7,1},{8,14},{9,15},{10,... | collective-permute-start | bytes 442376 | tf_op jit(solution)/shard_map/ppermute | solution.py:346

commit v6 on v5

--- a/solution.py
+++ b/solution.py
@@ -302,7 +302,7 @@
     add_ref[...] = jnp.where(token < place[5], 0.0, LOW)
 
 
-def halves_kernel(vq_ref, _, __, low_ref, high_ref):
+def halves_kernel(vq_ref, _, low_ref, high_ref):
     half = low_ref.shape[0]
     low_ref[...] = vq_ref[:half, 0]
     high_ref[...] = vq_ref[half:, 0]
@@ -394,10 +394,10 @@
 
     v_low, v_high = pl.pallas_call(
         halves_kernel,
-        in_specs=[pl.BlockSpec()] + [ANY] * 2,
+        in_specs=[pl.BlockSpec(), ANY],
         out_shape=[jax.ShapeDtypeStruct((heads, rows, part), jnp.bfloat16)] * 2,
         compiler_params=SMALL,
-    )(vq, k_before, k_after)
+    )(vq, k_before)
     v_before, v_after = shifted(v_high, 1), shifted(v_low, -1)
     partial = near_attention(tiles, bias, vq, far_memory(k), k_before, k_after, keep, got, add)
     outs = far_attention(place, v_before, v_after, *partial)

time: 108 us -> 107 us (level)
  waiting for transfers between devices: 41.6 us -> 38.2 us
  local copies, waits for them, and re-layouts: 0.9 us -> 2.52 us
  starting transfers between devices: 33.6 us -> 35 us
    ppermute x7, waiting for transfers between devices: 26.2 us -> 14.2 us  [shifted(): lax.ppermute(x, AXES, [(i, (i + by * ways) % count) for i in range(count)])]
    all_to_all x2, waiting for transfers between devices: 0.01 us -> 8.69 us  [exchange(): lax.all_to_all(x, AXES, split_axis=0, concat_axis=0, tiled=True, axis_ind...]
    ppermute x7, starting transfers between devices: 13.3 us -> 14.8 us  [shifted(): lax.ppermute(x, AXES, [(i, (i + by * ways) % count) for i in range(count)])]
  transfers between devices with their start and end apart: 18 -> 18, of which waited for: 11 -> 10; matrix products, arithmetic and copies ran while one was open for 0% -> 1% of each run, Pallas kernels for 22% -> 22%
where the time goes in v6:
time: 107 us
  waiting for transfers between devices  38.2 us (36%)
  starting transfers between devices  35 us (33%)
  Pallas kernels  30.4 us (28%)
  local copies, waits for them, and re-layouts  2.52 us (2%)
    pallas_call x1, Pallas kernels, near_attention(): pl.pallas_call(functools.partial(near_kernel, tiles, CHUNK if tiles % CHU...  18.1 us
    ppermute x7, starting transfers between devices, shifted(): lax.ppermute(x, AXES, [(i, (i + by * ways) % count) for i in range(count)])  14.8 us
    ppermute x7, waiting for transfers between devices, shifted(): lax.ppermute(x, AXES, [(i, (i + by * ways) % count) for i in range(count)])  14.2 us
    all_to_all x2, starting transfers between devices, exchange(): lax.all_to_all(x, AXES, split_axis=0, concat_axis=0, tiled=True, axis_ind...  8.8 us
    all_to_all x2, waiting for transfers between devices, exchange(): lax.all_to_all(x, AXES, split_axis=0, concat_axis=0, tiled=True, axis_ind...  8.69 us
    ppermute x7, waiting for transfers between devices, crossed(): lax.ppermute(x, AXES, [(i, i // ways * ways + (i % ways ^ by)) for i in r...  7.95 us
    ppermute x7, starting transfers between devices, crossed(): lax.ppermute(x, AXES, [(i, i // ways * ways + (i % ways ^ by)) for i in r...  7.75 us
    ppermute x2, waiting for transfers between devices, swapped(): return lax.ppermute(x, AXES, [(i, flip(i)) for i in range(count)])  7.43 us
  transfers between devices with their start and end apart: 18, of which 10 were waited for; matrix products, arithmetic and copies ran while one was open for 1% of the time, Pallas kernels for 22%

profile of v6, /device:TPU:0, one launch (start us, length us, event | category | flops | bytes accessed | tf_op | source)
XLA Modules:
  0.0 107.0 jit_solution(16831230215837889668)
XLA Ops:
  0.0 2.2 %shard_map.83 = bf16[8,192,384]{2,1,0:T(8,128)(2,1)} custom-call(bf16[192,3072]{1,0:T(8,128)(2,1)} %refs_0_.3), custom_call_target="tpu_custom_call" | custom-call | tf_op jit(solution)/shard_map/pallas_call | solution.py:235
  2.2 0.0 copy-start.2
  2.2 5.2 %all-to-all-start = ((bf16[8,192,384]{2,1,0:T(8,128)(2,1)}), bf16[8,192,384]{2,1,0:T(8,128)(2,1)S(1)}, u32[]{:S(2)}, u32[]{:S(2)}) async-start(bf16[8,192,384]{2,1,0:T(8,128)(2,1)} %shard_map.83), calls=%async_computation | async-start | bytes 2359296 | tf_op jit(solution)/shard_map/all_to_all | solution.py:349
  8.0 0.1 stack.27.place
  8.1 0.0 copy-done.2
  8.1 1.5 %shard_map.84 = (bf16[16,128]{1,0:T(8,128)(2,1)S(1)}, bf16[2,32,768]{2,1,0:T(8,128)(2,1)S(1)}) custom-call(s32[7]{0:T(128)S(1)} %stack.27.place, s32[6]{0:T(128)S(1)} %copy-done.2, s32[6,12]{1,0:T(8,128)} %list_hbm.1, bf16[32,768]{1,0:T(8,128)(2,1)} %k_ref.1, bf16[32,768]{1,0:T(8,128)(2,1)} %v_ref.1), custom_call_target="tpu_custom_call" | custom-call | tf_op jit(solution)/shard_map/pallas_call | solution.py:359
  9.6 1.6 %collective-permute-start.1 = (bf16[2,32,768]{2,1,0:T(8,128)(2,1)S(1)}, bf16[2,32,768]{2,1,0:T(8,128)(2,1)S(1)}, u32[]{:S(2)}, u32[]{:S(2)}) collective-permute-start(bf16[2,32,768]{2,1,0:T(8,128)(2,1)S(1)} %get-tuple-element.25.refs_0_), channel_id=1, source_target_pairs={{0,8},{1,9},{2,10},{3,11},{4,12},{5,13},{6,14},{7,15},{8,16},{9,17... | collective-permute-start | bytes 294920 | tf_op jit(solution)/shard_map/ppermute | solution.py:339
  11.2 2.6 %collective-permute-start.2 = (bf16[2,32,768]{2,1,0:T(8,128)(2,1)S(1)}, bf16[2,32,768]{2,1,0:T(8,128)(2,1)S(1)}, u32[]{:S(2)}, u32[]{:S(2)}) collective-permute-start(bf16[2,32,768]{2,1,0:T(8,128)(2,1)S(1)} %get-tuple-element.25.refs_0_), channel_id=1, source_target_pairs={{0,16},{1,17},{2,18},{3,19},{4,20},{5,21},{6,22},{7,23},{8,24},{9,... | collective-permute-start | bytes 294920 | tf_op jit(solution)/shard_map/ppermute | solution.py:339
  13.8 1.3 %collective-permute-start.3 = (bf16[2,32,768]{2,1,0:T(8,128)(2,1)S(1)}, bf16[2,32,768]{2,1,0:T(8,128)(2,1)S(1)}, u32[]{:S(2)}, u32[]{:S(2)}) collective-permute-start(bf16[2,32,768]{2,1,0:T(8,128)(2,1)S(1)} %get-tuple-element.25.refs_0_), channel_id=1, source_target_pairs={{0,24},{1,25},{2,26},{3,27},{4,28},{5,29},{6,30},{7,31},{8,0},{9,1... | collective-permute-start | bytes 294920 | tf_op jit(solution)/shard_map/ppermute | solution.py:339
  15.2 2.0 %collective-permute-start = (bf16[16,128]{1,0:T(8,128)(2,1)S(1)}, bf16[16,128]{1,0:T(8,128)(2,1)S(1)}, u32[]{:S(2)}, u32[]{:S(2)}) collective-permute-start(bf16[16,128]{1,0:T(8,128)(2,1)S(1)} %get-tuple-element.24.mask_ref), channel_id=1, source_target_pairs={{0,4},{1,5},{2,6},{3,7},{4,0},{5,1},{6,2},{7,3},{8,12},{9,13},{10,... | collective-permute-start | bytes 12296 | tf_op jit(solution)/shard_map/ppermute | solution.py:343
  17.2 2.7 %shard_map.82.__0_ = bf16[8,2,192,384]{3,2,1,0:T(8,128)(2,1)} custom-call(bf16[192,3072]{1,0:T(8,128)(2,1)} %refs_0_.2, bf16[192,3072]{1,0:T(8,128)(2,1)} %refs_1_.1), custom_call_target="tpu_custom_call" | custom-call | tf_op jit(solution)/shard_map/pallas_call | solution.py:235
  19.9 3.4 %collective-permute-done.their_ref = bf16[16,128]{1,0:T(8,128)(2,1)S(1)} collective-permute-done((bf16[16,128]{1,0:T(8,128)(2,1)S(1)}, bf16[16,128]{1,0:T(8,128)(2,1)S(1)}, u32[]{:S(2)}, u32[]{:S(2)}) %collective-permute-start) | collective-permute-done | bytes 4128 | tf_op jit(solution)/shard_map/ppermute | solution.py:343
  23.3 0.0 collective-permute-done.1.refs_1_
  23.3 0.0 collective-permute-done.2.refs_2_
  23.3 0.0 collective-permute-done.3.refs_3_
  23.3 1.4 %shard_map.85 = (bf16[2,128,384]{2,1,0:T(8,128)(2,1)}, bf16[2,128,384]{2,1,0:T(8,128)(2,1)}, f32[16,128]{1,0:T(8,128)}, f32[256,128]{1,0:T(8,128)}) custom-call(s32[7]{0:T(128)S(1)} %stack.27.place, bf16[16,128]{1,0:T(8,128)(2,1)S(1)} %get-tuple-element.24.mask_ref, bf16[16,128]{1,0:T(8,128)(2,1)S(1)} %collective-permute-done.their_ref, ...), custom_call_target="tpu_custom_call" | custom-call | tf_op jit(solution)/shard_map/pallas_call | solution.py:379
  24.7 0.0 all-to-all-done.__1_.k_ref
  24.7 0.0 copy-start
  24.7 3.6 %all-to-all-start.1 = ((bf16[8,2,192,384]{3,2,1,0:T(8,128)(2,1)}), bf16[8,2,192,384]{3,2,1,0:T(8,128)(2,1)S(1)}, u32[]{:S(2)}, u32[]{:S(2)}) async-start(bf16[8,2,192,384]{3,2,1,0:T(8,128)(2,1)} %shard_map.86), calls=%async_computation.1 | async-start | bytes 4718592 | tf_op jit(solution)/shard_map/all_to_all | solution.py:349
  28.4 0.0 copy-done
  28.4 0.9 fusion
  29.3 1.6 %collective-permute-start.4 = (bf16[4,192,384]{2,1,0:T(8,128)(2,1)S(1)}, bf16[4,192,384]{2,1,0:T(8,128)(2,1)S(1)}, u32[]{:S(2)}, u32[]{:S(2)}) collective-permute-start(bf16[4,192,384]{2,1,0:T(8,128)(2,1)S(1)} %get-tuple-element.44), channel_id=1, source_target_pairs={{0,8},{1,9},{2,10},{3,11},{4,12},{5,13},{6,14},{7,15},{8,16},{9,17... | collective-permute-start | bytes 1769480 | tf_op jit(solution)/shard_map/ppermute | solution.py:339
  30.9 0.0 copy-start.5
  30.9 0.0 copy-start.1
  30.9 2.2 %collective-permute-start.7 = (bf16[4,192,384]{2,1,0:T(8,128)(2,1)}, bf16[4,192,384]{2,1,0:T(8,128)(2,1)}, u32[]{:S(2)}, u32[]{:S(2)}) collective-permute-start(bf16[4,192,384]{2,1,0:T(8,128)(2,1)} %get-tuple-element.43), channel_id=1, source_target_pairs={{0,24},{1,25},{2,26},{3,27},{4,28},{5,29},{6,30},{7,31},{8,0},{9,1... | collective-permute-start | bytes 1769480 | tf_op jit(solution)/shard_map/ppermute | solution.py:339
  33.1 14.1 %collective-permute-done.4._.before_ref = bf16[4,192,384]{2,1,0:T(8,128)(2,1)S(1)} collective-permute-done((bf16[4,192,384]{2,1,0:T(8,128)(2,1)S(1)}, bf16[4,192,384]{2,1,0:T(8,128)(2,1)S(1)}, u32[]{:S(2)}, u32[]{:S(2)}) %collective-permute-start.4) | collective-permute-done | bytes 589856 | tf_op jit(solution)/shard_map/ppermute | solution.py:339
  47.3 0.0 copy-start.3
  47.3 0.8 copy-done.3
  48.1 8.7 %all-to-all-done.1.vq_ref.q_ref.v_ref = bf16[8,2,192,384]{3,2,1,0:T(8,128)(2,1)S(1)} async-done(((bf16[8,2,192,384]{3,2,1,0:T(8,128)(2,1)}), bf16[8,2,192,384]{3,2,1,0:T(8,128)(2,1)S(1)}, u32[]{:S(2)}, u32[]{:S(2)}) %all-to-all-start.1) | async-done | bytes 2359328 | tf_op jit(solution)/shard_map/all_to_all | solution.py:349
  56.8 0.1 shard_map.87
  56.9 1.6 %collective-permute-start.5 = (bf16[4,192,384]{2,1,0:T(8,128)(2,1)S(1)}, bf16[4,192,384]{2,1,0:T(8,128)(2,1)S(1)}, u32[]{:S(2)}, u32[]{:S(2)}) collective-permute-start(bf16[4,192,384]{2,1,0:T(8,128)(2,1)S(1)} %get-tuple-element.27), channel_id=1, source_target_pairs={{0,8},{1,9},{2,10},{3,11},{4,12},{5,13},{6,14},{7,15},{8,16},{9,17... | collective-permute-start | bytes 1769480 | tf_op jit(solution)/shard_map/ppermute | solution.py:339
  58.5 3.7 %collective-permute-start.6 = (bf16[4,192,384]{2,1,0:T(8,128)(2,1)S(1)}, bf16[4,192,384]{2,1,0:T(8,128)(2,1)S(1)}, u32[]{:S(2)}, u32[]{:S(2)}) collective-permute-start(bf16[4,192,384]{2,1,0:T(8,128)(2,1)S(1)} %get-tuple-element.28), channel_id=1, source_target_pairs={{0,24},{1,25},{2,26},{3,27},{4,28},{5,29},{6,30},{7,31},{8,0},{9,1... | collective-permute-start | bytes 1769480 | tf_op jit(solution)/shard_map/ppermute | solution.py:339
  62.3 0.0 copy-done.5
  62.3 1.7 %collective-permute-start.8 = (bf16[2,128,384]{2,1,0:T(8,128)(2,1)S(1)}, bf16[2,128,384]{2,1,0:T(8,128)(2,1)S(1)}, u32[]{:S(2)}, u32[]{:S(2)}) collective-permute-start(bf16[2,128,384]{2,1,0:T(8,128)(2,1)S(1)} %copy-done.5), channel_id=1, source_target_pairs={{0,4},{1,5},{2,6},{3,7},{4,0},{5,1},{6,2},{7,3},{8,12},{9,13},{10,... | collective-permute-start | bytes 589832 | tf_op jit(solution)/shard_map/ppermute | solution.py:343
  63.9 4.0 %collective-permute-done.8.got_ref = bf16[2,128,384]{2,1,0:T(8,128)(2,1)S(1)} collective-permute-done((bf16[2,128,384]{2,1,0:T(8,128)(2,1)S(1)}, bf16[2,128,384]{2,1,0:T(8,128)(2,1)S(1)}, u32[]{:S(2)}, u32[]{:S(2)}) %collective-permute-start.8) | collective-permute-done | bytes 196640 | tf_op jit(solution)/shard_map/ppermute | solution.py:343
  67.9 0.0 copy-start.4
  67.9 0.0 collective-permute-done.7.after_ref
  67.9 0.7 copy-done.4
  68.6 0.0 copy-done.1
  68.6 18.1 %shard_map.88 = (f32[3,2,128,768]{3,2,1,0:T(8,128)S(1)}, bf16[3,2,768,768]{3,2,1,0:T(8,128)(2,1)S(1)}, f32[3,2,1,768]{3,2,1,0:T(1,128)S(1)}) custom-call(f32[16,128]{1,0:T(8,128)S(1)} %copy-done.1, bf16[8,2,192,384]{3,2,1,0:T(8,128)(2,1)S(1)} %all-to-all-done.1.vq_ref.q_ref.v_ref, bf16[8,2,192,384]{3,2,1,0:T(8,128)(2,1)S(1)} %all-to-all-done.1.vq_ref.q_ref.v_ref, ...), custom_call_target="tpu_custom_call" | custom-call | tf_op jit(solution)/shard_map/pallas_call | solution.py:144
  86.7 0.0 collective-permute-done.5.before_ref
  86.7 0.0 collective-permute-done.6.after_ref
  86.8 2.8 %shard_map.89 = (bf16[192,384]{1,0:T(8,128)(2,1)S(1)}, bf16[192,384]{1,0:T(8,128)(2,1)S(1)}, bf16[192,384]{1,0:T(8,128)(2,1)S(1)}, bf16[192,384]{1,0:T(8,128)(2,...) custom-call(s32[7]{0:T(128)S(1)} %stack.27.place, ...), custom_call_target="tpu_custom_call" | custom-call | tf_op jit(solution)/shard_map/pallas_call | solution.py:177
  89.6 1.7 %collective-permute-start.10 = (bf16[192,384]{1,0:T(8,128)(2,1)S(1)}, bf16[192,384]{1,0:T(8,128)(2,1)S(1)}, u32[]{:S(2)}, u32[]{:S(2)}) collective-permute-start(bf16[192,384]{1,0:T(8,128)(2,1)S(1)} %get-tuple-element.37), channel_id=1, source_target_pairs={{0,2},{1,3},{2,0},{3,1},{4,6},{5,7},{6,4},{7,5},{8,10},{9,11},{10,... | collective-permute-start | bytes 442376 | tf_op jit(solution)/shard_map/ppermute | solution.py:346
  91.3 1.5 %collective-permute-start.11 = (bf16[192,384]{1,0:T(8,128)(2,1)S(1)}, bf16[192,384]{1,0:T(8,128)(2,1)S(1)}, u32[]{:S(2)}, u32[]{:S(2)}) collective-permute-start(bf16[192,384]{1,0:T(8,128)(2,1)S(1)} %get-tuple-element.38), channel_id=1, source_target_pairs={{0,4},{1,5},{2,6},{3,7},{4,0},{5,1},{6,2},{7,3},{8,12},{9,13},{10,... | collective-permute-start | bytes 442376 | tf_op jit(solution)/shard_map/ppermute | solution.py:346
  92.8 0.0 collective-permute-start.12
  92.8 1.7 %collective-permute-start.13 = (bf16[192,384]{1,0:T(8,128)(2,1)S(1)}, bf16[192,384]{1,0:T(8,128)(2,1)S(1)}, u32[]{:S(2)}, u32[]{:S(2)}) collective-permute-start(bf16[192,384]{1,0:T(8,128)(2,1)S(1)} %get-tuple-element.40), channel_id=1, source_target_pairs={{0,3},{1,2},{2,1},{3,0},{4,7},{5,6},{6,5},{7,4},{8,11},{9,10},{10,... | collective-permute-start | bytes 442376 | tf_op jit(solution)/shard_map/ppermute | solution.py:346
  94.5 0.0 collective-permute-start.14
  94.5 0.3 collective-permute-done.10.refs_2_
  94.8 1.3 %collective-permute-start.15 = (bf16[192,384]{1,0:T(8,128)(2,1)S(1)}, bf16[192,384]{1,0:T(8,128)(2,1)S(1)}, u32[]{:S(2)}, u32[]{:S(2)}) collective-permute-start(bf16[192,384]{1,0:T(8,128)(2,1)S(1)} %get-tuple-element.42), channel_id=1, source_target_pairs={{0,1},{1,0},{2,3},{3,2},{4,5},{5,4},{6,7},{7,6},{8,9},{9,8},{10,11... | collective-permute-start | bytes 442376 | tf_op jit(solution)/shard_map/ppermute | solution.py:346
  96.1 1.0 collective-permute-done.11.refs_3_
  97.1 1.5 %collective-permute-start.9 = (bf16[192,384]{1,0:T(8,128)(2,1)S(1)}, bf16[192,384]{1,0:T(8,128)(2,1)S(1)}, u32[]{:S(2)}, u32[]{:S(2)}) collective-permute-start(bf16[192,384]{1,0:T(8,128)(2,1)S(1)} %get-tuple-element.36), channel_id=1, source_target_pairs={{0,6},{1,7},{2,4},{3,5},{4,2},{5,3},{6,0},{7,1},{8,14},{9,15},{10,... | collective-permute-start | bytes 442376 | tf_op jit(solution)/shard_map/ppermute | solution.py:346
  98.6 1.6 %collective-permute-done.12.refs_4_ = bf16[192,384]{1,0:T(8,128)(2,1)S(1)} collective-permute-done((bf16[192,384]{1,0:T(8,128)(2,1)S(1)}, bf16[192,384]{1,0:T(8,128)(2,1)S(1)}, u32[]{:S(2)}, u32[]{:S(2)}) %collective-permute-start.12) | collective-permute-done | bytes 147488 | tf_op jit(solution)/shard_map/ppermute | solution.py:346
  100.2 1.4 %collective-permute-done.13.refs_5_ = bf16[192,384]{1,0:T(8,128)(2,1)S(1)} collective-permute-done((bf16[192,384]{1,0:T(8,128)(2,1)S(1)}, bf16[192,384]{1,0:T(8,128)(2,1)S(1)}, u32[]{:S(2)}, u32[]{:S(2)}) %collective-permute-start.13) | collective-permute-done | bytes 147488 | tf_op jit(solution)/shard_map/ppermute | solution.py:346
  101.6 1.6 %collective-permute-done.14.refs_6_ = bf16[192,384]{1,0:T(8,128)(2,1)S(1)} collective-permute-done((bf16[192,384]{1,0:T(8,128)(2,1)S(1)}, bf16[192,384]{1,0:T(8,128)(2,1)S(1)}, u32[]{:S(2)}, u32[]{:S(2)}) %collective-permute-start.14) | collective-permute-done | bytes 147488 | tf_op jit(solution)/shard_map/ppermute | solution.py:346
  103.1 0.0 collective-permute-done.15.refs_7_
  103.1 2.2 %collective-permute-done.9.refs_1_ = bf16[192,384]{1,0:T(8,128)(2,1)S(1)} collective-permute-done((bf16[192,384]{1,0:T(8,128)(2,1)S(1)}, bf16[192,384]{1,0:T(8,128)(2,1)S(1)}, u32[]{:S(2)}, u32[]{:S(2)}) %collective-permute-start.9) | collective-permute-done | bytes 147488 | tf_op jit(solution)/shard_map/ppermute | solution.py:346
  105.3 1.7 %shard_map.90 = bf16[192,3072]{1,0:T(8,128)(2,1)} custom-call(s32[7]{0:T(128)S(1)} %stack.27.place, bf16[192,384]{1,0:T(8,128)(2,1)S(1)} %get-tuple-element.35.refs_0_, bf16[192,384]{1,0:T(8,128)(2,1)S(1)} %collective-permute-done.9.refs_1_, bf16[192,384]{1,0:T(8,128)(2,1)S(1)} %collective-permute-done.10.refs_2_, ...), custom_call_target="tpu_custom_call" | custom-call | tf_op jit(solution)/shard_map/pallas_call | solution.py:251
  (1 shorter events, 0.0 us)
Async XLA Ops:
  2.2 5.9 %copy-start.2 = (s32[6]{0:T(128)S(1)}, s32[6]{0:T(128)}, u32[]{:S(2)}) copy-start(s32[6]{0:T(128)} %count.1) | copy-start | bytes 76
  2.2 22.6 %all-to-all-start = ((bf16[8,192,384]{2,1,0:T(8,128)(2,1)}), bf16[8,192,384]{2,1,0:T(8,128)(2,1)S(1)}, u32[]{:S(2)}, u32[]{:S(2)}) async-start(bf16[8,192,384]{2,1,0:T(8,128)(2,1)} %shard_map.83), calls=%async_computation | async-start | bytes 2359296 | tf_op jit(solution)/shard_map/all_to_all | solution.py:349
  9.6 13.7 %collective-permute-start.1 = (bf16[2,32,768]{2,1,0:T(8,128)(2,1)S(1)}, bf16[2,32,768]{2,1,0:T(8,128)(2,1)S(1)}, u32[]{:S(2)}, u32[]{:S(2)}) collective-permute-start(bf16[2,32,768]{2,1,0:T(8,128)(2,1)S(1)} %get-tuple-element.25.refs_0_), channel_id=1, source_target_pairs={{0,8},{1,9},{2,10},{3,11},{4,12},{5,13},{6,14},{7,15},{8,16},{9,17... | collective-permute-start | bytes 294920 | tf_op jit(solution)/shard_map/ppermute | solution.py:339
  11.2 12.1 %collective-permute-start.2 = (bf16[2,32,768]{2,1,0:T(8,128)(2,1)S(1)}, bf16[2,32,768]{2,1,0:T(8,128)(2,1)S(1)}, u32[]{:S(2)}, u32[]{:S(2)}) collective-permute-start(bf16[2,32,768]{2,1,0:T(8,128)(2,1)S(1)} %get-tuple-element.25.refs_0_), channel_id=1, source_target_pairs={{0,16},{1,17},{2,18},{3,19},{4,20},{5,21},{6,22},{7,23},{8,24},{9,... | collective-permute-start | bytes 294920 | tf_op jit(solution)/shard_map/ppermute | solution.py:339
  13.8 9.5 %collective-permute-start.3 = (bf16[2,32,768]{2,1,0:T(8,128)(2,1)S(1)}, bf16[2,32,768]{2,1,0:T(8,128)(2,1)S(1)}, u32[]{:S(2)}, u32[]{:S(2)}) collective-permute-start(bf16[2,32,768]{2,1,0:T(8,128)(2,1)S(1)} %get-tuple-element.25.refs_0_), channel_id=1, source_target_pairs={{0,24},{1,25},{2,26},{3,27},{4,28},{5,29},{6,30},{7,31},{8,0},{9,1... | collective-permute-start | bytes 294920 | tf_op jit(solution)/shard_map/ppermute | solution.py:339
  15.2 8.1 %collective-permute-start = (bf16[16,128]{1,0:T(8,128)(2,1)S(1)}, bf16[16,128]{1,0:T(8,128)(2,1)S(1)}, u32[]{:S(2)}, u32[]{:S(2)}) collective-permute-start(bf16[16,128]{1,0:T(8,128)(2,1)S(1)} %get-tuple-element.24.mask_ref), channel_id=1, source_target_pairs={{0,4},{1,5},{2,6},{3,7},{4,0},{5,1},{6,2},{7,3},{8,12},{9,13},{10,... | collective-permute-start | bytes 12296 | tf_op jit(solution)/shard_map/ppermute | solution.py:343
  24.7 3.6 %copy-start = (bf16[8,192,384]{2,1,0:T(8,128)(2,1)}, bf16[8,192,384]{2,1,0:T(8,128)(2,1)S(1)}, u32[]{:S(2)}) copy-start(bf16[8,192,384]{2,1,0:T(8,128)(2,1)S(1)} %all-to-all-done.__1_.k_ref) | copy-start | bytes 3538948
  24.7 32.1 %all-to-all-start.1 = ((bf16[8,2,192,384]{3,2,1,0:T(8,128)(2,1)}), bf16[8,2,192,384]{3,2,1,0:T(8,128)(2,1)S(1)}, u32[]{:S(2)}, u32[]{:S(2)}) async-start(bf16[8,2,192,384]{3,2,1,0:T(8,128)(2,1)} %shard_map.86), calls=%async_computation.1 | async-start | bytes 4718592 | tf_op jit(solution)/shard_map/all_to_all | solution.py:349
  29.3 18.0 %collective-permute-start.4 = (bf16[4,192,384]{2,1,0:T(8,128)(2,1)S(1)}, bf16[4,192,384]{2,1,0:T(8,128)(2,1)S(1)}, u32[]{:S(2)}, u32[]{:S(2)}) collective-permute-start(bf16[4,192,384]{2,1,0:T(8,128)(2,1)S(1)} %get-tuple-element.44), channel_id=1, source_target_pairs={{0,8},{1,9},{2,10},{3,11},{4,12},{5,13},{6,14},{7,15},{8,16},{9,17... | collective-permute-start | bytes 1769480 | tf_op jit(solution)/shard_map/ppermute | solution.py:339
  30.9 31.4 %copy-start.5 = (bf16[2,128,384]{2,1,0:T(8,128)(2,1)S(1)}, bf16[2,128,384]{2,1,0:T(8,128)(2,1)}, u32[]{:S(2)}) copy-start(bf16[2,128,384]{2,1,0:T(8,128)(2,1)} %get-tuple-element.31) | copy-start | bytes 589828
  30.9 37.7 %copy-start.1 = (f32[16,128]{1,0:T(8,128)S(1)}, f32[16,128]{1,0:T(8,128)}, u32[]{:S(2)}) copy-start(f32[16,128]{1,0:T(8,128)} %get-tuple-element.29.bias) | copy-start | bytes 24580
  30.9 37.0 %collective-permute-start.7 = (bf16[4,192,384]{2,1,0:T(8,128)(2,1)}, bf16[4,192,384]{2,1,0:T(8,128)(2,1)}, u32[]{:S(2)}, u32[]{:S(2)}) collective-permute-start(bf16[4,192,384]{2,1,0:T(8,128)(2,1)} %get-tuple-element.43), channel_id=1, source_target_pairs={{0,24},{1,25},{2,26},{3,27},{4,28},{5,29},{6,30},{7,31},{8,0},{9,1... | collective-permute-start | bytes 1769480 | tf_op jit(solution)/shard_map/ppermute | solution.py:339
  47.3 0.8 copy-start.3
  56.9 29.8 %collective-permute-start.5 = (bf16[4,192,384]{2,1,0:T(8,128)(2,1)S(1)}, bf16[4,192,384]{2,1,0:T(8,128)(2,1)S(1)}, u32[]{:S(2)}, u32[]{:S(2)}) collective-permute-start(bf16[4,192,384]{2,1,0:T(8,128)(2,1)S(1)} %get-tuple-element.27), channel_id=1, source_target_pairs={{0,8},{1,9},{2,10},{3,11},{4,12},{5,13},{6,14},{7,15},{8,16},{9,17... | collective-permute-start | bytes 1769480 | tf_op jit(solution)/shard_map/ppermute | solution.py:339
  58.5 28.2 %collective-permute-start.6 = (bf16[4,192,384]{2,1,0:T(8,128)(2,1)S(1)}, bf16[4,192,384]{2,1,0:T(8,128)(2,1)S(1)}, u32[]{:S(2)}, u32[]{:S(2)}) collective-permute-start(bf16[4,192,384]{2,1,0:T(8,128)(2,1)S(1)} %get-tuple-element.28), channel_id=1, source_target_pairs={{0,24},{1,25},{2,26},{3,27},{4,28},{5,29},{6,30},{7,31},{8,0},{9,1... | collective-permute-start | bytes 1769480 | tf_op jit(solution)/shard_map/ppermute | solution.py:339
  62.3 5.7 %collective-permute-start.8 = (bf16[2,128,384]{2,1,0:T(8,128)(2,1)S(1)}, bf16[2,128,384]{2,1,0:T(8,128)(2,1)S(1)}, u32[]{:S(2)}, u32[]{:S(2)}) collective-permute-start(bf16[2,128,384]{2,1,0:T(8,128)(2,1)S(1)} %copy-done.5), channel_id=1, source_target_pairs={{0,4},{1,5},{2,6},{3,7},{4,0},{5,1},{6,2},{7,3},{8,12},{9,13},{10,... | collective-permute-start | bytes 589832 | tf_op jit(solution)/shard_map/ppermute | solution.py:343
  67.9 0.7 copy-start.4
  89.6 5.2 %collective-permute-start.10 = (bf16[192,384]{1,0:T(8,128)(2,1)S(1)}, bf16[192,384]{1,0:T(8,128)(2,1)S(1)}, u32[]{:S(2)}, u32[]{:S(2)}) collective-permute-start(bf16[192,384]{1,0:T(8,128)(2,1)S(1)} %get-tuple-element.37), channel_id=1, source_target_pairs={{0,2},{1,3},{2,0},{3,1},{4,6},{5,7},{6,4},{7,5},{8,10},{9,11},{10,... | collective-permute-start | bytes 442376 | tf_op jit(solution)/shard_map/ppermute | solution.py:346
  91.3 5.8 %collective-permute-start.11 = (bf16[192,384]{1,0:T(8,128)(2,1)S(1)}, bf16[192,384]{1,0:T(8,128)(2,1)S(1)}, u32[]{:S(2)}, u32[]{:S(2)}) collective-permute-start(bf16[192,384]{1,0:T(8,128)(2,1)S(1)} %get-tuple-element.38), channel_id=1, source_target_pairs={{0,4},{1,5},{2,6},{3,7},{4,0},{5,1},{6,2},{7,3},{8,12},{9,13},{10,... | collective-permute-start | bytes 442376 | tf_op jit(solution)/shard_map/ppermute | solution.py:346
  92.8 7.4 %collective-permute-start.12 = (bf16[192,384]{1,0:T(8,128)(2,1)S(1)}, bf16[192,384]{1,0:T(8,128)(2,1)S(1)}, u32[]{:S(2)}, u32[]{:S(2)}) collective-permute-start(bf16[192,384]{1,0:T(8,128)(2,1)S(1)} %get-tuple-element.39), channel_id=1, source_target_pairs={{0,7},{1,6},{2,5},{3,4},{4,3},{5,2},{6,1},{7,0},{8,15},{9,14},{10,... | collective-permute-start | bytes 442376 | tf_op jit(solution)/shard_map/ppermute | solution.py:346
  92.8 8.8 %collective-permute-start.13 = (bf16[192,384]{1,0:T(8,128)(2,1)S(1)}, bf16[192,384]{1,0:T(8,128)(2,1)S(1)}, u32[]{:S(2)}, u32[]{:S(2)}) collective-permute-start(bf16[192,384]{1,0:T(8,128)(2,1)S(1)} %get-tuple-element.40), channel_id=1, source_target_pairs={{0,3},{1,2},{2,1},{3,0},{4,7},{5,6},{6,5},{7,4},{8,11},{9,10},{10,... | collective-permute-start | bytes 442376 | tf_op jit(solution)/shard_map/ppermute | solution.py:346
  94.5 8.6 %collective-permute-start.14 = (bf16[192,384]{1,0:T(8,128)(2,1)S(1)}, bf16[192,384]{1,0:T(8,128)(2,1)S(1)}, u32[]{:S(2)}, u32[]{:S(2)}) collective-permute-start(bf16[192,384]{1,0:T(8,128)(2,1)S(1)} %get-tuple-element.41), channel_id=1, source_target_pairs={{0,5},{1,4},{2,7},{3,6},{4,1},{5,0},{6,3},{7,2},{8,13},{9,12},{10,... | collective-permute-start | bytes 442376 | tf_op jit(solution)/shard_map/ppermute | solution.py:346
  94.8 8.3 %collective-permute-start.15 = (bf16[192,384]{1,0:T(8,128)(2,1)S(1)}, bf16[192,384]{1,0:T(8,128)(2,1)S(1)}, u32[]{:S(2)}, u32[]{:S(2)}) collective-permute-start(bf16[192,384]{1,0:T(8,128)(2,1)S(1)} %get-tuple-element.42), channel_id=1, source_target_pairs={{0,1},{1,0},{2,3},{3,2},{4,5},{5,4},{6,7},{7,6},{8,9},{9,8},{10,11... | collective-permute-start | bytes 442376 | tf_op jit(solution)/shard_map/ppermute | solution.py:346
  97.1 8.2 %collective-permute-start.9 = (bf16[192,384]{1,0:T(8,128)(2,1)S(1)}, bf16[192,384]{1,0:T(8,128)(2,1)S(1)}, u32[]{:S(2)}, u32[]{:S(2)}) collective-permute-start(bf16[192,384]{1,0:T(8,128)(2,1)S(1)} %get-tuple-element.36), channel_id=1, source_target_pairs={{0,6},{1,7},{2,4},{3,5},{4,2},{5,3},{6,0},{7,1},{8,14},{9,15},{10,... | collective-permute-start | bytes 442376 | tf_op jit(solution)/shard_map/ppermute | solution.py:346

commit v7 on v6

--- a/solution.py
+++ b/solution.py
@@ -397,7 +397,7 @@
         in_specs=[pl.BlockSpec(), ANY],
         out_shape=[jax.ShapeDtypeStruct((heads, rows, part), jnp.bfloat16)] * 2,
         compiler_params=SMALL,
-    )(vq, k_before)
+    )(vq, k_after)
     v_before, v_after = shifted(v_high, 1), shifted(v_low, -1)
     partial = near_attention(tiles, bias, vq, far_memory(k), k_before, k_after, keep, got, add)
     outs = far_attention(place, v_before, v_after, *partial)

time: 107 us -> 107 us (level)
  starting transfers between devices: 35 us -> 30.5 us
  waiting for transfers between devices: 38.2 us -> 42.3 us
    ppermute x7, waiting for transfers between devices: 7.95 us -> 11 us  [crossed(): lax.ppermute(x, AXES, [(i, i // ways * ways + (i % ways ^ by)) for i in r...]
    ppermute x7, starting transfers between devices: 7.75 us -> 5.14 us  [crossed(): lax.ppermute(x, AXES, [(i, i // ways * ways + (i % ways ^ by)) for i in r...]
    ppermute x7, starting transfers between devices: 14.8 us -> 13 us  [shifted(): lax.ppermute(x, AXES, [(i, (i + by * ways) % count) for i in range(count)])]
  transfers between devices with their start and end apart: 18 -> 18, of which waited for: 10 -> 11; matrix products, arithmetic and copies ran while one was open for 1% -> 1% of each run, Pallas kernels for 22% -> 22%
where the time goes in v7:
time: 107 us
  waiting for transfers between devices  42.3 us (40%)
  starting transfers between devices  30.5 us (29%)
  Pallas kernels  30.4 us (28%)
  local copies, waits for them, and re-layouts  2.52 us (2%)
    pallas_call x1, Pallas kernels, near_attention(): pl.pallas_call(functools.partial(near_kernel, tiles, CHUNK if tiles % CHU...  18.1 us
    ppermute x7, waiting for transfers between devices, shifted(): lax.ppermute(x, AXES, [(i, (i + by * ways) % count) for i in range(count)])  13.9 us
    ppermute x7, starting transfers between devices, shifted(): lax.ppermute(x, AXES, [(i, (i + by * ways) % count) for i in range(count)])  13 us
    ppermute x7, waiting for transfers between devices, crossed(): lax.ppermute(x, AXES, [(i, i // ways * ways + (i % ways ^ by)) for i in r...  11 us
    all_to_all x2, waiting for transfers between devices, exchange(): lax.all_to_all(x, AXES, split_axis=0, concat_axis=0, tiled=True, axis_ind...  9.36 us
    all_to_all x2, starting transfers between devices, exchange(): lax.all_to_all(x, AXES, split_axis=0, concat_axis=0, tiled=True, axis_ind...  8.8 us
    ppermute x2, waiting for transfers between devices, swapped(): return lax.ppermute(x, AXES, [(i, flip(i)) for i in range(count)])  8.05 us
    ppermute x7, starting transfers between devices, crossed(): lax.ppermute(x, AXES, [(i, i // ways * ways + (i % ways ^ by)) for i in r...  5.14 us
  transfers between devices with their start and end apart: 18, of which 11 were waited for; matrix products, arithmetic and copies ran while one was open for 1% of the time, Pallas kernels for 22%

profile of v7, /device:TPU:0, one launch (start us, length us, event | category | flops | bytes accessed | tf_op | source)
XLA Modules:
  0.0 106.5 jit_solution(17524239321687861927)
XLA Ops:
  0.0 2.2 %shard_map.83 = bf16[8,192,384]{2,1,0:T(8,128)(2,1)} custom-call(bf16[192,3072]{1,0:T(8,128)(2,1)} %refs_0_.3), custom_call_target="tpu_custom_call" | custom-call | tf_op jit(solution)/shard_map/pallas_call | solution.py:235
  2.2 0.0 copy-start.2
  2.2 5.2 %all-to-all-start = ((bf16[8,192,384]{2,1,0:T(8,128)(2,1)}), bf16[8,192,384]{2,1,0:T(8,128)(2,1)S(1)}, u32[]{:S(2)}, u32[]{:S(2)}) async-start(bf16[8,192,384]{2,1,0:T(8,128)(2,1)} %shard_map.83), calls=%async_computation | async-start | bytes 2359296 | tf_op jit(solution)/shard_map/all_to_all | solution.py:349
  8.0 0.1 stack.27.place
  8.1 0.0 copy-done.2
  8.1 1.5 %shard_map.84 = (bf16[16,128]{1,0:T(8,128)(2,1)S(1)}, bf16[2,32,768]{2,1,0:T(8,128)(2,1)S(1)}) custom-call(s32[7]{0:T(128)S(1)} %stack.27.place, s32[6]{0:T(128)S(1)} %copy-done.2, s32[6,12]{1,0:T(8,128)} %list_hbm.1, bf16[32,768]{1,0:T(8,128)(2,1)} %k_ref.1, bf16[32,768]{1,0:T(8,128)(2,1)} %v_ref.1), custom_call_target="tpu_custom_call" | custom-call | tf_op jit(solution)/shard_map/pallas_call | solution.py:359
  9.6 1.6 %collective-permute-start.1 = (bf16[2,32,768]{2,1,0:T(8,128)(2,1)S(1)}, bf16[2,32,768]{2,1,0:T(8,128)(2,1)S(1)}, u32[]{:S(2)}, u32[]{:S(2)}) collective-permute-start(bf16[2,32,768]{2,1,0:T(8,128)(2,1)S(1)} %get-tuple-element.25.refs_0_), channel_id=1, source_target_pairs={{0,8},{1,9},{2,10},{3,11},{4,12},{5,13},{6,14},{7,15},{8,16},{9,17... | collective-permute-start | bytes 294920 | tf_op jit(solution)/shard_map/ppermute | solution.py:339
  11.2 2.6 %collective-permute-start.2 = (bf16[2,32,768]{2,1,0:T(8,128)(2,1)S(1)}, bf16[2,32,768]{2,1,0:T(8,128)(2,1)S(1)}, u32[]{:S(2)}, u32[]{:S(2)}) collective-permute-start(bf16[2,32,768]{2,1,0:T(8,128)(2,1)S(1)} %get-tuple-element.25.refs_0_), channel_id=1, source_target_pairs={{0,16},{1,17},{2,18},{3,19},{4,20},{5,21},{6,22},{7,23},{8,24},{9,... | collective-permute-start | bytes 294920 | tf_op jit(solution)/shard_map/ppermute | solution.py:339
  13.8 1.3 %collective-permute-start.3 = (bf16[2,32,768]{2,1,0:T(8,128)(2,1)S(1)}, bf16[2,32,768]{2,1,0:T(8,128)(2,1)S(1)}, u32[]{:S(2)}, u32[]{:S(2)}) collective-permute-start(bf16[2,32,768]{2,1,0:T(8,128)(2,1)S(1)} %get-tuple-element.25.refs_0_), channel_id=1, source_target_pairs={{0,24},{1,25},{2,26},{3,27},{4,28},{5,29},{6,30},{7,31},{8,0},{9,1... | collective-permute-start | bytes 294920 | tf_op jit(solution)/shard_map/ppermute | solution.py:339
  15.2 2.0 %collective-permute-start = (bf16[16,128]{1,0:T(8,128)(2,1)S(1)}, bf16[16,128]{1,0:T(8,128)(2,1)S(1)}, u32[]{:S(2)}, u32[]{:S(2)}) collective-permute-start(bf16[16,128]{1,0:T(8,128)(2,1)S(1)} %get-tuple-element.24.mask_ref), channel_id=1, source_target_pairs={{0,4},{1,5},{2,6},{3,7},{4,0},{5,1},{6,2},{7,3},{8,12},{9,13},{10,... | collective-permute-start | bytes 12296 | tf_op jit(solution)/shard_map/ppermute | solution.py:343
  17.2 2.7 %shard_map.82.__0_ = bf16[8,2,192,384]{3,2,1,0:T(8,128)(2,1)} custom-call(bf16[192,3072]{1,0:T(8,128)(2,1)} %refs_0_.2, bf16[192,3072]{1,0:T(8,128)(2,1)} %refs_1_.1), custom_call_target="tpu_custom_call" | custom-call | tf_op jit(solution)/shard_map/pallas_call | solution.py:235
  19.9 3.4 %collective-permute-done.their_ref = bf16[16,128]{1,0:T(8,128)(2,1)S(1)} collective-permute-done((bf16[16,128]{1,0:T(8,128)(2,1)S(1)}, bf16[16,128]{1,0:T(8,128)(2,1)S(1)}, u32[]{:S(2)}, u32[]{:S(2)}) %collective-permute-start) | collective-permute-done | bytes 4128 | tf_op jit(solution)/shard_map/ppermute | solution.py:343
  23.3 0.0 collective-permute-done.1.refs_1_
  23.3 0.0 collective-permute-done.2.refs_2_
  23.3 0.0 collective-permute-done.3.refs_3_
  23.3 1.4 %shard_map.85 = (bf16[2,128,384]{2,1,0:T(8,128)(2,1)}, bf16[2,128,384]{2,1,0:T(8,128)(2,1)}, f32[16,128]{1,0:T(8,128)}, f32[256,128]{1,0:T(8,128)}) custom-call(s32[7]{0:T(128)S(1)} %stack.27.place, bf16[16,128]{1,0:T(8,128)(2,1)S(1)} %get-tuple-element.24.mask_ref, bf16[16,128]{1,0:T(8,128)(2,1)S(1)} %collective-permute-done.their_ref, ...), custom_call_target="tpu_custom_call" | custom-call | tf_op jit(solution)/shard_map/pallas_call | solution.py:379
  24.7 0.0 all-to-all-done.__1_.k_ref
  24.7 0.0 copy-start
  24.7 3.6 %all-to-all-start.1 = ((bf16[8,2,192,384]{3,2,1,0:T(8,128)(2,1)}), bf16[8,2,192,384]{3,2,1,0:T(8,128)(2,1)S(1)}, u32[]{:S(2)}, u32[]{:S(2)}) async-start(bf16[8,2,192,384]{3,2,1,0:T(8,128)(2,1)} %shard_map.86), calls=%async_computation.1 | async-start | bytes 4718592 | tf_op jit(solution)/shard_map/all_to_all | solution.py:349
  28.4 0.0 copy-done
  28.4 0.9 fusion
  29.3 3.6 %collective-permute-start.4 = (bf16[4,192,384]{2,1,0:T(8,128)(2,1)S(1)}, bf16[4,192,384]{2,1,0:T(8,128)(2,1)S(1)}, u32[]{:S(2)}, u32[]{:S(2)}) collective-permute-start(bf16[4,192,384]{2,1,0:T(8,128)(2,1)S(1)} %get-tuple-element.44), channel_id=1, source_target_pairs={{0,24},{1,25},{2,26},{3,27},{4,28},{5,29},{6,30},{7,31},{8,0},{9,1... | collective-permute-start | bytes 1769480 | tf_op jit(solution)/shard_map/ppermute | solution.py:339
  32.9 0.0 copy-start.5
  32.9 0.0 copy-start.1
  32.9 0.0 collective-permute-start.7
  32.9 13.7 %collective-permute-done.4._.after_ref = bf16[4,192,384]{2,1,0:T(8,128)(2,1)S(1)} collective-permute-done((bf16[4,192,384]{2,1,0:T(8,128)(2,1)S(1)}, bf16[4,192,384]{2,1,0:T(8,128)(2,1)S(1)}, u32[]{:S(2)}, u32[]{:S(2)}) %collective-permute-start.4) | collective-permute-done | bytes 589856 | tf_op jit(solution)/shard_map/ppermute | solution.py:339
  46.6 0.0 copy-start.3
  46.6 0.8 copy-done.3
  47.4 9.4 %all-to-all-done.1.vq_ref.q_ref.v_ref = bf16[8,2,192,384]{3,2,1,0:T(8,128)(2,1)S(1)} async-done(((bf16[8,2,192,384]{3,2,1,0:T(8,128)(2,1)}), bf16[8,2,192,384]{3,2,1,0:T(8,128)(2,1)S(1)}, u32[]{:S(2)}, u32[]{:S(2)}) %all-to-all-start.1) | async-done | bytes 2359328 | tf_op jit(solution)/shard_map/all_to_all | solution.py:349
  56.8 0.1 shard_map.87
  56.9 1.6 %collective-permute-start.5 = (bf16[4,192,384]{2,1,0:T(8,128)(2,1)S(1)}, bf16[4,192,384]{2,1,0:T(8,128)(2,1)S(1)}, u32[]{:S(2)}, u32[]{:S(2)}) collective-permute-start(bf16[4,192,384]{2,1,0:T(8,128)(2,1)S(1)} %get-tuple-element.27), channel_id=1, source_target_pairs={{0,8},{1,9},{2,10},{3,11},{4,12},{5,13},{6,14},{7,15},{8,16},{9,17... | collective-permute-start | bytes 1769480 | tf_op jit(solution)/shard_map/ppermute | solution.py:339
  58.5 2.2 %collective-permute-start.6 = (bf16[4,192,384]{2,1,0:T(8,128)(2,1)S(1)}, bf16[4,192,384]{2,1,0:T(8,128)(2,1)S(1)}, u32[]{:S(2)}, u32[]{:S(2)}) collective-permute-start(bf16[4,192,384]{2,1,0:T(8,128)(2,1)S(1)} %get-tuple-element.28), channel_id=1, source_target_pairs={{0,24},{1,25},{2,26},{3,27},{4,28},{5,29},{6,30},{7,31},{8,0},{9,1... | collective-permute-start | bytes 1769480 | tf_op jit(solution)/shard_map/ppermute | solution.py:339
  60.8 0.0 copy-done.5
  60.8 1.5 %collective-permute-start.8 = (bf16[2,128,384]{2,1,0:T(8,128)(2,1)S(1)}, bf16[2,128,384]{2,1,0:T(8,128)(2,1)S(1)}, u32[]{:S(2)}, u32[]{:S(2)}) collective-permute-start(bf16[2,128,384]{2,1,0:T(8,128)(2,1)S(1)} %copy-done.5), channel_id=1, source_target_pairs={{0,4},{1,5},{2,6},{3,7},{4,0},{5,1},{6,2},{7,3},{8,12},{9,13},{10,... | collective-permute-start | bytes 589832 | tf_op jit(solution)/shard_map/ppermute | solution.py:343
  62.3 4.6 %collective-permute-done.8.got_ref = bf16[2,128,384]{2,1,0:T(8,128)(2,1)S(1)} collective-permute-done((bf16[2,128,384]{2,1,0:T(8,128)(2,1)S(1)}, bf16[2,128,384]{2,1,0:T(8,128)(2,1)S(1)}, u32[]{:S(2)}, u32[]{:S(2)}) %collective-permute-start.8) | collective-permute-done | bytes 196640 | tf_op jit(solution)/shard_map/ppermute | solution.py:343
  66.9 0.0 copy-start.4
  66.9 0.0 collective-permute-done.7.before_ref
  66.9 0.7 copy-done.4
  67.6 0.0 copy-done.1
  67.6 18.1 %shard_map.88 = (f32[3,2,128,768]{3,2,1,0:T(8,128)S(1)}, bf16[3,2,768,768]{3,2,1,0:T(8,128)(2,1)S(1)}, f32[3,2,1,768]{3,2,1,0:T(1,128)S(1)}) custom-call(f32[16,128]{1,0:T(8,128)S(1)} %copy-done.1, bf16[8,2,192,384]{3,2,1,0:T(8,128)(2,1)S(1)} %all-to-all-done.1.vq_ref.q_ref.v_ref, bf16[8,2,192,384]{3,2,1,0:T(8,128)(2,1)S(1)} %all-to-all-done.1.vq_ref.q_ref.v_ref, ...), custom_call_target="tpu_custom_call" | custom-call | tf_op jit(solution)/shard_map/pallas_call | solution.py:144
  85.7 0.0 collective-permute-done.5.before_ref
  85.7 0.2 collective-permute-done.6.after_ref
  85.9 2.8 %shard_map.89 = (bf16[192,384]{1,0:T(8,128)(2,1)S(1)}, bf16[192,384]{1,0:T(8,128)(2,1)S(1)}, bf16[192,384]{1,0:T(8,128)(2,1)S(1)}, bf16[192,384]{1,0:T(8,128)(2,...) custom-call(s32[7]{0:T(128)S(1)} %stack.27.place, ...), custom_call_target="tpu_custom_call" | custom-call | tf_op jit(solution)/shard_map/pallas_call | solution.py:177
  88.7 1.5 %collective-permute-start.10 = (bf16[192,384]{1,0:T(8,128)(2,1)S(1)}, bf16[192,384]{1,0:T(8,128)(2,1)S(1)}, u32[]{:S(2)}, u32[]{:S(2)}) collective-permute-start(bf16[192,384]{1,0:T(8,128)(2,1)S(1)} %get-tuple-element.37), channel_id=1, source_target_pairs={{0,2},{1,3},{2,0},{3,1},{4,6},{5,7},{6,4},{7,5},{8,10},{9,11},{10,... | collective-permute-start | bytes 442376 | tf_op jit(solution)/shard_map/ppermute | solution.py:346
  90.2 0.7 collective-permute-start.11
  90.9 0.0 collective-permute-start.12
  90.9 2.5 %collective-permute-start.13 = (bf16[192,384]{1,0:T(8,128)(2,1)S(1)}, bf16[192,384]{1,0:T(8,128)(2,1)S(1)}, u32[]{:S(2)}, u32[]{:S(2)}) collective-permute-start(bf16[192,384]{1,0:T(8,128)(2,1)S(1)} %get-tuple-element.40), channel_id=1, source_target_pairs={{0,3},{1,2},{2,1},{3,0},{4,7},{5,6},{6,5},{7,4},{8,11},{9,10},{10,... | collective-permute-start | bytes 442376 | tf_op jit(solution)/shard_map/ppermute | solution.py:346
  93.4 0.0 collective-permute-start.14
  93.4 0.5 collective-permute-done.10.refs_2_
  93.9 0.4 collective-permute-start.15
  94.3 2.3 %collective-permute-done.11.refs_3_ = bf16[192,384]{1,0:T(8,128)(2,1)S(1)} collective-permute-done((bf16[192,384]{1,0:T(8,128)(2,1)S(1)}, bf16[192,384]{1,0:T(8,128)(2,1)S(1)}, u32[]{:S(2)}, u32[]{:S(2)}) %collective-permute-start.11) | collective-permute-done | bytes 147488 | tf_op jit(solution)/shard_map/ppermute | solution.py:346
  96.6 0.0 collective-permute-start.9
  96.6 1.5 %collective-permute-done.12.refs_4_ = bf16[192,384]{1,0:T(8,128)(2,1)S(1)} collective-permute-done((bf16[192,384]{1,0:T(8,128)(2,1)S(1)}, bf16[192,384]{1,0:T(8,128)(2,1)S(1)}, u32[]{:S(2)}, u32[]{:S(2)}) %collective-permute-start.12) | collective-permute-done | bytes 147488 | tf_op jit(solution)/shard_map/ppermute | solution.py:346
  98.1 2.4 %collective-permute-done.13.refs_5_ = bf16[192,384]{1,0:T(8,128)(2,1)S(1)} collective-permute-done((bf16[192,384]{1,0:T(8,128)(2,1)S(1)}, bf16[192,384]{1,0:T(8,128)(2,1)S(1)}, u32[]{:S(2)}, u32[]{:S(2)}) %collective-permute-start.13) | collective-permute-done | bytes 147488 | tf_op jit(solution)/shard_map/ppermute | solution.py:346
  100.5 0.3 collective-permute-done.14.refs_6_
  100.8 0.0 collective-permute-done.15.refs_7_
  100.8 4.0 %collective-permute-done.9.refs_1_ = bf16[192,384]{1,0:T(8,128)(2,1)S(1)} collective-permute-done((bf16[192,384]{1,0:T(8,128)(2,1)S(1)}, bf16[192,384]{1,0:T(8,128)(2,1)S(1)}, u32[]{:S(2)}, u32[]{:S(2)}) %collective-permute-start.9) | collective-permute-done | bytes 147488 | tf_op jit(solution)/shard_map/ppermute | solution.py:346
  104.9 1.7 %shard_map.90 = bf16[192,3072]{1,0:T(8,128)(2,1)} custom-call(s32[7]{0:T(128)S(1)} %stack.27.place, bf16[192,384]{1,0:T(8,128)(2,1)S(1)} %get-tuple-element.35.refs_0_, bf16[192,384]{1,0:T(8,128)(2,1)S(1)} %collective-permute-done.9.refs_1_, bf16[192,384]{1,0:T(8,128)(2,1)S(1)} %collective-permute-done.10.refs_2_, ...), custom_call_target="tpu_custom_call" | custom-call | tf_op jit(solution)/shard_map/pallas_call | solution.py:251
  (1 shorter events, 0.0 us)
Async XLA Ops:
  2.2 5.9 %copy-start.2 = (s32[6]{0:T(128)S(1)}, s32[6]{0:T(128)}, u32[]{:S(2)}) copy-start(s32[6]{0:T(128)} %count.1) | copy-start | bytes 76
  2.2 22.6 %all-to-all-start = ((bf16[8,192,384]{2,1,0:T(8,128)(2,1)}), bf16[8,192,384]{2,1,0:T(8,128)(2,1)S(1)}, u32[]{:S(2)}, u32[]{:S(2)}) async-start(bf16[8,192,384]{2,1,0:T(8,128)(2,1)} %shard_map.83), calls=%async_computation | async-start | bytes 2359296 | tf_op jit(solution)/shard_map/all_to_all | solution.py:349
  9.6 13.7 %collective-permute-start.1 = (bf16[2,32,768]{2,1,0:T(8,128)(2,1)S(1)}, bf16[2,32,768]{2,1,0:T(8,128)(2,1)S(1)}, u32[]{:S(2)}, u32[]{:S(2)}) collective-permute-start(bf16[2,32,768]{2,1,0:T(8,128)(2,1)S(1)} %get-tuple-element.25.refs_0_), channel_id=1, source_target_pairs={{0,8},{1,9},{2,10},{3,11},{4,12},{5,13},{6,14},{7,15},{8,16},{9,17... | collective-permute-start | bytes 294920 | tf_op jit(solution)/shard_map/ppermute | solution.py:339
  11.2 12.1 %collective-permute-start.2 = (bf16[2,32,768]{2,1,0:T(8,128)(2,1)S(1)}, bf16[2,32,768]{2,1,0:T(8,128)(2,1)S(1)}, u32[]{:S(2)}, u32[]{:S(2)}) collective-permute-start(bf16[2,32,768]{2,1,0:T(8,128)(2,1)S(1)} %get-tuple-element.25.refs_0_), channel_id=1, source_target_pairs={{0,16},{1,17},{2,18},{3,19},{4,20},{5,21},{6,22},{7,23},{8,24},{9,... | collective-permute-start | bytes 294920 | tf_op jit(solution)/shard_map/ppermute | solution.py:339
  13.8 9.5 %collective-permute-start.3 = (bf16[2,32,768]{2,1,0:T(8,128)(2,1)S(1)}, bf16[2,32,768]{2,1,0:T(8,128)(2,1)S(1)}, u32[]{:S(2)}, u32[]{:S(2)}) collective-permute-start(bf16[2,32,768]{2,1,0:T(8,128)(2,1)S(1)} %get-tuple-element.25.refs_0_), channel_id=1, source_target_pairs={{0,24},{1,25},{2,26},{3,27},{4,28},{5,29},{6,30},{7,31},{8,0},{9,1... | collective-permute-start | bytes 294920 | tf_op jit(solution)/shard_map/ppermute | solution.py:339
  15.2 8.1 %collective-permute-start = (bf16[16,128]{1,0:T(8,128)(2,1)S(1)}, bf16[16,128]{1,0:T(8,128)(2,1)S(1)}, u32[]{:S(2)}, u32[]{:S(2)}) collective-permute-start(bf16[16,128]{1,0:T(8,128)(2,1)S(1)} %get-tuple-element.24.mask_ref), channel_id=1, source_target_pairs={{0,4},{1,5},{2,6},{3,7},{4,0},{5,1},{6,2},{7,3},{8,12},{9,13},{10,... | collective-permute-start | bytes 12296 | tf_op jit(solution)/shard_map/ppermute | solution.py:343
  24.7 3.6 %copy-start = (bf16[8,192,384]{2,1,0:T(8,128)(2,1)}, bf16[8,192,384]{2,1,0:T(8,128)(2,1)S(1)}, u32[]{:S(2)}) copy-start(bf16[8,192,384]{2,1,0:T(8,128)(2,1)S(1)} %all-to-all-done.__1_.k_ref) | copy-start | bytes 3538948
  24.7 32.1 %all-to-all-start.1 = ((bf16[8,2,192,384]{3,2,1,0:T(8,128)(2,1)}), bf16[8,2,192,384]{3,2,1,0:T(8,128)(2,1)S(1)}, u32[]{:S(2)}, u32[]{:S(2)}) async-start(bf16[8,2,192,384]{3,2,1,0:T(8,128)(2,1)} %shard_map.86), calls=%async_computation.1 | async-start | bytes 4718592 | tf_op jit(solution)/shard_map/all_to_all | solution.py:349
  29.3 17.3 %collective-permute-start.4 = (bf16[4,192,384]{2,1,0:T(8,128)(2,1)S(1)}, bf16[4,192,384]{2,1,0:T(8,128)(2,1)S(1)}, u32[]{:S(2)}, u32[]{:S(2)}) collective-permute-start(bf16[4,192,384]{2,1,0:T(8,128)(2,1)S(1)} %get-tuple-element.44), channel_id=1, source_target_pairs={{0,24},{1,25},{2,26},{3,27},{4,28},{5,29},{6,30},{7,31},{8,0},{9,1... | collective-permute-start | bytes 1769480 | tf_op jit(solution)/shard_map/ppermute | solution.py:339
  32.9 27.9 %copy-start.5 = (bf16[2,128,384]{2,1,0:T(8,128)(2,1)S(1)}, bf16[2,128,384]{2,1,0:T(8,128)(2,1)}, u32[]{:S(2)}) copy-start(bf16[2,128,384]{2,1,0:T(8,128)(2,1)} %get-tuple-element.31) | copy-start | bytes 589828
  32.9 34.7 %copy-start.1 = (f32[16,128]{1,0:T(8,128)S(1)}, f32[16,128]{1,0:T(8,128)}, u32[]{:S(2)}) copy-start(f32[16,128]{1,0:T(8,128)} %get-tuple-element.29.bias) | copy-start | bytes 24580
  32.9 34.0 %collective-permute-start.7 = (bf16[4,192,384]{2,1,0:T(8,128)(2,1)}, bf16[4,192,384]{2,1,0:T(8,128)(2,1)}, u32[]{:S(2)}, u32[]{:S(2)}) collective-permute-start(bf16[4,192,384]{2,1,0:T(8,128)(2,1)} %get-tuple-element.43), channel_id=1, source_target_pairs={{0,8},{1,9},{2,10},{3,11},{4,12},{5,13},{6,14},{7,15},{8,16},{9,17... | collective-permute-start | bytes 1769480 | tf_op jit(solution)/shard_map/ppermute | solution.py:339
  46.6 0.8 copy-start.3
  56.9 28.8 %collective-permute-start.5 = (bf16[4,192,384]{2,1,0:T(8,128)(2,1)S(1)}, bf16[4,192,384]{2,1,0:T(8,128)(2,1)S(1)}, u32[]{:S(2)}, u32[]{:S(2)}) collective-permute-start(bf16[4,192,384]{2,1,0:T(8,128)(2,1)S(1)} %get-tuple-element.27), channel_id=1, source_target_pairs={{0,8},{1,9},{2,10},{3,11},{4,12},{5,13},{6,14},{7,15},{8,16},{9,17... | collective-permute-start | bytes 1769480 | tf_op jit(solution)/shard_map/ppermute | solution.py:339
  58.5 27.3 %collective-permute-start.6 = (bf16[4,192,384]{2,1,0:T(8,128)(2,1)S(1)}, bf16[4,192,384]{2,1,0:T(8,128)(2,1)S(1)}, u32[]{:S(2)}, u32[]{:S(2)}) collective-permute-start(bf16[4,192,384]{2,1,0:T(8,128)(2,1)S(1)} %get-tuple-element.28), channel_id=1, source_target_pairs={{0,24},{1,25},{2,26},{3,27},{4,28},{5,29},{6,30},{7,31},{8,0},{9,1... | collective-permute-start | bytes 1769480 | tf_op jit(solution)/shard_map/ppermute | solution.py:339
  60.8 6.1 %collective-permute-start.8 = (bf16[2,128,384]{2,1,0:T(8,128)(2,1)S(1)}, bf16[2,128,384]{2,1,0:T(8,128)(2,1)S(1)}, u32[]{:S(2)}, u32[]{:S(2)}) collective-permute-start(bf16[2,128,384]{2,1,0:T(8,128)(2,1)S(1)} %copy-done.5), channel_id=1, source_target_pairs={{0,4},{1,5},{2,6},{3,7},{4,0},{5,1},{6,2},{7,3},{8,12},{9,13},{10,... | collective-permute-start | bytes 589832 | tf_op jit(solution)/shard_map/ppermute | solution.py:343
  66.9 0.7 copy-start.4
  88.7 5.2 %collective-permute-start.10 = (bf16[192,384]{1,0:T(8,128)(2,1)S(1)}, bf16[192,384]{1,0:T(8,128)(2,1)S(1)}, u32[]{:S(2)}, u32[]{:S(2)}) collective-permute-start(bf16[192,384]{1,0:T(8,128)(2,1)S(1)} %get-tuple-element.37), channel_id=1, source_target_pairs={{0,2},{1,3},{2,0},{3,1},{4,6},{5,7},{6,4},{7,5},{8,10},{9,11},{10,... | collective-permute-start | bytes 442376 | tf_op jit(solution)/shard_map/ppermute | solution.py:346
  90.2 6.4 %collective-permute-start.11 = (bf16[192,384]{1,0:T(8,128)(2,1)S(1)}, bf16[192,384]{1,0:T(8,128)(2,1)S(1)}, u32[]{:S(2)}, u32[]{:S(2)}) collective-permute-start(bf16[192,384]{1,0:T(8,128)(2,1)S(1)} %get-tuple-element.38), channel_id=1, source_target_pairs={{0,4},{1,5},{2,6},{3,7},{4,0},{5,1},{6,2},{7,3},{8,12},{9,13},{10,... | collective-permute-start | bytes 442376 | tf_op jit(solution)/shard_map/ppermute | solution.py:346
  90.9 7.1 %collective-permute-start.12 = (bf16[192,384]{1,0:T(8,128)(2,1)S(1)}, bf16[192,384]{1,0:T(8,128)(2,1)S(1)}, u32[]{:S(2)}, u32[]{:S(2)}) collective-permute-start(bf16[192,384]{1,0:T(8,128)(2,1)S(1)} %get-tuple-element.39), channel_id=1, source_target_pairs={{0,7},{1,6},{2,5},{3,4},{4,3},{5,2},{6,1},{7,0},{8,15},{9,14},{10,... | collective-permute-start | bytes 442376 | tf_op jit(solution)/shard_map/ppermute | solution.py:346
  90.9 9.6 %collective-permute-start.13 = (bf16[192,384]{1,0:T(8,128)(2,1)S(1)}, bf16[192,384]{1,0:T(8,128)(2,1)S(1)}, u32[]{:S(2)}, u32[]{:S(2)}) collective-permute-start(bf16[192,384]{1,0:T(8,128)(2,1)S(1)} %get-tuple-element.40), channel_id=1, source_target_pairs={{0,3},{1,2},{2,1},{3,0},{4,7},{5,6},{6,5},{7,4},{8,11},{9,10},{10,... | collective-permute-start | bytes 442376 | tf_op jit(solution)/shard_map/ppermute | solution.py:346
  93.4 7.4 %collective-permute-start.14 = (bf16[192,384]{1,0:T(8,128)(2,1)S(1)}, bf16[192,384]{1,0:T(8,128)(2,1)S(1)}, u32[]{:S(2)}, u32[]{:S(2)}) collective-permute-start(bf16[192,384]{1,0:T(8,128)(2,1)S(1)} %get-tuple-element.41), channel_id=1, source_target_pairs={{0,5},{1,4},{2,7},{3,6},{4,1},{5,0},{6,3},{7,2},{8,13},{9,12},{10,... | collective-permute-start | bytes 442376 | tf_op jit(solution)/shard_map/ppermute | solution.py:346
  93.9 6.9 %collective-permute-start.15 = (bf16[192,384]{1,0:T(8,128)(2,1)S(1)}, bf16[192,384]{1,0:T(8,128)(2,1)S(1)}, u32[]{:S(2)}, u32[]{:S(2)}) collective-permute-start(bf16[192,384]{1,0:T(8,128)(2,1)S(1)} %get-tuple-element.42), channel_id=1, source_target_pairs={{0,1},{1,0},{2,3},{3,2},{4,5},{5,4},{6,7},{7,6},{8,9},{9,8},{10,11... | collective-permute-start | bytes 442376 | tf_op jit(solution)/shard_map/ppermute | solution.py:346
  96.6 8.3 %collective-permute-start.9 = (bf16[192,384]{1,0:T(8,128)(2,1)S(1)}, bf16[192,384]{1,0:T(8,128)(2,1)S(1)}, u32[]{:S(2)}, u32[]{:S(2)}) collective-permute-start(bf16[192,384]{1,0:T(8,128)(2,1)S(1)} %get-tuple-element.36), channel_id=1, source_target_pairs={{0,6},{1,7},{2,4},{3,5},{4,2},{5,3},{6,0},{7,1},{8,14},{9,15},{10,... | collective-permute-start | bytes 442376 | tf_op jit(solution)/shard_map/ppermute | solution.py:346
